TPU v7x, 128 devices: a whole 4x4x4 slice. The times are simulated.
128 devices in a mesh: attn: 4 (over x), dev: 32 (over z, y, core).
Axes of the slice: x: 4, y: 4, z: 4, core: 2. Of those that a mesh axis runs over, the one named last changes fastest.
Arguments:
- queries: bfloat16 [2048, 8192], P(('attn', 'dev')), may hold values from -6 to 6
- new_keys: bfloat16 [2048, 512], P(('attn', 'dev')), may hold values from -6 to 6
- new_values: bfloat16 [2048, 512], P(('attn', 'dev')), may hold values from -6 to 6
- key_pages: bfloat16 [8192, 16, 512], P(('attn', 'dev')), may hold values from -6 to 6
- value_pages: bfloat16 [8192, 16, 512], P(('attn', 'dev')), may hold values from -6 to 6
- block_tables: int32 [2048, 4], P(('attn', 'dev')), may hold values from 0 to 63, as said below
- context_lengths: int32 [2048], P(('attn', 'dev')), may hold values from 1 to 64, as said below
- out_weight: bfloat16 [8192, 4096], P('dev'), may hold values from -0.0625 to 0.0625
- residual: bfloat16 [2048, 4096], P(('attn', 'dev')), may hold values from -6 to 6
- norm_gain: float32 [4096], replicated, may hold values from 0.5 to 1.5
- router_weight: bfloat16 [4096, 128], replicated, may hold values from -0.09375 to 0.09375
- routes: int32 [2048, 8], P(('attn', 'dev')), may hold values from 0 to 127, all different within a row; in each aligned block of 16 rows (0 to 15, 16 to 31, ...) at most 2 rows name the same one
- expert_gate: bfloat16 [128, 4096, 768], P(('attn', 'dev')), may hold values from -0.09375 to 0.09375
- expert_up: bfloat16 [128, 4096, 768], P(('attn', 'dev')), may hold values from -0.09375 to 0.09375
- expert_down: bfloat16 [128, 768, 4096], P(('attn', 'dev')), may hold values from -0.21875 to 0.21875
Outputs:
- layer_output: bfloat16 [2048, 4096], P(('attn', 'dev'))
Inputs may be any that keep to these rules, and one draw needn't show every extreme that they name: `block_tables`: on the rows of one device (16 requests in order) the entries are a permutation of 0 to 63, that device's pages in order. `context_lengths`: the rows of every device hold a request of exactly 64 cached tokens. `routes`: the 8 entries of a row differ; within the rows of one device no expert is named by more than 2 rows.
All inputs are finite; a program needn't handle non-finite values.
Results may differ from a plain program's by a relative error of at most 0.02.
Values may be sent and summed in bfloat16 or wider, within the bound.
No kernel may reach another device: no remote copies, remote signals or barrier semaphores. Data moves between devices by JAX's collectives and lax.ppermute only.
A program may use at most 128 MiB of HBM per device.

v0:
```python
import math

import jax
import jax.numpy as jnp
from jax import lax
from jax.sharding import PartitionSpec as P

HEADS = 64
KVH = 4
HD = 128
MAXCTX = 64


EPSILON = 1e-06


def attend(queries, new_keys, new_values, key_pool, value_pool, tables, lengths):
    count_rows = queries.shape[0]
    group_size = HEADS // KVH
    query_heads = queries.reshape(count_rows, KVH, group_size, HD)
    cached_keys = key_pool[tables].reshape(count_rows, MAXCTX, KVH, HD)
    cached_values = value_pool[tables].reshape(count_rows, MAXCTX, KVH, HD)
    own_key = new_keys.reshape(count_rows, KVH, HD)
    own_value = new_values.reshape(count_rows, KVH, 1, HD).astype(jnp.float32)
    scale_factor = 1.0 / math.sqrt(HD)
    scores = (
        jnp.einsum("rkgh,rskh->rkgs", query_heads, cached_keys, preferred_element_type=jnp.float32)
        * scale_factor
    )
    own_score = (
        jnp.einsum("rkgh,rkh->rkg", query_heads, own_key, preferred_element_type=jnp.float32)
        * scale_factor
    )
    live_mask = jnp.arange(MAXCTX, dtype=jnp.int32)[None, :] < lengths[:, None]
    scores = jnp.where(live_mask[:, None, None, :], scores, -jnp.inf)
    top_score = jnp.maximum(jnp.max(scores, axis=-1), own_score)
    weights = jnp.exp(scores - top_score[..., None])
    own_weight = jnp.exp(own_score - top_score)
    total_mass = jnp.sum(weights, axis=-1) + own_weight
    weights = (weights / total_mass[..., None]).astype(jnp.bfloat16)
    own_weight = lax.optimization_barrier((own_weight / total_mass).astype(jnp.bfloat16))
    blended = jnp.einsum(
        "rkgs,rskh->rkgh", weights, cached_values, preferred_element_type=jnp.float32
    )
    blended = blended + own_weight.astype(jnp.float32)[..., None] * own_value
    return blended.reshape(count_rows, HEADS * HD).astype(jnp.bfloat16)


def rms_norm(hidden_state, norm_gain):
    mean_square = jnp.mean(hidden_state * hidden_state, axis=-1, keepdims=True)
    return (hidden_state * lax.rsqrt(mean_square + EPSILON) * norm_gain).astype(jnp.bfloat16)


def route_gates(logits, routes):
    matches = routes[:, :, None] == jnp.arange(logits.shape[1], dtype=jnp.int32)[None, None, :]
    chosen = jnp.sum(jnp.where(matches, logits[:, None, :], 0.0), axis=-1)
    raised = jnp.exp(chosen)
    return raised / jnp.sum(raised, axis=1, keepdims=True)


def slot_index(flat_routes, experts, capacity):
    onehot = (flat_routes[:, None] == jnp.arange(experts, dtype=jnp.int32)[None, :]).astype(
        jnp.int32
    )
    earlier = jnp.cumsum(onehot, axis=0) - onehot
    rank_within = jnp.sum(earlier * onehot, axis=1)
    return flat_routes * capacity + rank_within


def shards(
    queries,
    new_keys,
    new_values,
    key_pages,
    value_pages,
    block_tables,
    context_lengths,
    out_weight,
    residual,
    norm_gain,
    router_weight,
    routes,
    expert_gate,
    expert_up,
    expert_down,
):
    attended = attend(
        queries, new_keys, new_values, key_pages, value_pages, block_tables, context_lengths
    )
    count_rows = attended.shape[0]
    regrouped = lax.all_to_all(attended, "dev", split_axis=1, concat_axis=0, tiled=True)
    projected = lax.psum_scatter(
        jnp.dot(regrouped, out_weight, preferred_element_type=jnp.float32).astype(jnp.bfloat16),
        "dev",
        scatter_dimension=0,
        tiled=True,
    ).astype(jnp.float32)
    hidden_state = residual.astype(jnp.float32) + projected
    normed = rms_norm(hidden_state, norm_gain)
    width_model = normed.shape[1]
    logits = jnp.dot(normed, router_weight, preferred_element_type=jnp.float32)
    gate_values = route_gates(logits, routes)
    experts = router_weight.shape[1]
    top_count = routes.shape[1]
    capacity = max(2, 2 * count_rows * top_count // experts)
    slot_count = experts * capacity
    slot_of = slot_index(routes.reshape(-1), experts, capacity)
    placing = jnp.any(
        jnp.arange(slot_count, dtype=jnp.int32)[:, None, None]
        == slot_of.reshape(count_rows, top_count)[None, :, :],
        axis=2,
    )
    outgoing = jnp.dot(
        placing.astype(jnp.bfloat16), normed, preferred_element_type=jnp.float32
    ).astype(jnp.bfloat16)
    outgoing = outgoing.reshape(experts, capacity, width_model)
    weight_gate = expert_gate[0]
    weight_up = expert_up[0]
    weight_down = expert_down[0]
    arrived = lax.all_to_all(outgoing, ("attn", "dev"), split_axis=0, concat_axis=0, tiled=True)
    arrived_shape = arrived.shape
    flat_rows = arrived.reshape(-1, arrived_shape[-1])
    gate_part = jnp.dot(flat_rows, weight_gate, preferred_element_type=jnp.float32)
    up_part = jnp.dot(flat_rows, weight_up, preferred_element_type=jnp.float32)
    expert_hidden = (jax.nn.silu(gate_part) * up_part).astype(jnp.bfloat16)
    output_rows = jnp.dot(expert_hidden, weight_down, preferred_element_type=jnp.float32).astype(
        jnp.bfloat16
    )
    returned = lax.all_to_all(
        output_rows.reshape(arrived_shape), ("attn", "dev"), split_axis=0, concat_axis=0, tiled=True
    )
    returned = returned.reshape(slot_count, width_model)
    chosen_rows = returned[slot_of].reshape(count_rows, top_count, width_model).astype(jnp.float32)
    expert_sum = jnp.sum(chosen_rows * gate_values[:, :, None], axis=1)
    return (hidden_state + expert_sum).astype(jnp.bfloat16)


def solution(mesh):
    in_specs = (
        P(("attn", "dev"), None),
        P(("attn", "dev"), None),
        P(("attn", "dev"), None),
        P(("attn", "dev"), None, None),
        P(("attn", "dev"), None, None),
        P(("attn", "dev"), None),
        P(("attn", "dev")),
        P("dev", None),
        P(("attn", "dev"), None),
        P(),
        P(),
        P(("attn", "dev"), None),
        P(("attn", "dev"), None, None),
        P(("attn", "dev"), None, None),
        P(("attn", "dev"), None, None),
    )
    out_specs = P(("attn", "dev"), None)
    return jax.shard_map(shards, mesh=mesh, in_specs=in_specs, out_specs=out_specs, check_vma=False)
```

profile of v0, /device:TPU:1, one launch (start us, length us, event | category | flops | bytes accessed | tf_op | source)
XLA Modules:
  0.0 245.2 jit_solution(9696262323915513263)
XLA Ops:
  6.5 0.8 compare_select_fusion
  7.4 0.7 iota_compare_fusion.3
  8.3 0.7 reshape.172
  9.0 0.7 reshape.137
  9.8 1.0 copy.38
  10.8 1.8 gather_fusion.1
  12.6 1.1 reshape.132
  13.7 1.8 gather_fusion
  15.6 1.2 reshape.129
  16.8 0.2 fusion.35
  17.0 2.0 fusion.34
  19.1 0.4 fusion.23
  19.6 0.5 fusion.18
  20.3 18.3 %all_to_all.26 = bf16[16,32,256]{2,0,1:T(8,128)(2,1)S(1)} all-to-all(bf16[16,32,256]{2,0,1:T(8,128)(2,1)S(1)} %copy.32), channel_id=1, replica_groups=mesh['attn'=4,'dev'=32] {'dev'}, dimensions={1} | all-to-all | bytes 524288 | tf_op jit(solution)/shard_map/all_to_all | solution.py:91
  38.6 3.2 %convolution_convert_fusion = bf16[512,4096]{1,0:T(8,128)(2,1)} fusion(bf16[512,256]{1,0:T(8,128)(2,1)S(1)} %bitcast.47, bf16[256,4096]{1,0:T(8,128)(2,1)S(1)} %copy-done), kind=kOutput, calls=%fused_computation.9 | convolution fusion | flops 1075838976 | bytes 6553600 | tf_op jit(solution)/shard_map/dot_general | solution.py:93
  41.9 0.7 copy-done.6
  43.3 76.5 %reduce-scatter.2.cloned.1.call-done = bf16[16,4096]{1,0:T(8,128)(2,1)} async-done(((bf16[512,4096]{1,0:T(8,128)(2,1)}), bf16[16,4096]{1,0:T(8,128)(2,1)}) %reduce-scatter.2.cloned.1.call-update) | async-done | bytes 131088 | tf_op jit(solution)/shard_map/reduce_scatter | solution.py:92
  119.8 1.1 multiply_reduce_fusion
  120.9 3.0 %convolution_convert_fusion.1 = bf16[256,4096]{1,0:T(8,128)(2,1)} fusion(pred[256,16]{0,1:T(8,128)(4,1)S(1)} %fusion.27, bf16[16,4096]{1,0:T(8,128)(2,1)} %reduce-scatter.2.cloned.1.call-done, bf16[16,4096]{1,0:T(8,128)(2,1)S(1)} %copy-done.1, f32[4096]{0:T(1024)S(1)} %copy-done.5, f32[16]{0:T(128)S(1)} %add_rsqrt_fusion), kind=kOutput, calls=%fused_computation.10 | convolution fusion | flops 34996224 | bytes 2379840 | tf_op jit(solution)/shard_map/dot_general | solution.py:113
  123.8 4.4 %reshape.133 = bf16[128,2,4096]{2,1,0:T(2,128)(2,1)} reshape(bf16[256,4096]{1,0:T(8,128)(2,1)} %convolution_convert_fusion.1) | data formatting | bytes 4194304 | tf_op jit(solution)/shard_map/reshape | solution.py:116
  128.2 39.6 %all_to_all.27 = bf16[128,2,4096]{2,1,0:T(2,128)(2,1)} all-to-all(bf16[128,2,4096]{2,1,0:T(2,128)(2,1)} %reshape.133), channel_id=1, replica_groups=mesh['attn'=4,'dev'=32] {'attn','dev'}, dimensions={0} | all-to-all | bytes 4194304 | tf_op jit(solution)/shard_map/all_to_all | solution.py:120
  167.9 4.1 %reshape.134 = bf16[256,4096]{1,0:T(8,128)(2,1)} reshape(bf16[128,2,4096]{2,1,0:T(2,128)(2,1)} %all_to_all.27) | data formatting | bytes 4194304 | tf_op jit(solution)/shard_map/reshape | solution.py:122
  172.0 5.2 %fusion.4 = f32[256,768]{1,0:T(8,128)S(1)} fusion(bf16[256,4096]{1,0:T(8,128)(2,1)} %reshape.134, bf16[1,4096,768]{2,1,0:T(8,128)(2,1)} %param.27), kind=kOutput, calls=%fused_computation.7 | convolution fusion | flops 1610612736 | bytes 9175040 | tf_op jit(solution)/shard_map/dot_general | solution.py:123
  177.2 11.1 %fusion.6 = bf16[256,4096]{1,0:T(8,128)(2,1)} fusion(bf16[1,768,4096]{2,1,0:T(8,128)(2,1)} %param.29, bf16[256,4096]{1,0:T(8,128)(2,1)} %reshape.134, bf16[1,4096,768]{2,1,0:T(8,128)(2,1)} %param.28, f32[256,768]{1,0:T(8,128)S(1)} %fusion.4), kind=kOutput, calls=%fused_computation.11 | convolution fusion | flops 3223453696 | bytes 17563648 | tf_op jit(solution)/shard_map/dot_general | solution.py:126
  188.3 4.4 %reshape.135 = bf16[128,2,4096]{2,1,0:T(2,128)(2,1)} reshape(bf16[256,4096]{1,0:T(8,128)(2,1)} %fusion.6) | data formatting | bytes 4194304 | tf_op jit(solution)/shard_map/reshape | solution.py:130
  192.7 5.7 %all-to-all-start.2 = ((bf16[128,2,4096]{2,1,0:T(2,128)(2,1)}), bf16[128,2,4096]{2,1,0:T(2,128)(2,1)}, u32[]{:S(2)}, u32[]{:S(2)}) async-start(bf16[128,2,4096]{2,1,0:T(2,128)(2,1)} %reshape.135), calls=%async_computation.3 | async-start | bytes 4194304 | tf_op jit(solution)/shard_map/all_to_all | solution.py:129
  198.6 0.3 fusion.33
  199.2 29.4 %all-to-all-done.2 = bf16[128,2,4096]{2,1,0:T(2,128)(2,1)} async-done(((bf16[128,2,4096]{2,1,0:T(2,128)(2,1)}), bf16[128,2,4096]{2,1,0:T(2,128)(2,1)}, u32[]{:S(2)}, u32[]{:S(2)}) %all-to-all-start.2) | async-done | bytes 2097184 | tf_op jit(solution)/shard_map/all_to_all | solution.py:129
  228.6 4.1 %reshape.136 = bf16[256,4096]{1,0:T(8,128)(2,1)} reshape(bf16[128,2,4096]{2,1,0:T(2,128)(2,1)} %all-to-all-done.2) | data formatting | bytes 4194304 | tf_op jit(solution)/shard_map/reshape | solution.py:132
  232.7 4.1 %gather_fusion.2 = bf16[128,4096]{1,0:T(8,128)(2,1)S(1)} fusion(bf16[256,4096]{1,0:T(8,128)(2,1)} %reshape.136, s32[1024]{0:T(1024)S(1)} %pad_clamp_fusion), kind=kCustom, calls=%fused_computation.2 | custom fusion | bytes 2097664 | tf_op jit(solution)/shard_map/gather | solution.py:133
  236.8 0.8 fusion.9
  237.6 0.7 add_convert_fusion
  (38 shorter events, 1.8 us)
Async XLA Ops:
  6.5 32.1 %copy-start = (bf16[256,4096]{1,0:T(8,128)(2,1)S(1)}, bf16[256,4096]{1,0:T(8,128)(2,1)}, u32[]{:S(2)}) copy-start(bf16[256,4096]{1,0:T(8,128)(2,1)} %param.22) | copy-start | bytes 6291460
  6.5 113.3 %reduce-scatter.2.cloned.1.call-start = ((), (), s32[]{:S(2)}) async-start(), calls=%async_computation.4 | async-start | bytes 4325376 | tf_op jit(solution)/shard_map/reduce_scatter | solution.py:92
  16.8 2.8 %copy-start.4 = (bf16[16,64,4,128]{3,2,1,0:T(4,128)(2,1)S(1)}, bf16[16,64,4,128]{3,2,1,0:T(4,128)(2,1)}, u32[]{:S(2)}) copy-start(bf16[16,64,4,128]{3,2,1,0:T(4,128)(2,1)} %reshape.132) | copy-start | bytes 3145732
  41.8 0.7 copy-start.6
  41.8 78.0 %copy-start.1 = (bf16[16,4096]{1,0:T(8,128)(2,1)S(1)}, bf16[16,4096]{1,0:T(8,128)(2,1)}, u32[]{:S(2)}) copy-start(bf16[16,4096]{1,0:T(8,128)(2,1)} %param.23) | copy-start | bytes 393220
  41.8 79.1 %copy-start.5 = (f32[4096]{0:T(1024)S(1)}, f32[4096]{0:T(1024)}, u32[]{:S(2)}) copy-start(f32[4096]{0:T(1024)} %param.24) | copy-start | bytes 49156
  192.7 5.9 %copy-start.2 = (bf16[16,4096]{1,0:T(8,128)(2,1)S(1)}, bf16[16,4096]{1,0:T(8,128)(2,1)}, u32[]{:S(2)}) copy-start(bf16[16,4096]{1,0:T(8,128)(2,1)} %reduce-scatter.2.cloned.1.call-done) | copy-start | bytes 393220
  192.7 5.9 %copy-start.3 = (bf16[4096,128]{1,0:T(8,128)(2,1)S(1)}, bf16[4096,128]{1,0:T(8,128)(2,1)}, u32[]{:S(2)}) copy-start(bf16[4096,128]{1,0:T(8,128)(2,1)} %param.25) | copy-start | bytes 3145732
  192.7 35.9 %all-to-all-start.2 = ((bf16[128,2,4096]{2,1,0:T(2,128)(2,1)}), bf16[128,2,4096]{2,1,0:T(2,128)(2,1)}, u32[]{:S(2)}, u32[]{:S(2)}) async-start(bf16[128,2,4096]{2,1,0:T(2,128)(2,1)} %reshape.135), calls=%async_computation.3 | async-start | bytes 4194304 | tf_op jit(solution)/shard_map/all_to_all | solution.py:129
Sparse Core Ops, SparseCore 0:
  42.0 77.7 reduce-scatter.1
where the time goes:
time: 246 us; the launch traced here: 245 us
  waiting for transfers between devices  106 us (43%)
  blocking collectives  57.9 us (24%)
  local copies, waits for them, and re-layouts  31 us (13%)
  matrix products  25.5 us (10%)
  between operations  13.6 us (6%)
  starting transfers between devices  5.75 us (2%)
  other arithmetic  5.56 us (2%)
    reduce_scatter x1, waiting for transfers between devices, shards(): lax.psum_scatter(jnp.dot(regrouped, out_weight, preferred_element_type=jn...  76.5 us
    all_to_all x1, blocking collectives, shards(): lax.all_to_all(outgoing, ('attn', 'dev'), split_axis=0, concat_axis=0, ti...  39.6 us
    all_to_all x1, waiting for transfers between devices, shards(): lax.all_to_all(output_rows.reshape(arrived_shape), ('attn', 'dev'), split...  29.4 us
    all_to_all x1, blocking collectives, shards(): lax.all_to_all(attended, 'dev', split_axis=1, concat_axis=0, tiled=True)  18.3 us
    dot_general x1, matrix products, shards(): jnp.dot(expert_hidden, weight_down, preferred_element_type=jnp.float32)  11.1 us
    all_to_all x1, starting transfers between devices, shards(): lax.all_to_all(output_rows.reshape(arrived_shape), ('attn', 'dev'), split...  5.74 us
    dot_general x1, matrix products, shards(): jnp.dot(flat_rows, weight_gate, preferred_element_type=jnp.float32)  5.2 us
  transfers between devices with their start and end apart: 2, of which 2 were waited for; matrix products, arithmetic and copies ran while one was open for 1% of the time, Pallas kernels for 0%

commit v1 on v0

--- a/solution.py
+++ b/solution.py
@@ -9,9 +9,8 @@
 KVH = 4
 HD = 128
 MAXCTX = 64
-
-
 EPSILON = 1e-06
+BLOCK = 512
 
 
 def attend(queries, new_keys, new_values, key_pool, value_pool, tables, lengths):
@@ -44,11 +43,6 @@
     )
     blended = blended + own_weight.astype(jnp.float32)[..., None] * own_value
     return blended.reshape(count_rows, HEADS * HD).astype(jnp.bfloat16)
-
-
-def rms_norm(hidden_state, norm_gain):
-    mean_square = jnp.mean(hidden_state * hidden_state, axis=-1, keepdims=True)
-    return (hidden_state * lax.rsqrt(mean_square + EPSILON) * norm_gain).astype(jnp.bfloat16)
 
 
 def route_gates(logits, routes):
@@ -84,54 +78,93 @@
     expert_up,
     expert_down,
 ):
+    rows = queries.shape[0]
+    width = out_weight.shape[1]
+    depth = out_weight.shape[0]
+    peers = lax.axis_size("dev")
+    chips = peers // 2
+    core = lax.axis_index("dev") % 2
+    same_core = [[2 * chip + side for chip in range(chips)] for side in range(2)]
+    experts = router_weight.shape[1]
+    capacity = 2
+    blocks = width // BLOCK
+
+    weight_beside = lax.ppermute(out_weight, "dev", [(i, i ^ 1) for i in range(peers)])
     attended = attend(
         queries, new_keys, new_values, key_pages, value_pages, block_tables, context_lengths
     )
-    count_rows = attended.shape[0]
-    regrouped = lax.all_to_all(attended, "dev", split_axis=1, concat_axis=0, tiled=True)
-    projected = lax.psum_scatter(
-        jnp.dot(regrouped, out_weight, preferred_element_type=jnp.float32).astype(jnp.bfloat16),
+    outgoing = attended.reshape(rows, chips, 2 * depth).transpose(1, 0, 2)
+    regrouped = lax.all_to_all(
+        outgoing, "dev", split_axis=0, concat_axis=0, axis_index_groups=same_core, tiled=True
+    ).reshape(chips * rows, 2 * depth)
+    first, second = regrouped[:, :depth], regrouped[:, depth:]
+    mine = jnp.where(core == 0, first, second)
+    beside = jnp.where(core == 0, second, first)
+    partial = (
+        jnp.dot(mine, out_weight, preferred_element_type=jnp.float32)
+        + jnp.dot(beside, weight_beside, preferred_element_type=jnp.float32)
+    ).astype(jnp.bfloat16)
+    partials = lax.all_to_all(
+        partial.reshape(chips, rows, width),
         "dev",
-        scatter_dimension=0,
+        split_axis=0,
+        concat_axis=0,
+        axis_index_groups=same_core,
         tiled=True,
-    ).astype(jnp.float32)
-    hidden_state = residual.astype(jnp.float32) + projected
-    normed = rms_norm(hidden_state, norm_gain)
-    width_model = normed.shape[1]
+    )
+    hidden_state = residual.astype(jnp.float32) + jnp.sum(partials.astype(jnp.float32), axis=0)
+
+    mean_square = jnp.mean(hidden_state * hidden_state, axis=-1, keepdims=True)
+    normed = (hidden_state * lax.rsqrt(mean_square + EPSILON) * norm_gain).astype(jnp.bfloat16)
     logits = jnp.dot(normed, router_weight, preferred_element_type=jnp.float32)
     gate_values = route_gates(logits, routes)
-    experts = router_weight.shape[1]
-    top_count = routes.shape[1]
-    capacity = max(2, 2 * count_rows * top_count // experts)
-    slot_count = experts * capacity
-    slot_of = slot_index(routes.reshape(-1), experts, capacity)
-    placing = jnp.any(
-        jnp.arange(slot_count, dtype=jnp.int32)[:, None, None]
-        == slot_of.reshape(count_rows, top_count)[None, :, :],
-        axis=2,
+
+    slot_of = slot_index(routes.reshape(-1), experts, capacity).reshape(rows, -1)
+    line = jnp.arange(experts * blocks * capacity, dtype=jnp.int32)
+    line_slot = line // (blocks * capacity) * capacity + line % capacity
+    line_block = line // capacity % blocks
+    cell = jnp.arange(blocks * rows, dtype=jnp.int32)
+    same_block = line_block[:, None] == (cell // rows)[None, :]
+    slot_of_cell = jnp.tile(slot_of, (blocks, 1))
+    hit = (line_slot[:, None, None] == slot_of_cell[None, :, :]) & same_block[:, :, None]
+    placing = jnp.any(hit, axis=2).astype(jnp.bfloat16)
+    stacked = normed.reshape(rows, blocks, BLOCK).transpose(1, 0, 2).reshape(blocks * rows, BLOCK)
+    sent = jnp.dot(placing, stacked, preferred_element_type=jnp.float32).astype(jnp.bfloat16)
+    arrived = lax.all_to_all(
+        sent.reshape(experts, blocks * capacity, BLOCK),
+        ("attn", "dev"),
+        split_axis=0,
+        concat_axis=0,
+        tiled=True,
     )
-    outgoing = jnp.dot(
-        placing.astype(jnp.bfloat16), normed, preferred_element_type=jnp.float32
+    flat_rows = (
+        arrived.reshape(experts, blocks, capacity, BLOCK)
+        .transpose(2, 0, 1, 3)
+        .reshape(experts * capacity, width)
+    )
+    gate_part = jnp.dot(flat_rows, expert_gate[0], preferred_element_type=jnp.float32)
+    up_part = jnp.dot(flat_rows, expert_up[0], preferred_element_type=jnp.float32)
+    expert_hidden = (jax.nn.silu(gate_part) * up_part).astype(jnp.bfloat16)
+    output_rows = jnp.dot(
+        expert_hidden, expert_down[0], preferred_element_type=jnp.float32
     ).astype(jnp.bfloat16)
-    outgoing = outgoing.reshape(experts, capacity, width_model)
-    weight_gate = expert_gate[0]
-    weight_up = expert_up[0]
-    weight_down = expert_down[0]
-    arrived = lax.all_to_all(outgoing, ("attn", "dev"), split_axis=0, concat_axis=0, tiled=True)
-    arrived_shape = arrived.shape
-    flat_rows = arrived.reshape(-1, arrived_shape[-1])
-    gate_part = jnp.dot(flat_rows, weight_gate, preferred_element_type=jnp.float32)
-    up_part = jnp.dot(flat_rows, weight_up, preferred_element_type=jnp.float32)
-    expert_hidden = (jax.nn.silu(gate_part) * up_part).astype(jnp.bfloat16)
-    output_rows = jnp.dot(expert_hidden, weight_down, preferred_element_type=jnp.float32).astype(
-        jnp.bfloat16
+    back = (
+        output_rows.reshape(capacity, experts, blocks, BLOCK)
+        .transpose(1, 2, 0, 3)
+        .reshape(experts, blocks * capacity, BLOCK)
     )
     returned = lax.all_to_all(
-        output_rows.reshape(arrived_shape), ("attn", "dev"), split_axis=0, concat_axis=0, tiled=True
+        back, ("attn", "dev"), split_axis=0, concat_axis=0, tiled=True
+    ).reshape(experts * blocks * capacity, BLOCK)
+    gate_of_cell = jnp.tile(gate_values, (blocks, 1))
+    mixing = jnp.sum(jnp.where(hit, gate_of_cell[None, :, :], 0.0), axis=2).T
+    high = mixing.astype(jnp.bfloat16)
+    low = (mixing - high.astype(jnp.float32)).astype(jnp.bfloat16)
+    mixed = jnp.dot(
+        jnp.concatenate([high, low], axis=0), returned, preferred_element_type=jnp.float32
     )
-    returned = returned.reshape(slot_count, width_model)
-    chosen_rows = returned[slot_of].reshape(count_rows, top_count, width_model).astype(jnp.float32)
-    expert_sum = jnp.sum(chosen_rows * gate_values[:, :, None], axis=1)
+    mixed = mixed[: blocks * rows] + mixed[blocks * rows :]
+    expert_sum = mixed.reshape(blocks, rows, BLOCK).transpose(1, 0, 2).reshape(rows, width)
     return (hidden_state + expert_sum).astype(jnp.bfloat16)
 
 

time: 246 us -> 164 us (0.67)
  waiting for transfers between devices: 106 us -> 35.9 us
  other arithmetic: 5.56 us -> 34.8 us
  blocking collectives: 57.9 us -> 37.8 us
  local copies, waits for them, and re-layouts: 31 us -> 13 us
  starting transfers between devices: 5.75 us -> 18.9 us
  between operations: 13.6 us -> 0.47 us
  matrix products: 25.5 us -> 22.8 us
    reduce_scatter x1 -> x0, waiting for transfers between devices: 76.5 us -> none  [shards(): lax.psum_scatter(jnp.dot(regrouped, out_weight, preferred_element_type=jn...]
    all_to_all x2 -> x1, blocking collectives: 57.9 us -> 37.8 us  [shards(): lax.all_to_all(sent.reshape(experts, blocks * capacity, BLOCK), ('attn',...]
    reduce_or x1, other arithmetic: 0.13 us -> 15.2 us  [shards(): placing = jnp.any(hit, axis=2).astype(jnp.bfloat16)]
    reshape x4 -> x3, local copies, waits for them, and re-layouts: 17 us -> 3.15 us  [the longest x1 2.46 us: shards(): back = output_rows.reshape(capacity, experts, blocks, BLOCK).transpose(1,...]
    reduce_sum x2 -> x3, other arithmetic: 1.85 us -> 15.7 us  [the longest x1 15.2 us: shards(): mixing = jnp.sum(jnp.where(hit, gate_of_cell[None, :, :], 0.0), axis=2).T]
    all_to_all x1 -> x3, starting transfers between devices: 5.74 us -> 17.5 us  [the longest x1 7.87 us: shards(): lax.all_to_all(outgoing, 'dev', split_axis=0, concat_axis=0, axis_index_g...]
    all_to_all x1 -> x3, waiting for transfers between devices: 29.4 us -> 35.9 us  [the longest x1 14.2 us: shards(): lax.all_to_all(back, ('attn', 'dev'), split_axis=0, concat_axis=0, tiled=...]
    gather x1 -> x0, local copies, waits for them, and re-layouts: 4.06 us -> none  [shards(): returned[slot_of].reshape(count_rows, top_count, width_model)]
  transfers between devices with their start and end apart: 2 -> 4, of which waited for: 2 -> 3; matrix products, arithmetic and copies ran while one was open for 1% -> 25% of each run, Pallas kernels for 0% -> 0%
where the time goes in v1:
time: 164 us
  blocking collectives  37.8 us (23%)
  waiting for transfers between devices  35.9 us (22%)
  other arithmetic  34.8 us (21%)
  matrix products  22.8 us (14%)
  starting transfers between devices  18.9 us (12%)
  local copies, waits for them, and re-layouts  13 us (8%)
    all_to_all x1, blocking collectives, shards(): lax.all_to_all(sent.reshape(experts, blocks * capacity, BLOCK), ('attn',...  37.8 us
    reduce_sum x1, other arithmetic, shards(): mixing = jnp.sum(jnp.where(hit, gate_of_cell[None, :, :], 0.0), axis=2).T  15.2 us
    reduce_or x1, other arithmetic, shards(): placing = jnp.any(hit, axis=2).astype(jnp.bfloat16)  15.2 us
    all_to_all x1, waiting for transfers between devices, shards(): lax.all_to_all(back, ('attn', 'dev'), split_axis=0, concat_axis=0, tiled=...  14.2 us
    all_to_all x1, waiting for transfers between devices, shards(): lax.all_to_all(partial.reshape(chips, rows, width), 'dev', split_axis=0,...  13.3 us
    dot_general x1, matrix products, shards(): jnp.dot(expert_hidden, expert_down[0], preferred_element_type=jnp.float32)  10.5 us
    all_to_all x1, waiting for transfers between devices, shards(): lax.all_to_all(outgoing, 'dev', split_axis=0, concat_axis=0, axis_index_g...  8.43 us
    all_to_all x1, starting transfers between devices, shards(): lax.all_to_all(outgoing, 'dev', split_axis=0, concat_axis=0, axis_index_g...  7.87 us
  transfers between devices with their start and end apart: 4, of which 3 were waited for; matrix products, arithmetic and copies ran while one was open for 25% of the time, Pallas kernels for 0%

profile of v1, /device:TPU:1, one launch (start us, length us, event | category | flops | bytes accessed | tf_op | source)
XLA Modules:
  0.0 163.6 jit_solution(13786366039349625058)
XLA Ops:
  0.0 1.4 collective-permute-start
  1.4 0.7 compare_select_fusion
  2.3 0.7 iota_compare_fusion.2
  3.1 0.6 gather_fusion
  4.3 0.8 fusion.58
  5.1 0.4 fusion.29
  5.9 0.6 gather_fusion.1
  6.9 1.7 %fusion.19 = bf16[16,4,16,128]{3,2,1,0:T(8,128)(2,1)S(1)} fusion(bf16[16,64,4,128]{3,2,1,0:T(4,128)(2,1)S(1)} %reshape.215, f32[16,4,16,64]{3,2,1,0:T(8,128)} %copy-done.8, f32[16,4,128]{2,1,0:T(4,128)S(1)} %reshape.228, f32[16,4,16]{2,1,0:T(4,128)S(1)} %convert_element_type.67, f32[16,4,16]{2,1,0:T(4,128)S(1)} %get-tuple-element.7, ...), kind=kOutput, calls=%fused_computation.22 | convolution fusion | flops 17367040 | bytes 1617920 | tf_op jit(solution)/shard_map/rkgs,rskh->rkgh/dot_general | solution.py:41
  8.7 0.9 copy.102
  9.6 7.9 %all-to-all-start = ((bf16[16,16,512]{2,1,0:T(8,128)(2,1)}), bf16[16,16,512]{2,1,0:T(8,128)(2,1)S(1)}, u32[]{:S(2)}, u32[]{:S(2)}) async-start(bf16[16,16,512]{2,1,0:T(8,128)(2,1)} %bitcast.76), calls=%async_computation | async-start | bytes 524288 | tf_op jit(solution)/shard_map/all_to_all | solution.py:97
  17.5 8.4 %all-to-all-done = bf16[16,16,512]{2,1,0:T(8,128)(2,1)S(1)} async-done(((bf16[16,16,512]{2,1,0:T(8,128)(2,1)}), bf16[16,16,512]{2,1,0:T(8,128)(2,1)S(1)}, u32[]{:S(2)}, u32[]{:S(2)}) %all-to-all-start) | async-done | bytes 262176 | tf_op jit(solution)/shard_map/all_to_all | solution.py:97
  25.9 0.7 fusion.34
  26.7 3.7 %fusion.7 = bf16[256,4096]{1,0:T(8,128)(2,1)} fusion(f32[256,4096]{1,0:T(8,128)S(1)} %fusion.34, bf16[256,4096]{1,0:T(8,128)(2,1)} %collective-permute-done, pred[]{:T(512)S(6)} %eq.67, bf16[256,512]{1,0:T(8,128)(2,1)S(1)} %bitcast.88), kind=kOutput, calls=%fused_computation.12 | convolution fusion | flops 539033600 | bytes 8650753 | tf_op jit(solution)/shard_map/dot_general | solution.py:105
  30.3 3.8 %all-to-all-start.1 = ((bf16[16,16,4096]{2,1,0:T(8,128)(2,1)}), bf16[16,16,4096]{2,1,0:T(8,128)(2,1)S(1)}, u32[]{:S(2)}, u32[]{:S(2)}) async-start(bf16[16,16,4096]{2,1,0:T(8,128)(2,1)} %bitcast.82), calls=%async_computation.1 | async-start | bytes 4194304 | tf_op jit(solution)/shard_map/all_to_all | solution.py:107
  35.1 0.3 broadcast_compare_fusion
  35.5 15.2 %fusion = pred[2048,128]{1,0:T(8,128)(4,1)S(1)} fusion(s32[128,8]{0,1:T(8,128)S(1)} %tile.16, s32[2048]{0:T(1024)S(1)} %fusion.50, pred[2048,128]{1,0:T(8,128)(4,1)S(1)} %broadcast_compare_fusion), kind=kLoop, calls=%fused_computation.4 | loop fusion | flops 6029312 | bytes 536576 | tf_op jit(solution)/shard_map/reduce_or | solution.py:130
  50.7 13.3 %all-to-all-done.1 = bf16[16,16,4096]{2,1,0:T(8,128)(2,1)S(1)} async-done(((bf16[16,16,4096]{2,1,0:T(8,128)(2,1)}), bf16[16,16,4096]{2,1,0:T(8,128)(2,1)S(1)}, u32[]{:S(2)}, u32[]{:S(2)}) %all-to-all-start.1) | async-done | bytes 2097184 | tf_op jit(solution)/shard_map/all_to_all | solution.py:107
  64.7 0.7 convolution_convert_fusion
  65.4 37.8 %all_to_all.20 = bf16[128,16,512]{2,1,0:T(8,128)(2,1)S(1)} all-to-all(bf16[128,16,512]{2,1,0:T(8,128)(2,1)S(1)} %bitcast.77), channel_id=1, replica_groups=mesh['attn'=4,'dev'=32] {'attn','dev'}, dimensions={0} | all-to-all | bytes 4194304 | tf_op jit(solution)/shard_map/all_to_all | solution.py:133
  103.2 1.2 copy.83
  104.4 1.2 copy.84
  105.5 0.9 copy.93
  106.5 1.9 %fusion.5 = f32[256,768]{1,0:T(8,128)S(1)} fusion(bf16[256,4096]{1,0:T(8,128)(2,1)S(1)} %bitcast.83, bf16[1,4096,768]{2,1,0:T(8,128)(2,1)S(1)} %bitcast.99), kind=kOutput, calls=%fused_computation.9 | convolution fusion | flops 1610612736 | bytes 9175040 | tf_op jit(solution)/shard_map/dot_general | solution.py:145
  108.3 10.5 %fusion.8 = bf16[256,4096]{1,0:T(8,128)(2,1)} fusion(bf16[1,768,4096]{2,1,0:T(8,128)(2,1)} %param.29, bf16[256,4096]{1,0:T(8,128)(2,1)S(1)} %bitcast.84, bf16[1,4096,768]{2,1,0:T(8,128)(2,1)} %param.28, f32[256,768]{1,0:T(8,128)S(1)} %fusion.5), kind=kOutput, calls=%fused_computation.13 | convolution fusion | flops 3223453696 | bytes 17563648 | tf_op jit(solution)/shard_map/dot_general | solution.py:148
  118.9 2.5 %copy.94 = bf16[32,8,8,512]{3,2,1,0:T(8,128)(2,1)S(1)} copy(bf16[32,8,8,512]{3,1,2,0:T(8,128)(2,1)} %bitcast.85) | data formatting | bytes 4194304
  121.3 0.7 copy.85
  122.0 2.5 %copy.86 = bf16[128,16,512]{2,1,0:T(8,128)(2,1)} copy(bf16[128,16,512]{2,0,1:T(8,128)(2,1)S(1)} %bitcast.81) | data formatting | bytes 4194304 | tf_op jit(solution)/shard_map/reshape | solution.py:154
  124.5 5.8 %all-to-all-start.3 = ((bf16[128,16,512]{2,1,0:T(8,128)(2,1)}), bf16[128,16,512]{2,1,0:T(8,128)(2,1)}, u32[]{:S(2)}, u32[]{:S(2)}) async-start(bf16[128,16,512]{2,1,0:T(8,128)(2,1)} %copy.86), calls=%async_computation.3 | async-start | bytes 4194304 | tf_op jit(solution)/shard_map/all_to_all | solution.py:156
  130.9 15.2 %select_reduce_fusion = f32[2048,128]{1,0:T(8,128)S(1)} fusion(f32[128,8]{0,1:T(8,128)S(1)} %tile.18, s32[128,8]{0,1:T(8,128)S(1)} %tile.16, s32[2048]{0:T(1024)S(1)} %fusion.50, pred[2048,128]{1,0:T(8,128)(4,1)S(1)} %copy-done.3), kind=kLoop, calls=%fused_computation.2 | loop fusion | flops 8126464 | bytes 1327104 | tf_op jit(solution)/shard_map/reduce_sum | solution.py:160
  146.3 14.2 %all-to-all-done.3 = bf16[128,16,512]{2,1,0:T(8,128)(2,1)} async-done(((bf16[128,16,512]{2,1,0:T(8,128)(2,1)}), bf16[128,16,512]{2,1,0:T(8,128)(2,1)}, u32[]{:S(2)}, u32[]{:S(2)}) %all-to-all-start.3) | async-done | bytes 2097184 | tf_op jit(solution)/shard_map/all_to_all | solution.py:156
  160.4 2.4 %fusion.20 = f32[256,512]{1,0:T(8,128)S(1)} fusion(bf16[2048,512]{1,0:T(8,128)(2,1)} %bitcast.17, bf16[128,2048]{0,1:T(8,128)(2,1)S(1)} %get-tuple-element.5, bf16[128,2048]{0,1:T(8,128)(2,1)S(1)} %get-tuple-element.6), kind=kOutput, calls=%fused_computation.23 | convolution fusion | flops 538968064 | bytes 3670016 | tf_op jit(solution)/shard_map/dot_general | solution.py:163
  162.9 0.7 add_convert_fusion
  (76 shorter events, 4.0 us)
Async XLA Ops:
  0.0 3.0 %copy-start = (bf16[64,16,512]{2,1,0:T(8,128)(2,1)S(1)}, bf16[64,16,512]{2,1,0:T(8,128)(2,1)}, u32[]{:S(2)}) copy-start(bf16[64,16,512]{2,1,0:T(8,128)(2,1)} %param.18) | copy-start | bytes 3145732
  0.0 26.6 %collective-permute-start = (bf16[256,4096]{1,0:T(8,128)(2,1)}, bf16[256,4096]{1,0:T(8,128)(2,1)}, u32[]{:S(2)}, u32[]{:S(2)}) collective-permute-start(bf16[256,4096]{1,0:T(8,128)(2,1)} %param.22), channel_id=1, source_target_pairs={{0,1},{1,0},{2,3},{3,2},{4,5},{5,4},{6,7},{7,6},{8,9},{9,8},{10,11... | collective-permute-start | bytes 6291464 | tf_op jit(solution)/shard_map/ppermute | solution.py:92
  3.0 1.0 copy-start.9
  3.0 1.0 copy-start.10
  4.0 1.9 %copy-start.7 = (bf16[64,16,512]{2,1,0:T(8,128)(2,1)S(1)}, bf16[64,16,512]{2,1,0:T(8,128)(2,1)}, u32[]{:S(2)}) copy-start(bf16[64,16,512]{2,1,0:T(8,128)(2,1)} %param.19) | copy-start | bytes 3145732
  5.1 0.8 copy-start.8
  5.9 0.9 copy-start.11
  6.9 19.1 %copy-start.4 = (bf16[256,4096]{1,0:T(8,128)(2,1)S(1)}, bf16[256,4096]{1,0:T(8,128)(2,1)}, u32[]{:S(2)}) copy-start(bf16[256,4096]{1,0:T(8,128)(2,1)} %param.22) | copy-start | bytes 6291460
  9.6 16.3 %all-to-all-start = ((bf16[16,16,512]{2,1,0:T(8,128)(2,1)}), bf16[16,16,512]{2,1,0:T(8,128)(2,1)S(1)}, u32[]{:S(2)}, u32[]{:S(2)}) async-start(bf16[16,16,512]{2,1,0:T(8,128)(2,1)} %bitcast.76), calls=%async_computation | async-start | bytes 524288 | tf_op jit(solution)/shard_map/all_to_all | solution.py:97
  30.3 3.9 %copy-start.13 = (s32[16,8]{0,1:T(8,128)S(1)}, s32[16,8]{0,1:T(8,128)}, u32[]{:S(2)}) copy-start(s32[16,8]{0,1:T(8,128)} %param.26) | copy-start | bytes 1540
  30.3 33.7 %all-to-all-start.1 = ((bf16[16,16,4096]{2,1,0:T(8,128)(2,1)}), bf16[16,16,4096]{2,1,0:T(8,128)(2,1)S(1)}, u32[]{:S(2)}, u32[]{:S(2)}) async-start(bf16[16,16,4096]{2,1,0:T(8,128)(2,1)} %bitcast.82), calls=%async_computation.1 | async-start | bytes 4194304 | tf_op jit(solution)/shard_map/all_to_all | solution.py:107
  34.2 30.1 %copy-start.5 = (bf16[16,4096]{1,0:T(8,128)(2,1)S(1)}, bf16[16,4096]{1,0:T(8,128)(2,1)}, u32[]{:S(2)}) copy-start(bf16[16,4096]{1,0:T(8,128)(2,1)} %param.23) | copy-start | bytes 393220
  34.2 30.3 %copy-start.12 = (f32[4096]{0:T(1024)S(1)}, f32[4096]{0:T(1024)}, u32[]{:S(2)}) copy-start(f32[4096]{0:T(1024)} %param.24) | copy-start | bytes 49156
  35.5 29.2 %copy-start.2 = (pred[2048,128]{1,0:T(8,128)(4,1)}, pred[2048,128]{1,0:T(8,128)(4,1)S(1)}, u32[]{:S(2)}) copy-start(pred[2048,128]{1,0:T(8,128)(4,1)S(1)} %broadcast_compare_fusion) | copy-start | bytes 786436
  103.2 3.3 %slice-start = ((s8[6291456]{0:T(1024)(128)(4,1)}), s8[4194304]{0:T(1024)(128)(4,1)S(1)}, s32[]{:S(2)}) async-start(s8[6291456]{0:T(1024)(128)(4,1)} %bitcast.98), calls=%async_computation.4 | async-start | bytes 8388608
  104.4 2.1 %slice-start.1 = ((s8[6291456]{0:T(1024)(128)(4,1)}), s8[2097152]{0:T(1024)(128)(4,1)S(1)}, s32[]{:S(2)}) async-start(s8[6291456]{0:T(1024)(128)(4,1)} %bitcast.98), calls=%async_computation.5 | async-start | bytes 4194304
  124.5 5.8 %copy-start.6 = (bf16[4096,128]{1,0:T(8,128)(2,1)S(1)}, bf16[4096,128]{1,0:T(8,128)(2,1)}, u32[]{:S(2)}) copy-start(bf16[4096,128]{1,0:T(8,128)(2,1)} %param.25) | copy-start | bytes 3145732
  124.5 6.4 %copy-start.3 = (pred[2048,128]{1,0:T(8,128)(4,1)S(1)}, pred[2048,128]{1,0:T(8,128)(4,1)}, u32[]{:S(2)}) copy-start(pred[2048,128]{1,0:T(8,128)(4,1)} %copy-done.2) | copy-start | bytes 786436
  124.5 35.9 %all-to-all-start.3 = ((bf16[128,16,512]{2,1,0:T(8,128)(2,1)}), bf16[128,16,512]{2,1,0:T(8,128)(2,1)}, u32[]{:S(2)}, u32[]{:S(2)}) async-start(bf16[128,16,512]{2,1,0:T(8,128)(2,1)} %copy.86), calls=%async_computation.3 | async-start | bytes 4194304 | tf_op jit(solution)/shard_map/all_to_all | solution.py:156
  160.4 3.2 %copy-start.1 = (bf16[64,16,512]{2,1,0:T(8,128)(2,1)S(1)}, bf16[64,16,512]{2,1,0:T(8,128)(2,1)}, u32[]{:S(2)}) copy-start(bf16[64,16,512]{2,1,0:T(8,128)(2,1)} %param.18) | copy-start | bytes 3145732

commit v2 on v1

v2 whole, which is shorter than its diff:
```python
import functools
import math

import jax
import jax.numpy as jnp
from jax import lax
from jax.experimental import pallas as pl
from jax.experimental.pallas import tpu as pltpu
from jax.sharding import PartitionSpec as P

HEADS = 64
KVH = 4
HD = 128
GROUP = HEADS // KVH
MAXCTX = 64
PAGE = 16
EPSILON = 1e-06
BLOCK = 512
TOGETHER = 4
CONTRACT_LAST = (((1,), (1,)), ((), ()))
VMEM = pl.BlockSpec(memory_space=pltpu.VMEM)
SMEM = pl.BlockSpec(memory_space=pltpu.SMEM)


def attention_kernel(
    tables, lengths, q_ref, own_key, own_value, keys, values, out_ref, q_turned, out_turned
):
    rows = q_ref.shape[0]
    pages = MAXCTX // PAGE
    tall, wide = TOGETHER * GROUP, TOGETHER * MAXCTX
    scale = 1.0 / math.sqrt(HD)
    for head in range(HEADS):
        q_turned[head // GROUP, pl.ds(head % GROUP * rows, rows), :] = q_ref[
            :, head * HD : (head + 1) * HD
        ].astype(jnp.float32)
    row_request = lax.broadcasted_iota(jnp.int32, (tall, wide), 0) // GROUP
    column = lax.broadcasted_iota(jnp.int32, (tall, wide), 1)
    own_row = lax.broadcasted_iota(jnp.int32, (tall, rows), 0) // GROUP
    own_column = lax.broadcasted_iota(jnp.int32, (tall, rows), 1)
    for first in range(0, rows, TOGETHER):
        limit = jnp.zeros((tall, wide), jnp.int32)
        for i in range(TOGETHER):
            limit = jnp.where(row_request == i, lengths[first + i], limit)
        place = column - row_request * MAXCTX
        live = (place >= 0) & (place < limit)
        is_own = own_column == own_row + first
        page_ids = [tables[first + i, j] for i in range(TOGETHER) for j in range(pages)]
        for kv in range(KVH):
            lanes = slice(kv * HD, (kv + 1) * HD)
            q = jnp.concatenate(
                [
                    q_turned[kv, pl.ds(first + i, GROUP, stride=rows), :]
                    for i in range(TOGETHER)
                ],
                axis=0,
            ).astype(jnp.bfloat16)
            k = jnp.concatenate([keys[page, :, lanes] for page in page_ids], axis=0)
            v = jnp.concatenate([values[page, :, lanes] for page in page_ids], axis=0)
            scores = (
                lax.dot_general(q, k, CONTRACT_LAST, preferred_element_type=jnp.float32) * scale
            )
            own_score = (
                lax.dot_general(
                    q, own_key[:, lanes], CONTRACT_LAST, preferred_element_type=jnp.float32
                )
                * scale
            )
            scores = jnp.where(live, scores, -jnp.inf)
            own_score = jnp.where(is_own, own_score, -jnp.inf)
            top = jnp.maximum(
                jnp.max(scores, axis=1, keepdims=True), jnp.max(own_score, axis=1, keepdims=True)
            )
            weights = jnp.exp(scores - top)
            own_weight = jnp.exp(own_score - top)
            total = jnp.sum(weights, axis=1, keepdims=True) + jnp.sum(
                own_weight, axis=1, keepdims=True
            )
            share = 1.0 / total
            blended = jnp.dot(
                (weights * share).astype(jnp.bfloat16), v, preferred_element_type=jnp.float32
            ) + jnp.dot(
                (own_weight * share).astype(jnp.bfloat16),
                own_value[:, lanes],
                preferred_element_type=jnp.float32,
            )
            for i in range(TOGETHER):
                out_turned[kv, pl.ds(first + i, GROUP, stride=rows), :] = blended[
                    i * GROUP : (i + 1) * GROUP
                ]
    held = out_ref.shape[2] // HD
    for head in range(HEADS):
        out_ref[head // held, :, head % held * HD : (head % held + 1) * HD] = out_turned[
            head // GROUP, pl.ds(head % GROUP * rows, rows), :
        ].astype(jnp.bfloat16)


def attend(queries, new_keys, new_values, key_pool, value_pool, tables, lengths, chips):
    rows = queries.shape[0]
    return pl.pallas_call(
        attention_kernel,
        out_shape=jax.ShapeDtypeStruct((chips, rows, HEADS * HD // chips), jnp.bfloat16),
        in_specs=[SMEM, SMEM, VMEM, VMEM, VMEM, VMEM, VMEM],
        out_specs=VMEM,
        scratch_shapes=[
            pltpu.VMEM((KVH, GROUP * rows, HD), jnp.float32),
            pltpu.VMEM((KVH, GROUP * rows, HD), jnp.float32),
        ],
        compiler_params=pltpu.CompilerParams(vmem_limit_bytes=24 << 20),
        cost_estimate=pl.CostEstimate(
            flops=600_000_000, bytes_accessed=5_000_000, transcendentals=300_000
        ),
        name="attention",
    )(tables, lengths, queries, new_keys, new_values, key_pool, value_pool)


def projection_kernel(masks, spot, x_ref, mine_ref, beside_ref, keep_ref, send_ref):
    chip, core = spot[0], spot[1]
    depth = mine_ref.shape[0]
    x = jnp.concatenate([x_ref[chip ^ mask] for mask in masks], axis=0)
    low, high = x[:, :depth], x[:, depth:]
    here = jnp.full(low.shape, core, jnp.int32) == 0
    mine = jnp.where(here, low, high)
    beside = jnp.where(here, high, low)
    summed = jnp.dot(mine, mine_ref[...], preferred_element_type=jnp.float32) + jnp.dot(
        beside, beside_ref[...], preferred_element_type=jnp.float32
    )
    summed = summed.astype(jnp.bfloat16)
    half = summed.shape[0] // 2
    keep_ref[...] = summed[:half].reshape(keep_ref.shape)
    send_ref[...] = summed[half:].reshape(send_ref.shape)


def project(regrouped, mine, beside, spot, masks, part, parts):
    chips, rows, depth_pair = regrouped.shape
    depth, width = mine.shape
    columns = width // parts
    shape = jax.ShapeDtypeStruct((chips // 2, rows, columns), jnp.bfloat16)
    weight_spec = pl.BlockSpec((depth, columns), lambda i: (0, part))
    return pl.pallas_call(
        functools.partial(projection_kernel, masks),
        out_shape=[shape, shape],
        grid=(1,),
        in_specs=[
            SMEM,
            pl.BlockSpec((chips, rows, depth_pair), lambda i: (0, 0, 0)),
            weight_spec,
            weight_spec,
        ],
        out_specs=[pl.BlockSpec(shape.shape, lambda i: (0, 0, 0))] * 2,
        compiler_params=pltpu.CompilerParams(vmem_limit_bytes=16 << 20),
        cost_estimate=pl.CostEstimate(
            flops=270_000_000, bytes_accessed=1_800_000, transcendentals=0
        ),
        name=f"projection_{part}",
    )(spot, regrouped, mine, beside)


def dispatch_kernel(
    keep_a, got_a, keep_b, got_b, residual, gain, placing, hidden_ref, normed_ref, sent_ref
):
    rows = residual.shape[0]
    halves = []
    at = 0
    for keep, got in ((keep_a, got_a), (keep_b, got_b)):
        span = keep.shape[1]
        halves.append(
            residual[:, at : at + span].astype(jnp.float32)
            + (keep[...].astype(jnp.float32) + got[...].astype(jnp.float32))
        )
        at += span
    hidden = jnp.concatenate(halves, axis=1)
    hidden_ref[...] = hidden
    mean_square = jnp.mean(hidden * hidden, axis=1, keepdims=True)
    normed = (hidden * lax.rsqrt(mean_square + EPSILON) * gain[...]).astype(jnp.bfloat16)
    normed_ref[...] = normed
    blocks = at // BLOCK
    stacked = jnp.concatenate(
        [normed[:, i * BLOCK : (i + 1) * BLOCK] for i in range(blocks)], axis=0
    )
    step = 512
    for i in range(0, placing.shape[0], step):
        sent_ref[pl.ds(i, step), :] = jnp.dot(
            placing[pl.ds(i, step), :], stacked, preferred_element_type=jnp.float32
        ).astype(jnp.bfloat16)


def dispatch(keep_a, got_a, keep_b, got_b, residual, gain, placing):
    rows, width = residual.shape
    return pl.pallas_call(
        dispatch_kernel,
        out_shape=[
            jax.ShapeDtypeStruct((rows, width), jnp.float32),
            jax.ShapeDtypeStruct((rows, width), jnp.bfloat16),
            jax.ShapeDtypeStruct((placing.shape[0], BLOCK), jnp.bfloat16),
        ],
        in_specs=[VMEM] * 7,
        out_specs=[VMEM] * 3,
        compiler_params=pltpu.CompilerParams(vmem_limit_bytes=16 << 20),
        cost_estimate=pl.CostEstimate(
            flops=270_000_000, bytes_accessed=4_000_000, transcendentals=16
        ),
        name="dispatch",
    )(keep_a, got_a, keep_b, got_b, residual, gain, placing)


def turning(blocks, capacity, sources, back):
    lines = blocks * capacity * sources
    left = lax.broadcasted_iota(jnp.int32, (lines, lines), 0)
    right = lax.broadcasted_iota(jnp.int32, (lines, lines), 1)
    if back:
        left, right = right, left
    wanted = left % sources * (blocks * capacity) + left // sources
    return (wanted == right).astype(jnp.float32).astype(jnp.bfloat16)


def expert_kernel(
    arrived, gate_ref, up_ref, down_ref, out_ref, rows_in, rows_out, gate_sum, up_sum, hidden
):
    step = pl.program_id(0)
    groups, lines, _ = rows_in.shape
    blocks = pl.num_programs(0) // 2
    sources = arrived.shape[0] // groups
    each = lines // blocks
    capacity = each // sources

    @pl.when(step == 0)
    def _():
        turn = turning(blocks, capacity, sources, False)
        for g in range(groups):
            rows_in[g] = jnp.dot(
                turn,
                arrived[g * sources : (g + 1) * sources].reshape(lines, BLOCK),
                preferred_element_type=jnp.float32,
            ).astype(jnp.bfloat16)

    @pl.when(step < blocks)
    def _():
        at = pl.ds(pl.multiple_of(step * each, each), each)
        x = rows_in[:, at, :].reshape(groups * each, BLOCK)
        gate = jnp.dot(x, gate_ref[0], preferred_element_type=jnp.float32)
        up = jnp.dot(x, up_ref[0], preferred_element_type=jnp.float32)

        @pl.when(step == 0)
        def _():
            gate_sum[...] = gate
            up_sum[...] = up

        @pl.when(step > 0)
        def _():
            gate_sum[...] += gate
            up_sum[...] += up

    @pl.when(step == blocks - 1)
    def _():
        gate = gate_sum[...]
        hidden[...] = (gate / (1.0 + jnp.exp(-gate)) * up_sum[...]).astype(jnp.bfloat16)

    @pl.when(step >= blocks)
    def _():
        at = pl.ds(pl.multiple_of((step - blocks) * each, each), each)
        y = jnp.dot(hidden[...], down_ref[0], preferred_element_type=jnp.float32)
        rows_out[:, at, :] = y.astype(jnp.bfloat16).reshape(groups, each, BLOCK)

    @pl.when(step == 2 * blocks - 1)
    def _():
        turn = turning(blocks, capacity, sources, True)
        for g in range(groups):
            out_ref[g * sources : (g + 1) * sources] = (
                jnp.dot(turn, rows_out[g], preferred_element_type=jnp.float32)
                .astype(jnp.bfloat16)
                .reshape(sources, lines // sources, BLOCK)
            )


def run_expert(arrived, gate, up, down):
    experts, lines, _ = arrived.shape
    _, width, units = gate.shape
    blocks = width // BLOCK
    groups = 8
    capacity = lines // blocks
    token_rows = experts * capacity
    whole = pl.BlockSpec(arrived.shape, lambda i: (0, 0, 0))
    inward = pl.BlockSpec((1, BLOCK, units), lambda i: (0, jnp.minimum(i, blocks - 1), 0))
    turned = pltpu.VMEM((groups, experts // groups * lines, BLOCK), jnp.bfloat16)
    return pl.pallas_call(
        expert_kernel,
        out_shape=jax.ShapeDtypeStruct(arrived.shape, jnp.bfloat16),
        grid=(2 * blocks,),
        in_specs=[
            whole,
            inward,
            inward,
            pl.BlockSpec((1, units, BLOCK), lambda i: (0, 0, jnp.maximum(i - blocks, 0))),
        ],
        out_specs=whole,
        scratch_shapes=[
            turned,
            turned,
            pltpu.VMEM((token_rows, units), jnp.float32),
            pltpu.VMEM((token_rows, units), jnp.float32),
            pltpu.VMEM((token_rows, units), jnp.bfloat16),
        ],
        compiler_params=pltpu.CompilerParams(vmem_limit_bytes=40 << 20),
        cost_estimate=pl.CostEstimate(
            flops=5_900_000_000, bytes_accessed=23_000_000, transcendentals=200_000
        ),
        name="expert",
    )(arrived, gate, up, down)


def combine_kernel(mixing, returned, hidden, out_ref):
    rows = hidden.shape[0]
    mixed = jnp.dot(mixing[...], returned[...], preferred_element_type=jnp.float32)
    half = mixed.shape[0] // 2
    mixed = mixed[:half] + mixed[half:]
    for i in range(half // rows):
        lanes = slice(i * BLOCK, (i + 1) * BLOCK)
        out_ref[:, lanes] = (hidden[:, lanes] + mixed[i * rows : (i + 1) * rows]).astype(
            jnp.bfloat16
        )


def combine(mixing, returned, hidden):
    return pl.pallas_call(
        combine_kernel,
        out_shape=jax.ShapeDtypeStruct(hidden.shape, jnp.bfloat16),
        in_specs=[VMEM] * 3,
        out_specs=VMEM,
        compiler_params=pltpu.CompilerParams(vmem_limit_bytes=16 << 20),
        cost_estimate=pl.CostEstimate(
            flops=540_000_000, bytes_accessed=3_500_000, transcendentals=0
        ),
        name="combine",
    )(mixing, returned, hidden)


def route_gates(logits, routes):
    matches = routes[:, :, None] == jnp.arange(logits.shape[1], dtype=jnp.int32)[None, None, :]
    chosen = jnp.sum(jnp.where(matches, logits[:, None, :], 0.0), axis=-1)
    raised = jnp.exp(chosen)
    return raised / jnp.sum(raised, axis=1, keepdims=True)


def rank_of(flat_routes, experts):
    onehot = (flat_routes[:, None] == jnp.arange(experts, dtype=jnp.int32)[None, :]).astype(
        jnp.int32
    )
    earlier = jnp.cumsum(onehot, axis=0) - onehot
    return jnp.sum(earlier * onehot, axis=1)


def add(left, right):
    return (left.astype(jnp.float32) + right.astype(jnp.float32)).astype(jnp.bfloat16)


def scatter_sum(regrouped, mine, beside, spot, peers):
    jump = {"y": 1, "Y": 3, "z": 4, "Z": 12}

    def swap(array, way):
        return lax.ppermute(array, "dev", [(i, i ^ (2 * jump[way])) for i in range(peers)])

    orders = ("yYzZ", "YyzZ", "zZyY", "ZzyY")
    kept, got = [], []
    for part, order in enumerate(orders):
        masks = []
        for place in range(16):
            mask = 0
            for bit, way in enumerate(order):
                if place >> (3 - bit) & 1:
                    mask ^= jump[way]
            masks.append(mask)
        keep, send = project(regrouped, mine, beside, spot, tuple(masks), part, len(orders))
        kept.append(keep)
        got.append(swap(send, order[0]))
    for part, order in enumerate(orders):
        both = add(kept[part], got[part])
        half = both.shape[0] // 2
        kept[part], got[part] = both[:half], swap(both[half:], order[1])
    merged = []
    for pair in (0, 2):
        way, last = orders[pair][2:]
        both = jnp.concatenate(
            [add(kept[pair], got[pair]), add(kept[pair + 1], got[pair + 1])], axis=2
        )
        merged.append((both[:2], swap(both[2:], way), last))
    ends = []
    for keep, arrived, last in merged:
        both = add(keep, arrived)
        ends += [both[0], swap(both[1], last)]
    return ends


def shards(
    queries,
    new_keys,
    new_values,
    key_pages,
    value_pages,
    block_tables,
    context_lengths,
    out_weight,
    residual,
    norm_gain,
    router_weight,
    routes,
    expert_gate,
    expert_up,
    expert_down,
):
    rows, width = residual.shape
    peers = lax.axis_size("dev")
    chips = peers // 2
    place = lax.axis_index("dev")
    spot = jnp.stack([place // 2, place % 2])
    same_core = [[2 * chip + side for chip in range(chips)] for side in range(2)]
    experts = router_weight.shape[1]
    capacity = 2
    blocks = width // BLOCK
    lines = blocks * capacity

    weight_beside = lax.ppermute(out_weight, "dev", [(i, i ^ 1) for i in range(peers)])
    attended = attend(
        queries,
        new_keys,
        new_values,
        key_pages,
        value_pages,
        block_tables,
        context_lengths,
        chips,
    )
    regrouped = lax.all_to_all(
        attended, "dev", split_axis=0, concat_axis=0, axis_index_groups=same_core, tiled=True
    )
    ends = scatter_sum(regrouped, out_weight, weight_beside, spot, peers)

    rank = rank_of(routes.reshape(-1), experts).reshape(rows, -1)
    block_ids = jnp.arange(blocks, dtype=jnp.int32)
    target = (routes * lines + rank)[None] + (block_ids * capacity)[:, None, None]
    target = target.reshape(blocks * rows, -1)
    line = jnp.arange(experts * lines, dtype=jnp.int32)
    placed = line[:, None] == target[:, 0][None, :]
    for k in range(1, target.shape[1]):
        placed = placed | (line[:, None] == target[:, k][None, :])
    placing = placed.astype(jnp.bfloat16)

    hidden_state, normed, sent = dispatch(*ends, residual, norm_gain[None], placing)
    arrived = lax.all_to_all(
        sent.reshape(experts, lines, BLOCK),
        ("attn", "dev"),
        split_axis=0,
        concat_axis=0,
        tiled=True,
    )
    output_rows = run_expert(arrived, expert_gate, expert_up, expert_down)
    returned = lax.all_to_all(
        output_rows, ("attn", "dev"), split_axis=0, concat_axis=0, tiled=True
    ).reshape(experts * lines, BLOCK)

    logits = jnp.dot(normed, router_weight, preferred_element_type=jnp.float32)
    gate_values = route_gates(logits, routes)
    gate_of = jnp.tile(gate_values, (blocks, 1))
    mixing = jnp.zeros((blocks * rows, experts * lines), jnp.float32)
    for k in range(target.shape[1]):
        mixing = jnp.where(line[None, :] == target[:, k][:, None], gate_of[:, k][:, None], mixing)
    high = mixing.astype(jnp.bfloat16)
    low = (mixing - high.astype(jnp.float32)).astype(jnp.bfloat16)
    return combine(jnp.concatenate([high, low], axis=0), returned, hidden_state)


def solution(mesh):
    in_specs = (
        P(("attn", "dev"), None),
        P(("attn", "dev"), None),
        P(("attn", "dev"), None),
        P(("attn", "dev"), None, None),
        P(("attn", "dev"), None, None),
        P(("attn", "dev"), None),
        P(("attn", "dev")),
        P("dev", None),
        P(("attn", "dev"), None),
        P(),
        P(),
        P(("attn", "dev"), None),
        P(("attn", "dev"), None, None),
        P(("attn", "dev"), None, None),
        P(("attn", "dev"), None, None),
    )
    out_specs = P(("attn", "dev"), None)
    return jax.shard_map(shards, mesh=mesh, in_specs=in_specs, out_specs=out_specs, check_vma=False)
```

time: 164 us -> 162 us (0.988)
  Pallas kernels: 0 us -> 31.1 us
  other arithmetic: 34.8 us -> 6.96 us
  matrix products: 22.8 us -> 0.24 us
  blocking collectives: 37.8 us -> 46.7 us
  starting transfers between devices: 18.9 us -> 25 us
  waiting for transfers between devices: 35.9 us -> 40.6 us
  local copies, waits for them, and re-layouts: 13 us -> 10.4 us
    pallas_call x0 -> x8, Pallas kernels: none -> 31.1 us  [the longest x1 16.5 us: run_expert(): pl.pallas_call(expert_kernel, out_shape=jax.ShapeDtypeStruct(arrived.shap...]
    dot_general x9 -> x0, matrix products: 22.5 us -> none  [the longest x1 10.5 us: shards(): jnp.dot(expert_hidden, expert_down[0], preferred_element_type=jnp.float32)]
    reduce_sum x5 -> x1, other arithmetic: 16.3 us -> 0.17 us  [rank_of(): return jnp.sum(earlier * onehot, axis=1)]
    reduce_or x1 -> x0, other arithmetic: 15.2 us -> none  [shards(): placing = jnp.any(hit, axis=2).astype(jnp.bfloat16)]
    ppermute x0 -> x12, starting transfers between devices: none -> 11.1 us  [swap(): lax.ppermute(array, 'dev', [(i, i ^ 2 * jump[way]) for i in range(peers)])]
    all_to_all x1, blocking collectives: 37.8 us -> 46.7 us  [shards(): lax.all_to_all(sent.reshape(experts, lines, BLOCK), ('attn', 'dev'), spli...]
    ppermute x0 -> x12, waiting for transfers between devices: none -> 8.27 us  [swap(): lax.ppermute(array, 'dev', [(i, i ^ 2 * jump[way]) for i in range(peers)])]
    unnamed x37 -> x46, local copies, waits for them, and re-layouts: 3.93 us -> 9.66 us
  transfers between devices with their start and end apart: 4 -> 15, of which waited for: 3 -> 11; matrix products, arithmetic and copies ran while one was open for 25% -> 5% of each run, Pallas kernels for 0% -> 7%
where the time goes in v2:
time: 162 us
  blocking collectives  46.7 us (29%)
  waiting for transfers between devices  40.6 us (25%)
  Pallas kernels  31.1 us (19%)
  starting transfers between devices  25 us (15%)
  local copies, waits for them, and re-layouts  10.4 us (6%)
  other arithmetic  6.96 us (4%)
    all_to_all x1, blocking collectives, shards(): lax.all_to_all(sent.reshape(experts, lines, BLOCK), ('attn', 'dev'), spli...  46.7 us
    all_to_all x1, waiting for transfers between devices, shards(): lax.all_to_all(output_rows, ('attn', 'dev'), split_axis=0, concat_axis=0,...  25.1 us
    pallas_call x1, Pallas kernels, run_expert(): pl.pallas_call(expert_kernel, out_shape=jax.ShapeDtypeStruct(arrived.shap...  16.5 us
    ppermute x12, starting transfers between devices, swap(): lax.ppermute(array, 'dev', [(i, i ^ 2 * jump[way]) for i in range(peers)])  11.1 us
    unnamed x46, local copies, waits for them, and re-layouts  9.66 us
    ppermute x12, waiting for transfers between devices, swap(): lax.ppermute(array, 'dev', [(i, i ^ 2 * jump[way]) for i in range(peers)])  8.27 us
    all_to_all x1, starting transfers between devices, shards(): lax.all_to_all(attended, 'dev', split_axis=0, concat_axis=0, axis_index_g...  7.93 us
    all_to_all x1, waiting for transfers between devices, shards(): lax.all_to_all(attended, 'dev', split_axis=0, concat_axis=0, axis_index_g...  7.24 us
  transfers between devices with their start and end apart: 15, of which 11 were waited for; matrix products, arithmetic and copies ran while one was open for 5% of the time, Pallas kernels for 7%

profile of v2, /device:TPU:1, one launch (start us, length us, event | category | flops | bytes accessed | tf_op | source)
XLA Modules:
  0.0 161.5 jit_solution(1398037571656675057)
XLA Ops:
  0.0 1.4 collective-permute-start
  1.4 0.8 copy.35.tables
  2.2 1.2 copy-done.5
  3.4 1.2 copy-done.6
  4.6 0.9 copy-done.7
  7.7 6.2 %attention.1 = bf16[16,16,512]{2,1,0:T(8,128)(2,1)S(1)} custom-call(s32[16,4]{1,0:T(8,128)S(1)} %copy.35.tables, s32[16]{0:T(128)S(1)} %copy-done.10, bf16[16,8192]{1,0:T(8,128)(2,1)S(1)} %copy-done.7, bf16[16,512]{1,0:T(8,128)(2,1)S(1)} %copy-done.8, bf16[16,512]{1,0:T(8,128)(2,1)S(1)} %copy-done.9, bf16[64,16,512]{2,1,0:T(8,128)(2,1)S(1)} %copy-done.5, ...), custom_call_target="tpu_custom_call" | custom-call | flops 600000000 | bytes 5000000 | tf_op jit(solution)/shard_map/attention/pallas_call | solution.py:99
  14.6 7.9 %all-to-all-start = ((bf16[16,16,512]{2,1,0:T(8,128)(2,1)}), bf16[16,16,512]{2,1,0:T(8,128)(2,1)S(1)}, u32[]{:S(2)}, u32[]{:S(2)}) async-start(bf16[16,16,512]{2,1,0:T(8,128)(2,1)} %copy-done.4), calls=%async_computation | async-start | bytes 524288 | tf_op jit(solution)/shard_map/all_to_all | solution.py:432
  23.7 7.2 %all-to-all-done.x_ref = bf16[16,16,512]{2,1,0:T(8,128)(2,1)S(1)} async-done(((bf16[16,16,512]{2,1,0:T(8,128)(2,1)}), bf16[16,16,512]{2,1,0:T(8,128)(2,1)S(1)}, u32[]{:S(2)}, u32[]{:S(2)}) %all-to-all-start) | async-done | bytes 262176 | tf_op jit(solution)/shard_map/all_to_all | solution.py:432
  30.9 1.5 projection_3.1
  33.1 1.5 projection_2.1
  34.8 1.5 projection_1.1
  37.0 1.7 %projection_0.1 = (bf16[8,16,1024]{2,1,0:T(8,128)(2,1)S(1)}, bf16[8,16,1024]{2,1,0:T(8,128)(2,1)S(1)}) custom-call(s32[2]{0:T(128)S(1)} %pad_add_fusion.spot, bf16[16,16,512]{2,1,0:T(8,128)(2,1)S(1)} %all-to-all-done.x_ref, bf16[256,4096]{1,0:T(8,128)(2,1)S(1)} %copy-done.1, bf16[256,4096]{1,0:T(8,128)(2,1)} %collective-permute-done.beside_ref), custom_call_target="tpu_custom_call" | custom-call | flops 270000000 | bytes 1800000 | tf_op jit(solution)/shard_map/projection_0/pallas_call | solution.py:139
  38.7 1.5 collective-permute-done.9
  41.1 2.2 %collective-permute-start.8 = (bf16[4,16,1024]{2,1,0:T(8,128)(2,1)S(1)}, bf16[4,16,1024]{2,1,0:T(8,128)(2,1)S(1)}, u32[]{:S(2)}, u32[]{:S(2)}) collective-permute-start(bf16[4,16,1024]{2,1,0:T(8,128)(2,1)S(1)} %slice.145), channel_id=1, source_target_pairs={{0,24},{1,25},{2,26},{3,27},{4,28},{5,29},{6,30},{7,31},{8,16},{9,... | collective-permute-start | bytes 393224 | tf_op jit(solution)/shard_map/ppermute | solution.py:360
  44.5 2.4 %collective-permute-start.2 = (bf16[4,16,1024]{2,1,0:T(8,128)(2,1)S(1)}, bf16[4,16,1024]{2,1,0:T(8,128)(2,1)S(1)}, u32[]{:S(2)}, u32[]{:S(2)}) collective-permute-start(bf16[4,16,1024]{2,1,0:T(8,128)(2,1)S(1)} %slice.137), channel_id=1, source_target_pairs={{0,6},{1,7},{2,4},{3,5},{4,2},{5,3},{6,0},{7,1},{8,14},{9,15},{10,... | collective-permute-start | bytes 393224 | tf_op jit(solution)/shard_map/ppermute | solution.py:360
  47.2 1.0 collective-permute-done.4
  48.2 1.8 %collective-permute-done.2 = bf16[4,16,1024]{2,1,0:T(8,128)(2,1)S(1)} collective-permute-done((bf16[4,16,1024]{2,1,0:T(8,128)(2,1)S(1)}, bf16[4,16,1024]{2,1,0:T(8,128)(2,1)S(1)}, u32[]{:S(2)}, u32[]{:S(2)}) %collective-permute-start.2) | collective-permute-done | bytes 131104 | tf_op jit(solution)/shard_map/ppermute | solution.py:360
  50.0 1.2 collective-permute-start.5
  51.9 1.5 collective-permute-start.12
  54.0 2.1 %collective-permute-start.6 = (bf16[16,2048]{1,0:T(8,128)(2,1)S(1)}, bf16[16,2048]{1,0:T(8,128)(2,1)S(1)}, u32[]{:S(2)}, u32[]{:S(2)}) collective-permute-start(bf16[16,2048]{1,0:T(8,128)(2,1)S(1)} %get-tuple-element.31), channel_id=1, source_target_pairs={{0,24},{1,25},{2,26},{3,27},{4,28},{5,29},{6,30},{7,31},{8,16},{9,... | collective-permute-start | bytes 196616 | tf_op jit(solution)/shard_map/ppermute | solution.py:360
  56.1 1.0 fusion.7.placing
  57.1 1.3 collective-permute-done.6.got_a
  58.4 0.9 dispatch.1
  59.3 46.7 %all_to_all.15.arrived = bf16[128,16,512]{2,1,0:T(8,128)(2,1)S(1)} all-to-all(bf16[128,16,512]{2,1,0:T(8,128)(2,1)S(1)} %bitcast.54), channel_id=1, replica_groups=mesh['attn'=4,'dev'=32] {'attn','dev'}, dimensions={0} | all-to-all | bytes 4194304 | tf_op jit(solution)/shard_map/all_to_all | solution.py:448
  106.0 16.5 %expert.1 = bf16[128,16,512]{2,1,0:T(8,128)(2,1)S(1)} custom-call(bf16[128,16,512]{2,1,0:T(8,128)(2,1)S(1)} %all_to_all.15.arrived, bf16[1,4096,768]{2,1,0:T(8,128)(2,1)S(1)} %bitcast.53, bf16[1,4096,768]{2,1,0:T(8,128)(2,1)} %up_ref.1, bf16[1,768,4096]{2,1,0:T(8,128)(2,1)} %down_ref.1), custom_call_target="tpu_custom_call" | custom-call | flops 5900000256 | bytes 23000000 | tf_op jit(solution)/shard_map/expert/pallas_call | solution.py:285
  122.5 1.4 copy-done.2
  123.8 4.5 %all-to-all-start.2 = ((bf16[128,16,512]{2,1,0:T(8,128)(2,1)}), bf16[128,16,512]{2,1,0:T(8,128)(2,1)S(1)}, u32[]{:S(2)}, u32[]{:S(2)}) async-start(bf16[128,16,512]{2,1,0:T(8,128)(2,1)} %copy-done.2), calls=%async_computation.2 | async-start | bytes 4194304 | tf_op jit(solution)/shard_map/all_to_all | solution.py:456
  129.2 3.5 %subtract_convert_fusion = (bf16[128,2048]{1,0:T(8,128)(2,1)S(1)}, bf16[128,2048]{1,0:T(8,128)(2,1)S(1)}) fusion(f32[128]{0:T(128)S(1)} %get-tuple-element.34, s32[128]{0:T(128)S(1)} %get-tuple-element.41, f32[128]{0:T(128)S(1)} %get-tuple-element.35, s32[128]{0:T(128)} %copy-done.18, f32[128]{0:T(128)S(1)} %get-tuple-element.36, s32[128]{0:T(128)} %copy-done.17, ...), kind=kLoop, calls=%fused_computation.1 | loop fusion | flops 7077888 | bytes 1056768 | tf_op jit(solution)/shard_map/convert_element_type | solution.py:467
  132.7 1.1 pad_maximum_fusion.mixing
  133.8 25.1 %all-to-all-done.2 = bf16[128,16,512]{2,1,0:T(8,128)(2,1)S(1)} async-done(((bf16[128,16,512]{2,1,0:T(8,128)(2,1)}), bf16[128,16,512]{2,1,0:T(8,128)(2,1)S(1)}, u32[]{:S(2)}, u32[]{:S(2)}) %all-to-all-start.2) | async-done | bytes 2097184 | tf_op jit(solution)/shard_map/all_to_all | solution.py:456
  158.9 1.2 copy-done.3
  160.1 1.4 combine.1
  (98 shorter events, 9.7 us)
Async XLA Ops:
  0.0 128.4 %copy-start = (bf16[4096,128]{1,0:T(8,128)(2,1)S(1)}, bf16[4096,128]{1,0:T(8,128)(2,1)}, u32[]{:S(2)}) copy-start(bf16[4096,128]{1,0:T(8,128)(2,1)} %param.25) | copy-start | bytes 3145732
  0.0 30.9 %copy-start.1 = (bf16[256,4096]{1,0:T(8,128)(2,1)S(1)}, bf16[256,4096]{1,0:T(8,128)(2,1)}, u32[]{:S(2)}) copy-start(bf16[256,4096]{1,0:T(8,128)(2,1)} %mine_ref.7) | copy-start | bytes 6291460
  0.0 30.9 %collective-permute-start = (bf16[256,4096]{1,0:T(8,128)(2,1)}, bf16[256,4096]{1,0:T(8,128)(2,1)}, u32[]{:S(2)}, u32[]{:S(2)}) collective-permute-start(bf16[256,4096]{1,0:T(8,128)(2,1)} %mine_ref.7), channel_id=1, source_target_pairs={{0,1},{1,0},{2,3},{3,2},{4,5},{5,4},{6,7},{7,6},{8,9},{9,8},{10,11... | collective-permute-start | bytes 6291464 | tf_op jit(solution)/shard_map/ppermute | solution.py:421
  2.2 1.2 copy-start.5
  3.4 1.2 copy-start.6
  7.7 14.9 %copy-start.13 = (s32[16,8]{0,1:T(8,128)S(1)}, s32[16,8]{0,1:T(8,128)}, u32[]{:S(2)}) copy-start(s32[16,8]{0,1:T(8,128)} %param.26) | copy-start | bytes 1540
  14.6 16.3 %all-to-all-start = ((bf16[16,16,512]{2,1,0:T(8,128)(2,1)}), bf16[16,16,512]{2,1,0:T(8,128)(2,1)S(1)}, u32[]{:S(2)}, u32[]{:S(2)}) async-start(bf16[16,16,512]{2,1,0:T(8,128)(2,1)} %copy-done.4), calls=%async_computation | async-start | bytes 524288 | tf_op jit(solution)/shard_map/all_to_all | solution.py:432
  32.4 7.8 %collective-permute-start.9 = (bf16[8,16,1024]{2,1,0:T(8,128)(2,1)S(1)}, bf16[8,16,1024]{2,1,0:T(8,128)(2,1)S(1)}, u32[]{:S(2)}, u32[]{:S(2)}) collective-permute-start(bf16[8,16,1024]{2,1,0:T(8,128)(2,1)S(1)} %get-tuple-element.23), channel_id=1, source_target_pairs={{0,24},{1,25},{2,26},{3,27},{4,28},{5,29},{6,30},{7,31},{8,16},{9,... | collective-permute-start | bytes 786440 | tf_op jit(solution)/shard_map/ppermute | solution.py:360
  33.1 23.0 %copy-start.14 = (s32[128]{0:T(128)}, s32[128]{0:T(128)S(1)}, u32[]{:S(2)}) copy-start(s32[128]{0:T(128)S(1)} %get-tuple-element.43) | copy-start | bytes 1540
  33.1 23.0 %copy-start.15 = (s32[128]{0:T(128)}, s32[128]{0:T(128)S(1)}, u32[]{:S(2)}) copy-start(s32[128]{0:T(128)S(1)} %get-tuple-element.44) | copy-start | bytes 1540
  33.1 23.0 %copy-start.16 = (s32[128]{0:T(128)}, s32[128]{0:T(128)S(1)}, u32[]{:S(2)}) copy-start(s32[128]{0:T(128)S(1)} %get-tuple-element.45) | copy-start | bytes 1540
  33.1 23.0 %copy-start.17 = (s32[128]{0:T(128)}, s32[128]{0:T(128)S(1)}, u32[]{:S(2)}) copy-start(s32[128]{0:T(128)S(1)} %get-tuple-element.46) | copy-start | bytes 1540
  33.1 23.0 %copy-start.18 = (s32[128]{0:T(128)}, s32[128]{0:T(128)S(1)}, u32[]{:S(2)}) copy-start(s32[128]{0:T(128)S(1)} %get-tuple-element.47) | copy-start | bytes 1540
  33.1 23.0 %copy-start.19 = (s32[128]{0:T(128)}, s32[128]{0:T(128)S(1)}, u32[]{:S(2)}) copy-start(s32[128]{0:T(128)S(1)} %get-tuple-element.48) | copy-start | bytes 1540
  34.7 6.3 %collective-permute-start.7 = (bf16[8,16,1024]{2,1,0:T(8,128)(2,1)S(1)}, bf16[8,16,1024]{2,1,0:T(8,128)(2,1)S(1)}, u32[]{:S(2)}, u32[]{:S(2)}) collective-permute-start(bf16[8,16,1024]{2,1,0:T(8,128)(2,1)S(1)} %get-tuple-element.21), channel_id=1, source_target_pairs={{0,8},{1,9},{2,10},{3,11},{4,12},{5,13},{6,14},{7,15},{8,0},{9,1},... | collective-permute-start | bytes 786440 | tf_op jit(solution)/shard_map/ppermute | solution.py:360
  36.3 7.5 %collective-permute-start.3 = (bf16[8,16,1024]{2,1,0:T(8,128)(2,1)S(1)}, bf16[8,16,1024]{2,1,0:T(8,128)(2,1)S(1)}, u32[]{:S(2)}, u32[]{:S(2)}) collective-permute-start(bf16[8,16,1024]{2,1,0:T(8,128)(2,1)S(1)} %get-tuple-element.19), channel_id=1, source_target_pairs={{0,6},{1,7},{2,4},{3,5},{4,2},{5,3},{6,0},{7,1},{8,14},{9,15},{10,... | collective-permute-start | bytes 786440 | tf_op jit(solution)/shard_map/ppermute | solution.py:360
  37.0 69.0 %slice-start = ((s8[6291456]{0:T(1024)(128)(4,1)}), s8[4194304]{0:T(1024)(128)(4,1)S(1)}, s32[]{:S(2)}) async-start(s8[6291456]{0:T(1024)(128)(4,1)} %bitcast.52), calls=%async_computation.3 | async-start | bytes 8388608
  38.6 5.8 %collective-permute-start.1 = (bf16[8,16,1024]{2,1,0:T(8,128)(2,1)S(1)}, bf16[8,16,1024]{2,1,0:T(8,128)(2,1)S(1)}, u32[]{:S(2)}, u32[]{:S(2)}) collective-permute-start(bf16[8,16,1024]{2,1,0:T(8,128)(2,1)S(1)} %get-tuple-element.17), channel_id=1, source_target_pairs={{0,2},{1,3},{2,0},{3,1},{4,6},{5,7},{6,4},{7,5},{8,10},{9,11},{10,... | collective-permute-start | bytes 786440 | tf_op jit(solution)/shard_map/ppermute | solution.py:360
  40.4 6.6 %collective-permute-start.10 = (bf16[4,16,1024]{2,1,0:T(8,128)(2,1)S(1)}, bf16[4,16,1024]{2,1,0:T(8,128)(2,1)S(1)}, u32[]{:S(2)}, u32[]{:S(2)}) collective-permute-start(bf16[4,16,1024]{2,1,0:T(8,128)(2,1)S(1)} %slice.147), channel_id=1, source_target_pairs={{0,8},{1,9},{2,10},{3,11},{4,12},{5,13},{6,14},{7,15},{8,0},{9,1},... | collective-permute-start | bytes 393224 | tf_op jit(solution)/shard_map/ppermute | solution.py:360
  41.1 5.9 %collective-permute-start.8 = (bf16[4,16,1024]{2,1,0:T(8,128)(2,1)S(1)}, bf16[4,16,1024]{2,1,0:T(8,128)(2,1)S(1)}, u32[]{:S(2)}, u32[]{:S(2)}) collective-permute-start(bf16[4,16,1024]{2,1,0:T(8,128)(2,1)S(1)} %slice.145), channel_id=1, source_target_pairs={{0,24},{1,25},{2,26},{3,27},{4,28},{5,29},{6,30},{7,31},{8,16},{9,... | collective-permute-start | bytes 393224 | tf_op jit(solution)/shard_map/ppermute | solution.py:360
  43.9 4.2 %collective-permute-start.4 = (bf16[4,16,1024]{2,1,0:T(8,128)(2,1)S(1)}, bf16[4,16,1024]{2,1,0:T(8,128)(2,1)S(1)}, u32[]{:S(2)}, u32[]{:S(2)}) collective-permute-start(bf16[4,16,1024]{2,1,0:T(8,128)(2,1)S(1)} %slice.139), channel_id=1, source_target_pairs={{0,2},{1,3},{2,0},{3,1},{4,6},{5,7},{6,4},{7,5},{8,10},{9,11},{10,... | collective-permute-start | bytes 393224 | tf_op jit(solution)/shard_map/ppermute | solution.py:360
  44.5 5.4 %collective-permute-start.2 = (bf16[4,16,1024]{2,1,0:T(8,128)(2,1)S(1)}, bf16[4,16,1024]{2,1,0:T(8,128)(2,1)S(1)}, u32[]{:S(2)}, u32[]{:S(2)}) collective-permute-start(bf16[4,16,1024]{2,1,0:T(8,128)(2,1)S(1)} %slice.137), channel_id=1, source_target_pairs={{0,6},{1,7},{2,4},{3,5},{4,2},{5,3},{6,0},{7,1},{8,14},{9,15},{10,... | collective-permute-start | bytes 393224 | tf_op jit(solution)/shard_map/ppermute | solution.py:360
  47.0 11.4 %copy-start.11 = (bf16[16,4096]{1,0:T(8,128)(2,1)S(1)}, bf16[16,4096]{1,0:T(8,128)(2,1)}, u32[]{:S(2)}) copy-start(bf16[16,4096]{1,0:T(8,128)(2,1)} %residual.1) | copy-start | bytes 393220
  47.0 11.4 %copy-start.12 = (f32[4096]{0:T(1024)S(1)}, f32[4096]{0:T(1024)}, u32[]{:S(2)}) copy-start(f32[4096]{0:T(1024)} %param.24) | copy-start | bytes 49156
  47.0 59.0 %slice-start.1 = ((s8[6291456]{0:T(1024)(128)(4,1)}), s8[2097152]{0:T(1024)(128)(4,1)S(1)}, s32[]{:S(2)}) async-start(s8[6291456]{0:T(1024)(128)(4,1)} %bitcast.52), calls=%async_computation.4 | async-start | bytes 4194304
  47.1 4.7 %collective-permute-start.11 = (bf16[2,16,2048]{2,1,0:T(8,128)(2,1)S(1)}, bf16[2,16,2048]{2,1,0:T(8,128)(2,1)S(1)}, u32[]{:S(2)}, u32[]{:S(2)}) collective-permute-start(bf16[2,16,2048]{2,1,0:T(8,128)(2,1)S(1)} %pad_maximum_fusion.1), channel_id=1, source_target_pairs={{0,2},{1,3},{2,0},{3,1},{4,6},{5,7},{6,4},{7,5},{8,10},{9,11},{10,... | collective-permute-start | bytes 393224 | tf_op jit(solution)/shard_map/ppermute | solution.py:360
  50.0 3.9 %collective-permute-start.5 = (bf16[2,16,2048]{2,1,0:T(8,128)(2,1)S(1)}, bf16[2,16,2048]{2,1,0:T(8,128)(2,1)S(1)}, u32[]{:S(2)}, u32[]{:S(2)}) collective-permute-start(bf16[2,16,2048]{2,1,0:T(8,128)(2,1)S(1)} %pad_maximum_fusion.2), channel_id=1, source_target_pairs={{0,8},{1,9},{2,10},{3,11},{4,12},{5,13},{6,14},{7,15},{8,0},{9,1},... | collective-permute-start | bytes 393224 | tf_op jit(solution)/shard_map/ppermute | solution.py:360
  51.9 5.2 %collective-permute-start.12 = (bf16[16,2048]{1,0:T(8,128)(2,1)S(1)}, bf16[16,2048]{1,0:T(8,128)(2,1)S(1)}, u32[]{:S(2)}, u32[]{:S(2)}) collective-permute-start(bf16[16,2048]{1,0:T(8,128)(2,1)S(1)} %get-tuple-element.29), channel_id=1, source_target_pairs={{0,6},{1,7},{2,4},{3,5},{4,2},{5,3},{6,0},{7,1},{8,14},{9,15},{10,... | collective-permute-start | bytes 196616 | tf_op jit(solution)/shard_map/ppermute | solution.py:360
  54.0 4.4 %collective-permute-start.6 = (bf16[16,2048]{1,0:T(8,128)(2,1)S(1)}, bf16[16,2048]{1,0:T(8,128)(2,1)S(1)}, u32[]{:S(2)}, u32[]{:S(2)}) collective-permute-start(bf16[16,2048]{1,0:T(8,128)(2,1)S(1)} %get-tuple-element.31), channel_id=1, source_target_pairs={{0,24},{1,25},{2,26},{3,27},{4,28},{5,29},{6,30},{7,31},{8,16},{9,... | collective-permute-start | bytes 196616 | tf_op jit(solution)/shard_map/ppermute | solution.py:360
  122.5 1.4 copy-start.2
  123.8 35.1 %all-to-all-start.2 = ((bf16[128,16,512]{2,1,0:T(8,128)(2,1)}), bf16[128,16,512]{2,1,0:T(8,128)(2,1)S(1)}, u32[]{:S(2)}, u32[]{:S(2)}) async-start(bf16[128,16,512]{2,1,0:T(8,128)(2,1)} %copy-done.2), calls=%async_computation.2 | async-start | bytes 4194304 | tf_op jit(solution)/shard_map/all_to_all | solution.py:456
  158.9 1.2 copy-start.3
  (5 other events, 3.7 us)

commit v3 on v2

v3 whole, which is shorter than its diff:
```python
import functools
import math

import jax
import jax.numpy as jnp
from jax import lax
from jax.experimental import pallas as pl
from jax.experimental.pallas import tpu as pltpu
from jax.sharding import PartitionSpec as P

HEADS = 64
KVH = 4
HD = 128
GROUP = HEADS // KVH
MAXCTX = 64
PAGE = 16
EPSILON = 1e-06
BLOCK = 512
ROWS = 32
TOGETHER = 4
CONTRACT_LAST = (((1,), (1,)), ((), ()))
VMEM = pl.BlockSpec(memory_space=pltpu.VMEM)
SMEM = pl.BlockSpec(memory_space=pltpu.SMEM)
HBM = pl.BlockSpec(memory_space=pltpu.HBM)


def attention_kernel(
    tables_far,
    lengths_far,
    q_far,
    own_key_far,
    own_value_far,
    keys_far,
    values_far,
    out_far,
    tables,
    lengths,
    q_near,
    own_key,
    own_value,
    keys,
    values,
    q_turned,
    out_turned,
    scores_held,
    own_held,
    weights_held,
    own_weights_held,
    out_near,
    sems,
    out_sems,
):
    rows = q_near.shape[0]
    pages = MAXCTX // PAGE
    tall, wide = TOGETHER * GROUP, TOGETHER * MAXCTX
    big = tall * KVH
    scale = 1.0 / math.sqrt(HD)
    inward = [
        pltpu.make_async_copy(far, near, sems.at[i])
        for i, (far, near) in enumerate(
            (
                (q_far, q_near),
                (own_key_far, own_key),
                (keys_far, keys),
                (values_far, values),
                (own_value_far, own_value),
                (tables_far, tables),
                (lengths_far, lengths),
            )
        )
    ]
    for copy in inward:
        copy.start()
    inward[0].wait()
    for head in range(HEADS):
        q_turned[head // GROUP, pl.ds(head % GROUP * rows, rows), :] = q_near[
            :, head * HD : (head + 1) * HD
        ].astype(jnp.float32)
    inward[1].wait()
    inward[2].wait()
    inward[5].wait()
    inward[6].wait()
    for first in range(0, rows, TOGETHER):
        page_ids = [tables[j, first + i] for i in range(TOGETHER) for j in range(pages)]
        for kv in range(KVH):
            lanes = slice(kv * HD, (kv + 1) * HD)
            q = jnp.concatenate(
                [
                    q_turned[kv, pl.ds(first + i, GROUP, stride=rows), :]
                    for i in range(TOGETHER)
                ],
                axis=0,
            ).astype(jnp.bfloat16)
            k = jnp.concatenate([keys[page, :, lanes] for page in page_ids], axis=0)
            at = pl.ds(first // TOGETHER * big + kv * tall, tall)
            scores_held[at, :] = (
                lax.dot_general(q, k, CONTRACT_LAST, preferred_element_type=jnp.float32) * scale
            )
            own_held[at, :] = (
                lax.dot_general(
                    q, own_key[:, lanes], CONTRACT_LAST, preferred_element_type=jnp.float32
                )
                * scale
            )
    row_request = lax.broadcasted_iota(jnp.int32, (big, wide), 0) // GROUP % TOGETHER
    place = lax.broadcasted_iota(jnp.int32, (big, wide), 1) - row_request * MAXCTX
    own_request = lax.broadcasted_iota(jnp.int32, (big, rows), 0) // GROUP % TOGETHER
    own_column = lax.broadcasted_iota(jnp.int32, (big, rows), 1)
    for first in range(0, rows, TOGETHER):
        at = pl.ds(first // TOGETHER * big, big)
        limit = jnp.zeros((big, wide), jnp.int32)
        for i in range(TOGETHER):
            limit = jnp.where(row_request == i, lengths[first + i], limit)
        scores = jnp.where((place >= 0) & (place < limit), scores_held[at, :], -jnp.inf)
        own_score = jnp.where(own_column == own_request + first, own_held[at, :], -jnp.inf)
        top = jnp.maximum(
            jnp.max(scores, axis=1, keepdims=True), jnp.max(own_score, axis=1, keepdims=True)
        )
        weights = jnp.exp(scores - top)
        own_weights = jnp.exp(own_score - top)
        share = 1.0 / (
            jnp.sum(weights, axis=1, keepdims=True) + jnp.sum(own_weights, axis=1, keepdims=True)
        )
        weights_held[at, :] = (weights * share).astype(jnp.bfloat16)
        own_weights_held[at, :] = (own_weights * share).astype(jnp.bfloat16)
    inward[3].wait()
    inward[4].wait()
    outward = []
    held = out_near.shape[2] // HD
    span = GROUP // held
    for kv in range(KVH):
        lanes = slice(kv * HD, (kv + 1) * HD)
        for first in range(0, rows, TOGETHER):
            page_ids = [tables[j, first + i] for i in range(TOGETHER) for j in range(pages)]
            at = pl.ds(first // TOGETHER * big + kv * tall, tall)
            v = jnp.concatenate([values[page, :, lanes] for page in page_ids], axis=0)
            blended = jnp.dot(
                weights_held[at, :], v, preferred_element_type=jnp.float32
            ) + jnp.dot(
                own_weights_held[at, :], own_value[:, lanes], preferred_element_type=jnp.float32
            )
            for i in range(TOGETHER):
                out_turned[kv, pl.ds(first + i, GROUP, stride=rows), :] = blended[
                    i * GROUP : (i + 1) * GROUP
                ]
        for head in range(kv * GROUP, (kv + 1) * GROUP):
            out_near[head // held, :, head % held * HD : (head % held + 1) * HD] = out_turned[
                kv, pl.ds(head % GROUP * rows, rows), :
            ].astype(jnp.bfloat16)
        part = pl.ds(kv * span, span)
        copy = pltpu.make_async_copy(out_near.at[part], out_far.at[part], out_sems.at[kv])
        copy.start()
        outward.append(copy)
    for copy in outward:
        copy.wait()


def attend(queries, new_keys, new_values, key_pool, value_pool, tables, lengths, chips):
    rows = queries.shape[0]
    total = HEADS * rows
    shape = (chips, rows, HEADS * HD // chips)
    wide = TOGETHER * MAXCTX
    bf16, f32 = jnp.bfloat16, jnp.float32
    return pl.pallas_call(
        attention_kernel,
        out_shape=pltpu.HBM(shape, bf16),
        in_specs=[HBM] * 7,
        out_specs=HBM,
        scratch_shapes=[
            pltpu.SMEM(tables.shape[::-1], jnp.int32),
            pltpu.SMEM(lengths.shape, jnp.int32),
            pltpu.VMEM(queries.shape, bf16),
            pltpu.VMEM(new_keys.shape, bf16),
            pltpu.VMEM(new_values.shape, bf16),
            pltpu.VMEM(key_pool.shape, bf16),
            pltpu.VMEM(value_pool.shape, bf16),
            pltpu.VMEM((KVH, GROUP * rows, HD), f32),
            pltpu.VMEM((KVH, GROUP * rows, HD), f32),
            pltpu.VMEM((total, wide), f32),
            pltpu.VMEM((total, rows), f32),
            pltpu.VMEM((total, wide), bf16),
            pltpu.VMEM((total, rows), bf16),
            pltpu.VMEM(shape, bf16),
            pltpu.SemaphoreType.DMA((7,)),
            pltpu.SemaphoreType.DMA((KVH,)),
        ],
        compiler_params=pltpu.CompilerParams(vmem_limit_bytes=12 << 20),
        cost_estimate=pl.CostEstimate(
            flops=600_000_000, bytes_accessed=5_000_000, transcendentals=300_000
        ),
        name="attention",
    )(
        *(
            pltpu.with_memory_space_constraint(array, pltpu.HBM)
            for array in (
                tables.T,
                lengths,
                queries,
                new_keys,
                new_values,
                key_pool,
                value_pool,
            )
        )
    )


def projection_kernel(orders, spot, x_ref, mine_far, beside_far, *refs):
    parts = len(orders)
    outs, weights, sems = refs[:parts], refs[parts], refs[parts + 1]
    chip, core = spot[0], spot[1]
    depth = mine_far.shape[0]
    _, rows, columns = outs[0].shape
    copies = []
    for i in range(parts):
        lanes = pl.ds(i * columns, columns)
        for j, (far, half) in enumerate(((mine_far, core), (beside_far, 1 - core))):
            at = pl.ds(pl.multiple_of(half * depth, depth), depth)
            copies.append(
                pltpu.make_async_copy(far.at[:, lanes], weights.at[i, at, :], sems.at[i, j])
            )
    ahead = 4
    for copy in copies[:ahead]:
        copy.start()
    for i, masks in enumerate(orders):
        x = jnp.concatenate([x_ref[chip ^ mask] for mask in masks], axis=0)
        copies[2 * i].wait()
        copies[2 * i + 1].wait()
        for copy in copies[2 * i + ahead : 2 * i + ahead + 2]:
            copy.start()
        outs[i][...] = (
            jnp.dot(x, weights[i], preferred_element_type=jnp.float32)
            .astype(jnp.bfloat16)
            .reshape(outs[i].shape)
        )


def project(regrouped, mine, beside, spot, orders, name):
    _, rows, depth = regrouped.shape
    parts = len(orders)
    columns = mine.shape[1] // parts
    return pl.pallas_call(
        functools.partial(projection_kernel, orders),
        out_shape=[
            jax.ShapeDtypeStruct((len(masks), rows, columns), jnp.bfloat16) for masks in orders
        ],
        in_specs=[SMEM, VMEM, HBM, HBM],
        out_specs=[VMEM] * parts,
        scratch_shapes=[
            pltpu.VMEM((parts, depth, columns), jnp.bfloat16),
            pltpu.SemaphoreType.DMA((parts, 2)),
        ],
        compiler_params=pltpu.CompilerParams(vmem_limit_bytes=12 << 20),
        cost_estimate=pl.CostEstimate(
            flops=540_000_000, bytes_accessed=5_500_000, transcendentals=0
        ),
        name=name,
    )(
        spot,
        regrouped,
        pltpu.with_memory_space_constraint(mine, pltpu.HBM),
        pltpu.with_memory_space_constraint(beside, pltpu.HBM),
    )


def dispatch_kernel(
    keep_a,
    got_a,
    keep_b,
    got_b,
    residual,
    gain,
    placing,
    hidden_far,
    normed_far,
    sent_ref,
    hidden_ref,
    normed_ref,
    sems,
):
    rows = residual.shape[0]
    halves = []
    at = 0
    for keep, got in ((keep_a, got_a), (keep_b, got_b)):
        span = keep.shape[1]
        halves.append(
            residual[:, at : at + span].astype(jnp.float32)
            + (keep[...].astype(jnp.float32) + got[...].astype(jnp.float32))
        )
        at += span
    hidden = jnp.concatenate(halves, axis=1)
    hidden_ref[...] = hidden
    mean_square = jnp.mean(hidden * hidden, axis=1, keepdims=True)
    normed = (hidden * lax.rsqrt(mean_square + EPSILON) * gain[...]).astype(jnp.bfloat16)
    normed_ref[...] = normed
    copies = [
        pltpu.make_async_copy(hidden_ref, hidden_far, sems.at[0]),
        pltpu.make_async_copy(normed_ref, normed_far, sems.at[1]),
    ]
    for copy in copies:
        copy.start()
    blocks = at // BLOCK
    stacked = jnp.concatenate(
        [normed[:, i * BLOCK : (i + 1) * BLOCK] for i in range(blocks)], axis=0
    )
    step = 512
    for i in range(0, placing.shape[0], step):
        part = pl.ds(i, step)
        sent_ref[part, :] = jnp.dot(
            placing[part, :], stacked, preferred_element_type=jnp.float32
        ).astype(jnp.bfloat16)
    for copy in copies:
        copy.wait()


def dispatch(keep_a, got_a, keep_b, got_b, residual, gain, placing):
    rows, width = residual.shape
    return pl.pallas_call(
        dispatch_kernel,
        out_shape=[
            pltpu.HBM((rows, width), jnp.float32),
            pltpu.HBM((rows, width), jnp.bfloat16),
            jax.ShapeDtypeStruct((placing.shape[0], BLOCK), jnp.bfloat16),
        ],
        in_specs=[VMEM] * 7,
        out_specs=[HBM, HBM, VMEM],
        scratch_shapes=[
            pltpu.VMEM((rows, width), jnp.float32),
            pltpu.VMEM((rows, width), jnp.bfloat16),
            pltpu.SemaphoreType.DMA((2,)),
        ],
        compiler_params=pltpu.CompilerParams(vmem_limit_bytes=8 << 20),
        cost_estimate=pl.CostEstimate(
            flops=270_000_000, bytes_accessed=4_000_000, transcendentals=16
        ),
        name="dispatch",
    )(keep_a, got_a, keep_b, got_b, residual, gain, placing)


def turning(blocks, capacity, sources, back):
    lines = blocks * capacity * sources
    left = lax.broadcasted_iota(jnp.int32, (lines, lines), 0)
    right = lax.broadcasted_iota(jnp.int32, (lines, lines), 1)
    if back:
        left, right = right, left
    wanted = left % sources * (blocks * capacity) + left // sources
    return (wanted == right).astype(jnp.float32).astype(jnp.bfloat16)


def rows_kernel(arrived, out_ref):
    groups = out_ref.shape[0] // ROWS
    sources = arrived.shape[0] // groups
    blocks = out_ref.shape[1] // BLOCK
    lines = arrived.shape[1] * sources
    turn = turning(blocks, arrived.shape[1] // blocks, sources, False)
    for g in range(groups):
        turned = jnp.dot(
            turn,
            arrived[g * sources : (g + 1) * sources].reshape(lines, BLOCK),
            preferred_element_type=jnp.float32,
        ).astype(jnp.bfloat16)
        for i in range(blocks):
            out_ref[g * ROWS : (g + 1) * ROWS, i * BLOCK : (i + 1) * BLOCK] = turned[
                i * ROWS : (i + 1) * ROWS
            ]


def lines_kernel(rows_ref, out_far, out_near, sems):
    groups = rows_ref.shape[0] // ROWS
    blocks = rows_ref.shape[1] // BLOCK
    sources = out_near.shape[0] // groups
    turn = turning(blocks, out_near.shape[1] // blocks, sources, True)
    outward = []
    for g in range(groups):
        part = pl.ds(g * sources, sources)
        stacked = jnp.concatenate(
            [
                rows_ref[g * ROWS : (g + 1) * ROWS, i * BLOCK : (i + 1) * BLOCK]
                for i in range(blocks)
            ],
            axis=0,
        )
        out_near[part] = (
            jnp.dot(turn, stacked, preferred_element_type=jnp.float32)
            .astype(jnp.bfloat16)
            .reshape(sources, out_near.shape[1], BLOCK)
        )
        copy = pltpu.make_async_copy(out_near.at[part], out_far.at[part], sems.at[g])
        copy.start()
        outward.append(copy)
    for copy in outward:
        copy.wait()


def run_expert(arrived, gate, up, down):
    experts, lines, _ = arrived.shape
    width = gate.shape[0]
    token_rows = experts * lines // (width // BLOCK)
    groups = token_rows // ROWS
    params = pltpu.CompilerParams(vmem_limit_bytes=12 << 20)
    cost = pl.CostEstimate(flops=540_000_000, bytes_accessed=4_200_000, transcendentals=0)
    rows = pl.pallas_call(
        rows_kernel,
        out_shape=jax.ShapeDtypeStruct((token_rows, width), jnp.bfloat16),
        in_specs=[VMEM],
        out_specs=VMEM,
        compiler_params=params,
        cost_estimate=cost,
        name="slots_to_rows",
    )(arrived)
    gate_part = jnp.dot(rows, gate, preferred_element_type=jnp.float32)
    gate_part, up = lax.optimization_barrier((gate_part, up))
    up_part = jnp.dot(rows, up, preferred_element_type=jnp.float32)
    expert_hidden, down = lax.optimization_barrier(
        ((jax.nn.silu(gate_part) * up_part).astype(jnp.bfloat16), down)
    )
    output = jnp.dot(expert_hidden, down, preferred_element_type=jnp.float32).astype(jnp.bfloat16)
    return pl.pallas_call(
        lines_kernel,
        out_shape=pltpu.HBM(arrived.shape, jnp.bfloat16),
        in_specs=[VMEM],
        out_specs=HBM,
        scratch_shapes=[
            pltpu.VMEM(arrived.shape, jnp.bfloat16),
            pltpu.SemaphoreType.DMA((groups,)),
        ],
        compiler_params=params,
        cost_estimate=cost,
        name="rows_to_slots",
    )(output)


def mixing_kernel(target, gate_of, high_far, low_far, high_ref, low_ref, sems):
    tall, wide = high_ref.shape
    step = 256
    for at in range(0, wide, step):
        line = lax.broadcasted_iota(jnp.int32, (tall, step), 1) + at
        mixing = jnp.zeros((tall, step), jnp.float32)
        for k in range(target.shape[1]):
            mixing = jnp.where(line == target[:, k : k + 1], gate_of[:, k : k + 1], mixing)
        high = mixing.astype(jnp.bfloat16)
        high_ref[:, at : at + step] = high
        low_ref[:, at : at + step] = (mixing - high.astype(jnp.float32)).astype(jnp.bfloat16)
    copies = [
        pltpu.make_async_copy(high_ref, high_far, sems.at[0]),
        pltpu.make_async_copy(low_ref, low_far, sems.at[1]),
    ]
    for copy in copies:
        copy.start()
    for copy in copies:
        copy.wait()


def mix(target, gate_of, lines):
    shape = (target.shape[0], lines)
    return pl.pallas_call(
        mixing_kernel,
        out_shape=[pltpu.HBM(shape, jnp.bfloat16)] * 2,
        in_specs=[VMEM, VMEM],
        out_specs=[HBM, HBM],
        scratch_shapes=[
            pltpu.VMEM(shape, jnp.bfloat16),
            pltpu.VMEM(shape, jnp.bfloat16),
            pltpu.SemaphoreType.DMA((2,)),
        ],
        compiler_params=pltpu.CompilerParams(vmem_limit_bytes=8 << 20),
        cost_estimate=pl.CostEstimate(flops=6_000_000, bytes_accessed=1_200_000, transcendentals=0),
        name="mixing",
    )(target, gate_of)


def combine_kernel(high_far, low_far, returned, hidden_far, out_ref, mixing, hidden, sems):
    rows = hidden.shape[0]
    half = high_far.shape[0]
    copies = [
        pltpu.make_async_copy(high_far, mixing.at[pl.ds(0, half)], sems.at[0]),
        pltpu.make_async_copy(low_far, mixing.at[pl.ds(half, half)], sems.at[1]),
        pltpu.make_async_copy(hidden_far, hidden, sems.at[2]),
    ]
    for copy in copies:
        copy.start()
    for copy in copies:
        copy.wait()
    mixed = jnp.dot(mixing[...], returned[...], preferred_element_type=jnp.float32)
    mixed = mixed[:half] + mixed[half:]
    for i in range(half // rows):
        lanes = slice(i * BLOCK, (i + 1) * BLOCK)
        out_ref[:, lanes] = (hidden[:, lanes] + mixed[i * rows : (i + 1) * rows]).astype(
            jnp.bfloat16
        )


def combine(high, low, returned, hidden):
    far = [pltpu.with_memory_space_constraint(array, pltpu.HBM) for array in (high, low, hidden)]
    return pl.pallas_call(
        combine_kernel,
        out_shape=jax.ShapeDtypeStruct(hidden.shape, jnp.bfloat16),
        in_specs=[HBM, HBM, VMEM, HBM],
        out_specs=VMEM,
        scratch_shapes=[
            pltpu.VMEM((2 * high.shape[0], high.shape[1]), jnp.bfloat16),
            pltpu.VMEM(hidden.shape, jnp.float32),
            pltpu.SemaphoreType.DMA((3,)),
        ],
        compiler_params=pltpu.CompilerParams(vmem_limit_bytes=8 << 20),
        cost_estimate=pl.CostEstimate(
            flops=540_000_000, bytes_accessed=3_500_000, transcendentals=0
        ),
        name="combine",
    )(far[0], far[1], returned, far[2])


def route_gates(logits, routes):
    matches = routes[:, :, None] == jnp.arange(logits.shape[1], dtype=jnp.int32)[None, None, :]
    chosen = jnp.sum(jnp.where(matches, logits[:, None, :], 0.0), axis=-1)
    raised = jnp.exp(chosen)
    return raised / jnp.sum(raised, axis=1, keepdims=True)


def rank_of(flat_routes, experts):
    onehot = (flat_routes[:, None] == jnp.arange(experts, dtype=jnp.int32)[None, :]).astype(
        jnp.int32
    )
    earlier = jnp.cumsum(onehot, axis=0) - onehot
    return jnp.sum(earlier * onehot, axis=1)


def add(left, right):
    return (left.astype(jnp.float32) + right.astype(jnp.float32)).astype(jnp.bfloat16)


def scatter_sum(regrouped, mine, beside, spot, peers):
    jump = {"y": 1, "Y": 3, "z": 4, "Z": 12}

    def swap(array, way):
        return lax.ppermute(array, "dev", [(i, i ^ (2 * jump[way])) for i in range(peers)])

    orders = ("yYzZ", "YyzZ", "zZyY", "ZzyY")
    masks = []
    for order in orders:
        places = []
        for place in range(16):
            mask = 0
            for bit, way in enumerate(order):
                if place >> (3 - bit) & 1:
                    mask ^= jump[way]
            places.append(mask)
        masks.append(tuple(places))
    sent = project(regrouped, mine, beside, spot, [places[8:] for places in masks], "project_sent")
    got = [swap(array, order[0]) for array, order in zip(sent, orders)]
    regrouped, _ = lax.optimization_barrier((regrouped, sent[0]))
    kept = list(
        project(regrouped, mine, beside, spot, [places[:8] for places in masks], "project_kept")
    )
    for part, order in enumerate(orders):
        both = add(kept[part], got[part])
        half = both.shape[0] // 2
        kept[part], got[part] = both[:half], swap(both[half:], order[1])
    merged = []
    for pair in (0, 2):
        way, last = orders[pair][2:]
        both = jnp.concatenate(
            [add(kept[pair], got[pair]), add(kept[pair + 1], got[pair + 1])], axis=2
        )
        merged.append((both[:2], swap(both[2:], way), last))
    ends = []
    for keep, arrived, last in merged:
        both = add(keep, arrived)
        ends += [both[0], swap(both[1], last)]
    return ends


def shards(
    queries,
    new_keys,
    new_values,
    key_pages,
    value_pages,
    block_tables,
    context_lengths,
    out_weight,
    residual,
    norm_gain,
    router_weight,
    routes,
    expert_gate,
    expert_up,
    expert_down,
):
    rows, width = residual.shape
    peers = lax.axis_size("dev")
    chips = peers // 2
    place = lax.axis_index("dev")
    same_core = [[2 * chip + side for chip in range(chips)] for side in range(2)]
    experts = router_weight.shape[1]
    capacity = 2
    blocks = width // BLOCK
    lines = blocks * capacity

    weight_beside = lax.ppermute(out_weight, "dev", [(i, i ^ 1) for i in range(peers)])
    attended = attend(
        queries,
        new_keys,
        new_values,
        key_pages,
        value_pages,
        block_tables,
        context_lengths,
        chips,
    )
    regrouped = lax.all_to_all(
        attended, "dev", split_axis=0, concat_axis=0, axis_index_groups=same_core, tiled=True
    )
    spot = jnp.stack([place // 2, place % 2])
    ends = scatter_sum(regrouped, out_weight, weight_beside, spot, peers)

    rank = rank_of(routes.reshape(-1), experts).reshape(rows, -1)
    block_ids = jnp.arange(blocks, dtype=jnp.int32)
    target = (routes * lines + rank)[None] + (block_ids * capacity)[:, None, None]
    target = target.reshape(blocks * rows, -1)
    line = jnp.arange(experts * lines, dtype=jnp.int32)
    placed = line[:, None] == target[:, 0][None, :]
    for k in range(1, target.shape[1]):
        placed = placed | (line[:, None] == target[:, k][None, :])
    placing = placed.astype(jnp.bfloat16)

    hidden_state, normed, sent = dispatch(*ends, residual, norm_gain[None], placing)
    arrived = lax.all_to_all(
        sent.reshape(experts, lines, BLOCK),
        ("attn", "dev"),
        split_axis=0,
        concat_axis=0,
        tiled=True,
    )
    output_rows = run_expert(arrived, expert_gate[0], expert_up[0], expert_down[0])
    returned = lax.all_to_all(
        output_rows, ("attn", "dev"), split_axis=0, concat_axis=0, tiled=True
    ).reshape(experts * lines, BLOCK)

    logits = jnp.dot(normed, router_weight, preferred_element_type=jnp.float32)
    gate_values = route_gates(logits, routes)
    gate_of = jnp.tile(gate_values, (blocks, 1))
    high, low = mix(target, gate_of, experts * lines)
    return combine(high, low, returned, hidden_state)


def solution(mesh):
    in_specs = (
        P(("attn", "dev"), None),
        P(("attn", "dev"), None),
        P(("attn", "dev"), None),
        P(("attn", "dev"), None, None),
        P(("attn", "dev"), None, None),
        P(("attn", "dev"), None),
        P(("attn", "dev")),
        P("dev", None),
        P(("attn", "dev"), None),
        P(),
        P(),
        P(("attn", "dev"), None),
        P(("attn", "dev"), None, None),
        P(("attn", "dev"), None, None),
        P(("attn", "dev"), None, None),
    )
    out_specs = P(("attn", "dev"), None)
    return jax.shard_map(shards, mesh=mesh, in_specs=in_specs, out_specs=out_specs, check_vma=False)
```

time: 162 us -> 140 us (0.86)
  Pallas kernels: 31.1 us -> 20.6 us
  local copies, waits for them, and re-layouts: 10.4 us -> 2.55 us
  matrix products: 0.24 us -> 5.74 us
  other arithmetic: 6.96 us -> 2.41 us
  blocking collectives: 46.7 us -> 42.7 us
  waiting for transfers between devices: 40.6 us -> 38.9 us
    pallas_call x7, Pallas kernels: 29.8 us -> 18 us  [the longest x2 7.48 us: project(): pl.pallas_call(functools.partial(projection_kernel, orders), out_shape=[j...]
    unnamed x46 -> x23, local copies, waits for them, and re-layouts: 9.66 us -> 1.78 us
    dot_general x0 -> x3, matrix products: none -> 5.49 us  [the longest x1 1.86 us: run_expert(): up_part = jnp.dot(rows, up, preferred_element_type=jnp.float32)]
    all_to_all x1, blocking collectives: 46.7 us -> 42.7 us  [shards(): lax.all_to_all(sent.reshape(experts, lines, BLOCK), ('attn', 'dev'), spli...]
    convert_element_type x1 -> x0, other arithmetic: 3.53 us -> none  [shards(): low = (mixing - high.astype(jnp.float32)).astype(jnp.bfloat16)]
    ppermute x12, waiting for transfers between devices: 8.27 us -> 5.09 us  [swap(): lax.ppermute(array, 'dev', [(i, i ^ 2 * jump[way]) for i in range(peers)])]
  transfers between devices with their start and end apart: 15 -> 15, of which waited for: 11 -> 8; matrix products, arithmetic and copies ran while one was open for 5% -> 2% of each run, Pallas kernels for 7% -> 8%
where the time goes in v3:
time: 140 us
  blocking collectives  42.7 us (30%)
  waiting for transfers between devices  38.9 us (28%)
  starting transfers between devices  26.3 us (19%)
  Pallas kernels  20.6 us (15%)
  matrix products  5.74 us (4%)
  local copies, waits for them, and re-layouts  2.55 us (2%)
  other arithmetic  2.41 us (2%)
    all_to_all x1, blocking collectives, shards(): lax.all_to_all(sent.reshape(experts, lines, BLOCK), ('attn', 'dev'), spli...  42.7 us
    all_to_all x1, waiting for transfers between devices, shards(): lax.all_to_all(output_rows, ('attn', 'dev'), split_axis=0, concat_axis=0,...  26.2 us
    ppermute x12, starting transfers between devices, swap(): lax.ppermute(array, 'dev', [(i, i ^ 2 * jump[way]) for i in range(peers)])  12.3 us
    all_to_all x1, starting transfers between devices, shards(): lax.all_to_all(attended, 'dev', split_axis=0, concat_axis=0, axis_index_g...  7.88 us
    all_to_all x1, waiting for transfers between devices, shards(): lax.all_to_all(attended, 'dev', split_axis=0, concat_axis=0, axis_index_g...  7.63 us
    pallas_call x2, Pallas kernels, project(): pl.pallas_call(functools.partial(projection_kernel, orders), out_shape=[j...  7.48 us
    ppermute x12, waiting for transfers between devices, swap(): lax.ppermute(array, 'dev', [(i, i ^ 2 * jump[way]) for i in range(peers)])  5.09 us
    all_to_all x1, starting transfers between devices, shards(): lax.all_to_all(output_rows, ('attn', 'dev'), split_axis=0, concat_axis=0,...  4.7 us
  transfers between devices with their start and end apart: 15, of which 8 were waited for; matrix products, arithmetic and copies ran while one was open for 2% of the time, Pallas kernels for 8%

profile of v3, /device:TPU:1, one launch (start us, length us, event | category | flops | bytes accessed | tf_op | source)
XLA Modules:
  0.0 139.9 jit_solution(13322124196078476760)
XLA Ops:
  0.0 1.4 %collective-permute-start = (bf16[256,4096]{1,0:T(8,128)(2,1)}, bf16[256,4096]{1,0:T(8,128)(2,1)}, u32[]{:S(2)}, u32[]{:S(2)}) collective-permute-start(bf16[256,4096]{1,0:T(8,128)(2,1)} %mine_far.3), channel_id=1, source_target_pairs={{0,1},{1,0},{2,3},{3,2},{4,5},{5,4},{6,7},{7,6},{8,9},{9,8},{10,11... | collective-permute-start | bytes 6291464 | tf_op jit(solution)/shard_map/ppermute | solution.py:600
  1.4 3.6 %attention.1 = bf16[16,16,512]{2,1,0:T(8,128)(2,1)} custom-call(s32[4,16]{1,0:T(4,128)} %bitcast.33, s32[16]{0:T(128)} %lengths_far.1, bf16[16,8192]{1,0:T(8,128)(2,1)} %q_far.1, bf16[16,512]{1,0:T(8,128)(2,1)} %own_key_far.1, bf16[16,512]{1,0:T(8,128)(2,1)} %own_value_far.1, bf16[64,16,512]{2,1,0:T(8,128)(2,1)} %keys_far.1, bf16[64,16,512]{2,1,0:T(8,128)(2,1)} %values_far.1), custom_call_target="tpu_custom_call" | custom-call | flops 600000000 | bytes 5000000 | tf_op jit(solution)/shard_map/attention/pallas_call | solution.py:164
  5.0 7.9 %all-to-all-start = ((bf16[16,16,512]{2,1,0:T(8,128)(2,1)}), bf16[16,16,512]{2,1,0:T(8,128)(2,1)S(1)}, u32[]{:S(2)}, u32[]{:S(2)}) async-start(bf16[16,16,512]{2,1,0:T(8,128)(2,1)} %attention.1), calls=%async_computation | async-start | bytes 524288 | tf_op jit(solution)/shard_map/all_to_all | solution.py:611
  13.7 7.6 %all-to-all-done.x_ref = bf16[16,16,512]{2,1,0:T(8,128)(2,1)S(1)} async-done(((bf16[16,16,512]{2,1,0:T(8,128)(2,1)}), bf16[16,16,512]{2,1,0:T(8,128)(2,1)S(1)}, u32[]{:S(2)}, u32[]{:S(2)}) %all-to-all-start) | async-done | bytes 262176 | tf_op jit(solution)/shard_map/all_to_all | solution.py:611
  21.4 3.7 %project_sent.1 = (bf16[8,16,1024]{2,1,0:T(8,128)(2,1)S(1)}, bf16[8,16,1024]{2,1,0:T(8,128)(2,1)S(1)}, bf16[8,16,1024]{2,1,0:T(8,128)(2,1)S(1)}, bf16[8,16,1024]{2,1,0:T(8,128)(2,1)S(1)}) custom-call(s32[2]{0:T(128)S(1)} %pad_add_fusion.spot, bf16[16,16,512]{2,1,0:T(8,128)(2,1)S(1)} %all-to-all-done.x_ref, bf16[256,4096]{1,0:T(8,128)(2,1)} %mine_far.3, ...), custom_call_target="tpu_custom_call" | custom-call | flops 540000000 | bytes 5500000 | tf_op jit(solution)/shard_map/project_sent/pallas_call | solution.py:242
  25.9 1.1 collective-permute-start.9
  27.0 1.2 collective-permute-start.3
  28.2 3.7 %project_kept.1 = (bf16[8,16,1024]{2,1,0:T(8,128)(2,1)S(1)}, bf16[8,16,1024]{2,1,0:T(8,128)(2,1)S(1)}, bf16[8,16,1024]{2,1,0:T(8,128)(2,1)S(1)}, bf16[8,16,1024]{2,1,0:T(8,128)(2,1)S(1)}) custom-call(s32[2]{0:T(128)S(1)} %pad_add_fusion.spot, bf16[16,16,512]{2,1,0:T(8,128)(2,1)S(1)} %all-to-all-done.x_ref, bf16[256,4096]{1,0:T(8,128)(2,1)} %mine_far.3, ...), custom_call_target="tpu_custom_call" | custom-call | flops 540000000 | bytes 5500000 | tf_op jit(solution)/shard_map/project_kept/pallas_call | solution.py:242
  32.0 1.5 %collective-permute-start.8 = (bf16[4,16,1024]{2,1,0:T(8,128)(2,1)S(1)}, bf16[4,16,1024]{2,1,0:T(8,128)(2,1)S(1)}, u32[]{:S(2)}, u32[]{:S(2)}) collective-permute-start(bf16[4,16,1024]{2,1,0:T(8,128)(2,1)S(1)} %slice.105), channel_id=1, source_target_pairs={{0,24},{1,25},{2,26},{3,27},{4,28},{5,29},{6,30},{7,31},{8,16},{9,... | collective-permute-start | bytes 393224 | tf_op jit(solution)/shard_map/ppermute | solution.py:536
  33.8 2.0 %collective-permute-start.2 = (bf16[4,16,1024]{2,1,0:T(8,128)(2,1)S(1)}, bf16[4,16,1024]{2,1,0:T(8,128)(2,1)S(1)}, u32[]{:S(2)}, u32[]{:S(2)}) collective-permute-start(bf16[4,16,1024]{2,1,0:T(8,128)(2,1)S(1)} %slice.97), channel_id=1, source_target_pairs={{0,6},{1,7},{2,4},{3,5},{4,2},{5,3},{6,0},{7,1},{8,14},{9,15},{10,... | collective-permute-start | bytes 393224 | tf_op jit(solution)/shard_map/ppermute | solution.py:536
  36.2 1.0 collective-permute-done.8
  37.6 1.7 %collective-permute-start.11 = (bf16[2,16,2048]{2,1,0:T(8,128)(2,1)S(1)}, bf16[2,16,2048]{2,1,0:T(8,128)(2,1)S(1)}, u32[]{:S(2)}, u32[]{:S(2)}) collective-permute-start(bf16[2,16,2048]{2,1,0:T(8,128)(2,1)S(1)} %pad_maximum_fusion), channel_id=1, source_target_pairs={{0,2},{1,3},{2,0},{3,1},{4,6},{5,7},{6,4},{7,5},{8,10},{9,11},{10,... | collective-permute-start | bytes 393224 | tf_op jit(solution)/shard_map/ppermute | solution.py:536
  39.4 0.8 collective-permute-done.4
  40.2 1.3 collective-permute-start.5
  41.5 0.5 collective-permute-done.11
  42.0 1.6 %collective-permute-start.12 = (bf16[16,2048]{1,0:T(8,128)(2,1)S(1)}, bf16[16,2048]{1,0:T(8,128)(2,1)S(1)}, u32[]{:S(2)}, u32[]{:S(2)}) collective-permute-start(bf16[16,2048]{1,0:T(8,128)(2,1)S(1)} %get-tuple-element.49), channel_id=1, source_target_pairs={{0,6},{1,7},{2,4},{3,5},{4,2},{5,3},{6,0},{7,1},{8,14},{9,15},{10,... | collective-permute-start | bytes 196616 | tf_op jit(solution)/shard_map/ppermute | solution.py:536
  43.7 0.4 collective-permute-done.5
  44.2 1.3 collective-permute-start.6
  45.5 0.9 fusion.10.placing
  46.5 2.1 %collective-permute-done.6.got_a = bf16[16,2048]{1,0:T(8,128)(2,1)S(1)} collective-permute-done((bf16[16,2048]{1,0:T(8,128)(2,1)S(1)}, bf16[16,2048]{1,0:T(8,128)(2,1)S(1)}, u32[]{:S(2)}, u32[]{:S(2)}) %collective-permute-start.6) | collective-permute-done | bytes 65568 | tf_op jit(solution)/shard_map/ppermute | solution.py:536
  48.6 0.9 dispatch.1
  49.5 42.7 %all_to_all.15.arrived = bf16[128,16,512]{2,1,0:T(8,128)(2,1)S(1)} all-to-all(bf16[128,16,512]{2,1,0:T(8,128)(2,1)S(1)} %bitcast.30), channel_id=1, replica_groups=mesh['attn'=4,'dev'=32] {'attn','dev'}, dimensions={0} | all-to-all | bytes 4194304 | tf_op jit(solution)/shard_map/all_to_all | solution.py:628
  92.2 0.7 slots_to_rows.1
  93.0 1.8 %fusion = f32[256,768]{1,0:T(8,128)S(1)} fusion(bf16[256,4096]{1,0:T(8,128)(2,1)S(1)} %slots_to_rows.1, bf16[1,4096,768]{2,1,0:T(8,128)(2,1)S(1)} %bitcast.35), kind=kOutput, calls=%fused_computation | convolution fusion | flops 1610612736 | bytes 9175040 | tf_op jit(solution)/shard_map/dot_general | solution.py:411
  94.8 1.6 %slice-done.3 = s8[2097152]{0:T(1024)(128)(4,1)S(1)} async-done(((s8[6291456]{0:T(1024)(128)(4,1)}), s8[2097152]{0:T(1024)(128)(4,1)S(1)}, s32[]{:S(2)}) %slice-start.3) | async-done | bytes 2097176
  96.5 1.9 %fusion.2 = bf16[256,768]{1,0:T(8,128)(2,1)S(1)} fusion(bf16[256,4096]{1,0:T(8,128)(2,1)S(1)} %slots_to_rows.1, bf16[4096,768]{1,0:T(8,128)(2,1)S(1)} %bitcast.38, f32[256,768]{1,0:T(8,128)S(1)} %fusion), kind=kOutput, calls=%fused_computation.4 | convolution fusion | flops 1611792384 | bytes 9568256 | tf_op jit(solution)/shard_map/dot_general | solution.py:413
  98.4 1.8 %convolution_convert_fusion.rows_ref = bf16[256,4096]{1,0:T(8,128)(2,1)S(1)} fusion(bf16[256,768]{1,0:T(8,128)(2,1)S(1)} %fusion.2, bf16[768,4096]{1,0:T(8,128)(2,1)S(1)} %bitcast.41), kind=kOutput, calls=%fused_computation.2 | convolution fusion | flops 1611661312 | bytes 8781824 | tf_op jit(solution)/shard_map/dot_general | solution.py:417
  100.2 1.6 %rows_to_slots.1 = bf16[128,16,512]{2,1,0:T(8,128)(2,1)} custom-call(bf16[256,4096]{1,0:T(8,128)(2,1)S(1)} %convolution_convert_fusion.rows_ref), custom_call_target="tpu_custom_call" | custom-call | flops 540000000 | bytes 4200000 | tf_op jit(solution)/shard_map/rows_to_slots/pallas_call | solution.py:418
  101.9 4.7 %all-to-all-start.2 = ((bf16[128,16,512]{2,1,0:T(8,128)(2,1)}), bf16[128,16,512]{2,1,0:T(8,128)(2,1)S(1)}, u32[]{:S(2)}, u32[]{:S(2)}) async-start(bf16[128,16,512]{2,1,0:T(8,128)(2,1)} %rows_to_slots.1), calls=%async_computation.2 | async-start | bytes 4194304 | tf_op jit(solution)/shard_map/all_to_all | solution.py:636
  107.2 3.7 %mixing.1 = (bf16[128,2048]{1,0:T(8,128)(2,1)}, bf16[128,2048]{1,0:T(8,128)(2,1)}) custom-call(s32[128,8]{1,0:T(8,128)S(1)} %broadcast_add_fusion.target, f32[128,8]{1,0:T(8,128)S(1)} %bitcast.31), custom_call_target="tpu_custom_call" | custom-call | flops 6000000 | bytes 1200000 | tf_op jit(solution)/shard_map/mixing/pallas_call | solution.py:456
  110.9 26.2 %all-to-all-done.2 = bf16[128,16,512]{2,1,0:T(8,128)(2,1)S(1)} async-done(((bf16[128,16,512]{2,1,0:T(8,128)(2,1)}), bf16[128,16,512]{2,1,0:T(8,128)(2,1)S(1)}, u32[]{:S(2)}, u32[]{:S(2)}) %all-to-all-start.2) | async-done | bytes 2097184 | tf_op jit(solution)/shard_map/all_to_all | solution.py:636
  137.1 2.7 %combine.1 = bf16[16,4096]{1,0:T(8,128)(2,1)} custom-call(bf16[128,2048]{1,0:T(8,128)(2,1)} %get-tuple-element.33.high_far, bf16[128,2048]{1,0:T(8,128)(2,1)} %get-tuple-element.34.low_far, bf16[2048,512]{1,0:T(8,128)(2,1)S(1)} %bitcast.29, f32[16,4096]{1,0:T(8,128)} %get-tuple-element.40.hidden_far), custom_call_target="tpu_custom_call" | custom-call | flops 540000000 | bytes 3500000 | tf_op jit(solution)/shard_map/combine/pallas_call | solution.py:495
  (72 shorter events, 3.4 us)
Async XLA Ops:
  0.0 106.6 %copy-start = (bf16[4096,128]{1,0:T(8,128)(2,1)S(1)}, bf16[4096,128]{1,0:T(8,128)(2,1)}, u32[]{:S(2)}) copy-start(bf16[4096,128]{1,0:T(8,128)(2,1)} %param.25) | copy-start | bytes 3145732
  0.0 12.9 %copy-start.4 = (s32[16,8]{0,1:T(8,128)S(1)}, s32[16,8]{0,1:T(8,128)}, u32[]{:S(2)}) copy-start(s32[16,8]{0,1:T(8,128)} %param.26) | copy-start | bytes 1540
  0.0 21.4 %collective-permute-start = (bf16[256,4096]{1,0:T(8,128)(2,1)}, bf16[256,4096]{1,0:T(8,128)(2,1)}, u32[]{:S(2)}, u32[]{:S(2)}) collective-permute-start(bf16[256,4096]{1,0:T(8,128)(2,1)} %mine_far.3), channel_id=1, source_target_pairs={{0,1},{1,0},{2,3},{3,2},{4,5},{5,4},{6,7},{7,6},{8,9},{9,8},{10,11... | collective-permute-start | bytes 6291464 | tf_op jit(solution)/shard_map/ppermute | solution.py:600
  5.0 16.3 %all-to-all-start = ((bf16[16,16,512]{2,1,0:T(8,128)(2,1)}), bf16[16,16,512]{2,1,0:T(8,128)(2,1)S(1)}, u32[]{:S(2)}, u32[]{:S(2)}) async-start(bf16[16,16,512]{2,1,0:T(8,128)(2,1)} %attention.1), calls=%async_computation | async-start | bytes 524288 | tf_op jit(solution)/shard_map/all_to_all | solution.py:611
  25.1 6.8 %collective-permute-start.7 = (bf16[8,16,1024]{2,1,0:T(8,128)(2,1)S(1)}, bf16[8,16,1024]{2,1,0:T(8,128)(2,1)S(1)}, u32[]{:S(2)}, u32[]{:S(2)}) collective-permute-start(bf16[8,16,1024]{2,1,0:T(8,128)(2,1)S(1)} %get-tuple-element.29), channel_id=1, source_target_pairs={{0,8},{1,9},{2,10},{3,11},{4,12},{5,13},{6,14},{7,15},{8,0},{9,1},... | collective-permute-start | bytes 786440 | tf_op jit(solution)/shard_map/ppermute | solution.py:536
  25.8 7.9 %collective-permute-start.1 = (bf16[8,16,1024]{2,1,0:T(8,128)(2,1)S(1)}, bf16[8,16,1024]{2,1,0:T(8,128)(2,1)S(1)}, u32[]{:S(2)}, u32[]{:S(2)}) collective-permute-start(bf16[8,16,1024]{2,1,0:T(8,128)(2,1)S(1)} %get-tuple-element.23), channel_id=1, source_target_pairs={{0,2},{1,3},{2,0},{3,1},{4,6},{5,7},{6,4},{7,5},{8,10},{9,11},{10,... | collective-permute-start | bytes 786440 | tf_op jit(solution)/shard_map/ppermute | solution.py:536
  25.9 7.6 %collective-permute-start.9 = (bf16[8,16,1024]{2,1,0:T(8,128)(2,1)S(1)}, bf16[8,16,1024]{2,1,0:T(8,128)(2,1)S(1)}, u32[]{:S(2)}, u32[]{:S(2)}) collective-permute-start(bf16[8,16,1024]{2,1,0:T(8,128)(2,1)S(1)} %get-tuple-element.31), channel_id=1, source_target_pairs={{0,24},{1,25},{2,26},{3,27},{4,28},{5,29},{6,30},{7,31},{8,16},{9,... | collective-permute-start | bytes 786440 | tf_op jit(solution)/shard_map/ppermute | solution.py:536
  27.0 8.8 %collective-permute-start.3 = (bf16[8,16,1024]{2,1,0:T(8,128)(2,1)S(1)}, bf16[8,16,1024]{2,1,0:T(8,128)(2,1)S(1)}, u32[]{:S(2)}, u32[]{:S(2)}) collective-permute-start(bf16[8,16,1024]{2,1,0:T(8,128)(2,1)S(1)} %get-tuple-element.27), channel_id=1, source_target_pairs={{0,6},{1,7},{2,4},{3,5},{4,2},{5,3},{6,0},{7,1},{8,14},{9,15},{10,... | collective-permute-start | bytes 786440 | tf_op jit(solution)/shard_map/ppermute | solution.py:536
  32.0 5.1 %collective-permute-start.8 = (bf16[4,16,1024]{2,1,0:T(8,128)(2,1)S(1)}, bf16[4,16,1024]{2,1,0:T(8,128)(2,1)S(1)}, u32[]{:S(2)}, u32[]{:S(2)}) collective-permute-start(bf16[4,16,1024]{2,1,0:T(8,128)(2,1)S(1)} %slice.105), channel_id=1, source_target_pairs={{0,24},{1,25},{2,26},{3,27},{4,28},{5,29},{6,30},{7,31},{8,16},{9,... | collective-permute-start | bytes 393224 | tf_op jit(solution)/shard_map/ppermute | solution.py:536
  33.6 3.9 %collective-permute-start.10 = (bf16[4,16,1024]{2,1,0:T(8,128)(2,1)S(1)}, bf16[4,16,1024]{2,1,0:T(8,128)(2,1)S(1)}, u32[]{:S(2)}, u32[]{:S(2)}) collective-permute-start(bf16[4,16,1024]{2,1,0:T(8,128)(2,1)S(1)} %slice.107), channel_id=1, source_target_pairs={{0,8},{1,9},{2,10},{3,11},{4,12},{5,13},{6,14},{7,15},{8,0},{9,1},... | collective-permute-start | bytes 393224 | tf_op jit(solution)/shard_map/ppermute | solution.py:536
  33.8 5.5 %collective-permute-start.2 = (bf16[4,16,1024]{2,1,0:T(8,128)(2,1)S(1)}, bf16[4,16,1024]{2,1,0:T(8,128)(2,1)S(1)}, u32[]{:S(2)}, u32[]{:S(2)}) collective-permute-start(bf16[4,16,1024]{2,1,0:T(8,128)(2,1)S(1)} %slice.97), channel_id=1, source_target_pairs={{0,6},{1,7},{2,4},{3,5},{4,2},{5,3},{6,0},{7,1},{8,14},{9,15},{10,... | collective-permute-start | bytes 393224 | tf_op jit(solution)/shard_map/ppermute | solution.py:536
  36.0 4.2 %collective-permute-start.4 = (bf16[4,16,1024]{2,1,0:T(8,128)(2,1)S(1)}, bf16[4,16,1024]{2,1,0:T(8,128)(2,1)S(1)}, u32[]{:S(2)}, u32[]{:S(2)}) collective-permute-start(bf16[4,16,1024]{2,1,0:T(8,128)(2,1)S(1)} %slice.99), channel_id=1, source_target_pairs={{0,2},{1,3},{2,0},{3,1},{4,6},{5,7},{6,4},{7,5},{8,10},{9,11},{10,... | collective-permute-start | bytes 393224 | tf_op jit(solution)/shard_map/ppermute | solution.py:536
  37.2 11.4 %copy-start.1 = (bf16[16,4096]{1,0:T(8,128)(2,1)S(1)}, bf16[16,4096]{1,0:T(8,128)(2,1)}, u32[]{:S(2)}) copy-start(bf16[16,4096]{1,0:T(8,128)(2,1)} %residual.1) | copy-start | bytes 393220
  37.2 11.4 %copy-start.2 = (f32[4096]{0:T(1024)S(1)}, f32[4096]{0:T(1024)}, u32[]{:S(2)}) copy-start(f32[4096]{0:T(1024)} %param.24) | copy-start | bytes 49156
  37.6 4.4 %collective-permute-start.11 = (bf16[2,16,2048]{2,1,0:T(8,128)(2,1)S(1)}, bf16[2,16,2048]{2,1,0:T(8,128)(2,1)S(1)}, u32[]{:S(2)}, u32[]{:S(2)}) collective-permute-start(bf16[2,16,2048]{2,1,0:T(8,128)(2,1)S(1)} %pad_maximum_fusion), channel_id=1, source_target_pairs={{0,2},{1,3},{2,0},{3,1},{4,6},{5,7},{6,4},{7,5},{8,10},{9,11},{10,... | collective-permute-start | bytes 393224 | tf_op jit(solution)/shard_map/ppermute | solution.py:536
  40.2 3.9 %collective-permute-start.5 = (bf16[2,16,2048]{2,1,0:T(8,128)(2,1)S(1)}, bf16[2,16,2048]{2,1,0:T(8,128)(2,1)S(1)}, u32[]{:S(2)}, u32[]{:S(2)}) collective-permute-start(bf16[2,16,2048]{2,1,0:T(8,128)(2,1)S(1)} %pad_maximum_fusion.1), channel_id=1, source_target_pairs={{0,8},{1,9},{2,10},{3,11},{4,12},{5,13},{6,14},{7,15},{8,0},{9,1},... | collective-permute-start | bytes 393224 | tf_op jit(solution)/shard_map/ppermute | solution.py:536
  42.0 51.0 %slice-start = ((s8[6291456]{0:T(1024)(128)(4,1)}), s8[4194304]{0:T(1024)(128)(4,1)S(1)}, s32[]{:S(2)}) async-start(s8[6291456]{0:T(1024)(128)(4,1)} %bitcast.34), calls=%async_computation.3 | async-start | bytes 8388608
  42.0 4.4 %collective-permute-start.12 = (bf16[16,2048]{1,0:T(8,128)(2,1)S(1)}, bf16[16,2048]{1,0:T(8,128)(2,1)S(1)}, u32[]{:S(2)}, u32[]{:S(2)}) collective-permute-start(bf16[16,2048]{1,0:T(8,128)(2,1)S(1)} %get-tuple-element.49), channel_id=1, source_target_pairs={{0,6},{1,7},{2,4},{3,5},{4,2},{5,3},{6,0},{7,1},{8,14},{9,15},{10,... | collective-permute-start | bytes 196616 | tf_op jit(solution)/shard_map/ppermute | solution.py:536
  44.2 4.4 %collective-permute-start.6 = (bf16[16,2048]{1,0:T(8,128)(2,1)S(1)}, bf16[16,2048]{1,0:T(8,128)(2,1)S(1)}, u32[]{:S(2)}, u32[]{:S(2)}) collective-permute-start(bf16[16,2048]{1,0:T(8,128)(2,1)S(1)} %get-tuple-element.51), channel_id=1, source_target_pairs={{0,24},{1,25},{2,26},{3,27},{4,28},{5,29},{6,30},{7,31},{8,16},{9,... | collective-permute-start | bytes 196616 | tf_op jit(solution)/shard_map/ppermute | solution.py:536
  49.5 43.5 %slice-start.1 = ((s8[6291456]{0:T(1024)(128)(4,1)}), s8[2097152]{0:T(1024)(128)(4,1)S(1)}, s32[]{:S(2)}) async-start(s8[6291456]{0:T(1024)(128)(4,1)} %bitcast.34), calls=%async_computation.4 | async-start | bytes 4194304
  92.2 2.6 %slice-start.2 = ((s8[6291456]{0:T(1024)(128)(4,1)}), s8[4194304]{0:T(1024)(128)(4,1)S(1)}, s32[]{:S(2)}) async-start(s8[6291456]{0:T(1024)(128)(4,1)} %bitcast.36), calls=%async_computation.5 | async-start | bytes 8388608
  92.2 6.1 %slice-start.4 = ((s8[6291456]{0:T(1024)(128)(4,1)}), s8[4194304]{0:T(1024)(128)(4,1)S(1)}, s32[]{:S(2)}) async-start(s8[6291456]{0:T(1024)(128)(4,1)} %bitcast.39), calls=%async_computation.7 | async-start | bytes 8388608
  93.0 3.5 %slice-start.3 = ((s8[6291456]{0:T(1024)(128)(4,1)}), s8[2097152]{0:T(1024)(128)(4,1)S(1)}, s32[]{:S(2)}) async-start(s8[6291456]{0:T(1024)(128)(4,1)} %bitcast.36), calls=%async_computation.6 | async-start | bytes 4194304
  93.0 5.4 %slice-start.5 = ((s8[6291456]{0:T(1024)(128)(4,1)}), s8[2097152]{0:T(1024)(128)(4,1)S(1)}, s32[]{:S(2)}) async-start(s8[6291456]{0:T(1024)(128)(4,1)} %bitcast.39), calls=%async_computation.8 | async-start | bytes 4194304
  101.9 4.7 %copy-start.3 = (bf16[16,4096]{1,0:T(8,128)(2,1)S(1)}, bf16[16,4096]{1,0:T(8,128)(2,1)}, u32[]{:S(2)}) copy-start(bf16[16,4096]{1,0:T(8,128)(2,1)} %get-tuple-element.32) | copy-start | bytes 393220
  101.9 35.2 %all-to-all-start.2 = ((bf16[128,16,512]{2,1,0:T(8,128)(2,1)}), bf16[128,16,512]{2,1,0:T(8,128)(2,1)S(1)}, u32[]{:S(2)}, u32[]{:S(2)}) async-start(bf16[128,16,512]{2,1,0:T(8,128)(2,1)} %rows_to_slots.1), calls=%async_computation.2 | async-start | bytes 4194304 | tf_op jit(solution)/shard_map/all_to_all | solution.py:636

commit v4 on v3

--- a/solution.py
+++ b/solution.py
@@ -205,52 +205,44 @@
     )
 
 
-def projection_kernel(orders, spot, x_ref, mine_far, beside_far, *refs):
-    parts = len(orders)
-    outs, weights, sems = refs[:parts], refs[parts], refs[parts + 1]
+def projection_kernel(orders, spot, x_ref, mine, beside, *outs):
     chip, core = spot[0], spot[1]
-    depth = mine_far.shape[0]
-    _, rows, columns = outs[0].shape
-    copies = []
-    for i in range(parts):
-        lanes = pl.ds(i * columns, columns)
-        for j, (far, half) in enumerate(((mine_far, core), (beside_far, 1 - core))):
-            at = pl.ds(pl.multiple_of(half * depth, depth), depth)
-            copies.append(
-                pltpu.make_async_copy(far.at[:, lanes], weights.at[i, at, :], sems.at[i, j])
+    depth = mine.shape[0]
+    columns = outs[0].shape[2]
+    for i, (masks, out) in enumerate(zip(orders, outs)):
+        lanes = slice(i * columns, (i + 1) * columns)
+        x = jnp.concatenate([x_ref[chip ^ mask] for mask in masks], axis=0)
+        low, high = x[:, :depth], x[:, depth:]
+        here = jnp.full(low.shape, core, jnp.int32) == 0
+        out[...] = (
+            (
+                jnp.dot(
+                    jnp.where(here, low, high),
+                    mine[:, lanes],
+                    preferred_element_type=jnp.float32,
+                )
+                + jnp.dot(
+                    jnp.where(here, high, low),
+                    beside[:, lanes],
+                    preferred_element_type=jnp.float32,
+                )
             )
-    ahead = 4
-    for copy in copies[:ahead]:
-        copy.start()
-    for i, masks in enumerate(orders):
-        x = jnp.concatenate([x_ref[chip ^ mask] for mask in masks], axis=0)
-        copies[2 * i].wait()
-        copies[2 * i + 1].wait()
-        for copy in copies[2 * i + ahead : 2 * i + ahead + 2]:
-            copy.start()
-        outs[i][...] = (
-            jnp.dot(x, weights[i], preferred_element_type=jnp.float32)
             .astype(jnp.bfloat16)
-            .reshape(outs[i].shape)
+            .reshape(out.shape)
         )
 
 
 def project(regrouped, mine, beside, spot, orders, name):
-    _, rows, depth = regrouped.shape
-    parts = len(orders)
-    columns = mine.shape[1] // parts
+    _, rows, _ = regrouped.shape
+    columns = mine.shape[1] // len(orders)
     return pl.pallas_call(
         functools.partial(projection_kernel, orders),
         out_shape=[
             jax.ShapeDtypeStruct((len(masks), rows, columns), jnp.bfloat16) for masks in orders
         ],
-        in_specs=[SMEM, VMEM, HBM, HBM],
-        out_specs=[VMEM] * parts,
-        scratch_shapes=[
-            pltpu.VMEM((parts, depth, columns), jnp.bfloat16),
-            pltpu.SemaphoreType.DMA((parts, 2)),
-        ],
-        compiler_params=pltpu.CompilerParams(vmem_limit_bytes=12 << 20),
+        in_specs=[SMEM, VMEM, VMEM, VMEM],
+        out_specs=[VMEM] * len(orders),
+        compiler_params=pltpu.CompilerParams(vmem_limit_bytes=8 << 20),
         cost_estimate=pl.CostEstimate(
             flops=540_000_000, bytes_accessed=5_500_000, transcendentals=0
         ),
@@ -258,8 +250,8 @@
     )(
         spot,
         regrouped,
-        pltpu.with_memory_space_constraint(mine, pltpu.HBM),
-        pltpu.with_memory_space_constraint(beside, pltpu.HBM),
+        pltpu.with_memory_space_constraint(mine, pltpu.VMEM),
+        pltpu.with_memory_space_constraint(beside, pltpu.VMEM),
     )
 
 
@@ -347,12 +339,17 @@
     return (wanted == right).astype(jnp.float32).astype(jnp.bfloat16)
 
 
-def rows_kernel(arrived, out_ref):
-    groups = out_ref.shape[0] // ROWS
+def expert_kernel(
+    arrived, gate, up, down, out_far, rows_in, hidden, rows_out, out_near, sems
+):
+    groups = rows_out.shape[0]
+    width = rows_in.shape[1]
     sources = arrived.shape[0] // groups
-    blocks = out_ref.shape[1] // BLOCK
+    blocks = width // BLOCK
     lines = arrived.shape[1] * sources
-    turn = turning(blocks, arrived.shape[1] // blocks, sources, False)
+    each = lines // blocks
+    capacity = arrived.shape[1] // blocks
+    turn = turning(blocks, capacity, sources, False)
     for g in range(groups):
         turned = jnp.dot(
             turn,
@@ -360,30 +357,30 @@
             preferred_element_type=jnp.float32,
         ).astype(jnp.bfloat16)
         for i in range(blocks):
-            out_ref[g * ROWS : (g + 1) * ROWS, i * BLOCK : (i + 1) * BLOCK] = turned[
-                i * ROWS : (i + 1) * ROWS
+            rows_in[g * each : (g + 1) * each, i * BLOCK : (i + 1) * BLOCK] = turned[
+                i * each : (i + 1) * each
             ]
-
-
-def lines_kernel(rows_ref, out_far, out_near, sems):
-    groups = rows_ref.shape[0] // ROWS
-    blocks = rows_ref.shape[1] // BLOCK
-    sources = out_near.shape[0] // groups
-    turn = turning(blocks, out_near.shape[1] // blocks, sources, True)
+    units = hidden.shape[1]
+    step = 256
+    for at in range(0, units, step):
+        lanes = slice(at, at + step)
+        gated = jnp.dot(rows_in[...], gate[0, :, lanes], preferred_element_type=jnp.float32)
+        raised = jnp.dot(rows_in[...], up[0, :, lanes], preferred_element_type=jnp.float32)
+        hidden[:, lanes] = (gated / (1.0 + jnp.exp(-gated)) * raised).astype(jnp.bfloat16)
+    for i in range(blocks):
+        lanes = slice(i * BLOCK, (i + 1) * BLOCK)
+        output = jnp.dot(hidden[...], down[0, :, lanes], preferred_element_type=jnp.float32)
+        rows_out[:, i * each : (i + 1) * each, :] = output.astype(jnp.bfloat16).reshape(
+            groups, each, BLOCK
+        )
+    turn = turning(blocks, capacity, sources, True)
     outward = []
     for g in range(groups):
         part = pl.ds(g * sources, sources)
-        stacked = jnp.concatenate(
-            [
-                rows_ref[g * ROWS : (g + 1) * ROWS, i * BLOCK : (i + 1) * BLOCK]
-                for i in range(blocks)
-            ],
-            axis=0,
-        )
         out_near[part] = (
-            jnp.dot(turn, stacked, preferred_element_type=jnp.float32)
+            jnp.dot(turn, rows_out[g], preferred_element_type=jnp.float32)
             .astype(jnp.bfloat16)
-            .reshape(sources, out_near.shape[1], BLOCK)
+            .reshape(sources, arrived.shape[1], BLOCK)
         )
         copy = pltpu.make_async_copy(out_near.at[part], out_far.at[part], sems.at[g])
         copy.start()
@@ -394,40 +391,30 @@
 
 def run_expert(arrived, gate, up, down):
     experts, lines, _ = arrived.shape
-    width = gate.shape[0]
+    _, width, units = gate.shape
     token_rows = experts * lines // (width // BLOCK)
     groups = token_rows // ROWS
-    params = pltpu.CompilerParams(vmem_limit_bytes=12 << 20)
-    cost = pl.CostEstimate(flops=540_000_000, bytes_accessed=4_200_000, transcendentals=0)
-    rows = pl.pallas_call(
-        rows_kernel,
-        out_shape=jax.ShapeDtypeStruct((token_rows, width), jnp.bfloat16),
-        in_specs=[VMEM],
-        out_specs=VMEM,
-        compiler_params=params,
-        cost_estimate=cost,
-        name="slots_to_rows",
-    )(arrived)
-    gate_part = jnp.dot(rows, gate, preferred_element_type=jnp.float32)
-    gate_part, up = lax.optimization_barrier((gate_part, up))
-    up_part = jnp.dot(rows, up, preferred_element_type=jnp.float32)
-    expert_hidden, down = lax.optimization_barrier(
-        ((jax.nn.silu(gate_part) * up_part).astype(jnp.bfloat16), down)
-    )
-    output = jnp.dot(expert_hidden, down, preferred_element_type=jnp.float32).astype(jnp.bfloat16)
     return pl.pallas_call(
-        lines_kernel,
+        expert_kernel,
         out_shape=pltpu.HBM(arrived.shape, jnp.bfloat16),
-        in_specs=[VMEM],
+        in_specs=[VMEM] * 4,
         out_specs=HBM,
         scratch_shapes=[
+            pltpu.VMEM((token_rows, width), jnp.bfloat16),
+            pltpu.VMEM((token_rows, units), jnp.bfloat16),
+            pltpu.VMEM((groups, token_rows, BLOCK), jnp.bfloat16),
             pltpu.VMEM(arrived.shape, jnp.bfloat16),
             pltpu.SemaphoreType.DMA((groups,)),
         ],
-        compiler_params=params,
-        cost_estimate=cost,
-        name="rows_to_slots",
-    )(output)
+        compiler_params=pltpu.CompilerParams(vmem_limit_bytes=12 << 20),
+        cost_estimate=pl.CostEstimate(
+            flops=5_900_000_000, bytes_accessed=23_000_000, transcendentals=200_000
+        ),
+        name="expert",
+    )(
+        arrived,
+        *(pltpu.with_memory_space_constraint(array, pltpu.VMEM) for array in (gate, up, down)),
+    )
 
 
 def mixing_kernel(target, gate_of, high_far, low_far, high_ref, low_ref, sems):
@@ -591,6 +578,8 @@
     peers = lax.axis_size("dev")
     chips = peers // 2
     place = lax.axis_index("dev")
+    spot = jnp.stack([place >> 1, place & 1])
+    queries, spot = lax.optimization_barrier((queries, spot))
     same_core = [[2 * chip + side for chip in range(chips)] for side in range(2)]
     experts = router_weight.shape[1]
     capacity = 2
@@ -611,7 +600,7 @@
     regrouped = lax.all_to_all(
         attended, "dev", split_axis=0, concat_axis=0, axis_index_groups=same_core, tiled=True
     )
-    spot = jnp.stack([place // 2, place % 2])
+    routes, regrouped = lax.optimization_barrier((routes, regrouped))
     ends = scatter_sum(regrouped, out_weight, weight_beside, spot, peers)
 
     rank = rank_of(routes.reshape(-1), experts).reshape(rows, -1)
@@ -632,7 +621,7 @@
         concat_axis=0,
         tiled=True,
     )
-    output_rows = run_expert(arrived, expert_gate[0], expert_up[0], expert_down[0])
+    output_rows = run_expert(arrived, expert_gate, expert_up, expert_down)
     returned = lax.all_to_all(
         output_rows, ("attn", "dev"), split_axis=0, concat_axis=0, tiled=True
     ).reshape(experts * lines, BLOCK)

time: 140 us -> 138 us (0.986)
  matrix products: 5.74 us -> 0.24 us
  waiting for transfers between devices: 38.9 us -> 43.1 us
  starting transfers between devices: 26.3 us -> 23.1 us
  Pallas kernels: 20.6 us -> 22.9 us
    dot_general x3 -> x0, matrix products: 5.49 us -> none  [the longest x1 1.86 us: run_expert(): up_part = jnp.dot(rows, up, preferred_element_type=jnp.float32)]
    pallas_call x2 -> x1, Pallas kernels: 2.36 us -> 7.22 us  [run_expert(): pl.pallas_call(expert_kernel, out_shape=pltpu.HBM(arrived.shape, jnp.bflo...]
    ppermute x12, waiting for transfers between devices: 5.09 us -> 9 us  [swap(): lax.ppermute(array, 'dev', [(i, i ^ 2 * jump[way]) for i in range(peers)])]
    ppermute x12, starting transfers between devices: 12.3 us -> 9 us  [swap(): lax.ppermute(array, 'dev', [(i, i ^ 2 * jump[way]) for i in range(peers)])]
    pallas_call x2, Pallas kernels: 7.48 us -> 4.87 us  [project(): pl.pallas_call(functools.partial(projection_kernel, orders), out_shape=[j...]
    unnamed x23 -> x24, local copies, waits for them, and re-layouts: 1.78 us -> 0.08 us
  transfers between devices with their start and end apart: 15 -> 15, of which waited for: 8 -> 10; matrix products, arithmetic and copies ran while one was open for 2% -> 3% of each run, Pallas kernels for 8% -> 7%
where the time goes in v4:
time: 138 us; the launch traced here: 137 us
  blocking collectives  43.7 us (32%)
  waiting for transfers between devices  43.1 us (31%)
  starting transfers between devices  23.1 us (17%)
  Pallas kernels  22.9 us (17%)
  other arithmetic  2.39 us (2%)
  local copies, waits for them, and re-layouts  1.43 us (1%)
    all_to_all x1, blocking collectives, shards(): lax.all_to_all(sent.reshape(experts, lines, BLOCK), ('attn', 'dev'), spli...  43.7 us
    all_to_all x1, waiting for transfers between devices, shards(): lax.all_to_all(output_rows, ('attn', 'dev'), split_axis=0, concat_axis=0,...  26.2 us
    ppermute x12, waiting for transfers between devices, swap(): lax.ppermute(array, 'dev', [(i, i ^ 2 * jump[way]) for i in range(peers)])  9 us
    ppermute x12, starting transfers between devices, swap(): lax.ppermute(array, 'dev', [(i, i ^ 2 * jump[way]) for i in range(peers)])  9 us
    all_to_all x1, starting transfers between devices, shards(): lax.all_to_all(attended, 'dev', split_axis=0, concat_axis=0, axis_index_g...  7.99 us
    all_to_all x1, waiting for transfers between devices, shards(): lax.all_to_all(attended, 'dev', split_axis=0, concat_axis=0, axis_index_g...  7.87 us
    pallas_call x1, Pallas kernels, run_expert(): pl.pallas_call(expert_kernel, out_shape=pltpu.HBM(arrived.shape, jnp.bflo...  7.22 us
    pallas_call x2, Pallas kernels, project(): pl.pallas_call(functools.partial(projection_kernel, orders), out_shape=[j...  4.87 us
  transfers between devices with their start and end apart: 15, of which 10 were waited for; matrix products, arithmetic and copies ran while one was open for 3% of the time, Pallas kernels for 7%

profile of v4, /device:TPU:1, one launch (start us, length us, event | category | flops | bytes accessed | tf_op | source)
XLA Modules:
  0.0 137.4 jit_solution(9357450038840752873)
XLA Ops:
  0.0 1.4 %collective-permute-start = (bf16[256,4096]{1,0:T(8,128)(2,1)}, bf16[256,4096]{1,0:T(8,128)(2,1)}, u32[]{:S(2)}, u32[]{:S(2)}) collective-permute-start(bf16[256,4096]{1,0:T(8,128)(2,1)} %mine.3), channel_id=1, source_target_pairs={{0,1},{1,0},{2,3},{3,2},{4,5},{5,4},{6,7},{7,6},{8,9},{9,8},{10,11... | collective-permute-start | bytes 6291464 | tf_op jit(solution)/shard_map/ppermute | solution.py:589
  1.5 3.6 %attention.1 = bf16[16,16,512]{2,1,0:T(8,128)(2,1)} custom-call(s32[4,16]{1,0:T(4,128)} %bitcast.27, s32[16]{0:T(128)} %lengths_far.1, bf16[16,8192]{1,0:T(8,128)(2,1)} %q_far, bf16[16,512]{1,0:T(8,128)(2,1)} %own_key_far.1, bf16[16,512]{1,0:T(8,128)(2,1)} %own_value_far.1, bf16[64,16,512]{2,1,0:T(8,128)(2,1)} %keys_far.1, bf16[64,16,512]{2,1,0:T(8,128)(2,1)} %values_far.1), custom_call_target="tpu_custom_call" | custom-call | flops 600000000 | bytes 5000000 | tf_op jit(solution)/shard_map/attention/pallas_call | solution.py:164
  5.1 8.0 %all-to-all-start = ((bf16[16,16,512]{2,1,0:T(8,128)(2,1)}), bf16[16,16,512]{2,1,0:T(8,128)(2,1)S(1)}, u32[]{:S(2)}, u32[]{:S(2)}) async-start(bf16[16,16,512]{2,1,0:T(8,128)(2,1)} %attention.1), calls=%async_computation | async-start | bytes 524288 | tf_op jit(solution)/shard_map/all_to_all | solution.py:600
  13.2 0.6 add.57
  13.8 7.9 %all-to-all-done.x_ref = bf16[16,16,512]{2,1,0:T(8,128)(2,1)S(1)} async-done(((bf16[16,16,512]{2,1,0:T(8,128)(2,1)}), bf16[16,16,512]{2,1,0:T(8,128)(2,1)S(1)}, u32[]{:S(2)}, u32[]{:S(2)}) %all-to-all-start) | async-done | bytes 262176 | tf_op jit(solution)/shard_map/all_to_all | solution.py:600
  22.4 2.4 %project_sent.1 = (bf16[8,16,1024]{2,1,0:T(8,128)(2,1)S(1)}, bf16[8,16,1024]{2,1,0:T(8,128)(2,1)S(1)}, bf16[8,16,1024]{2,1,0:T(8,128)(2,1)S(1)}, bf16[8,16,1024]{2,1,0:T(8,128)(2,1)S(1)}) custom-call(s32[2]{0:T(128)S(1)} %pad_add_fusion.spot, bf16[16,16,512]{2,1,0:T(8,128)(2,1)S(1)} %all-to-all-done.x_ref, bf16[256,4096]{1,0:T(8,128)(2,1)S(1)} %copy-done.1, ...), custom_call_target="tpu_custom_call" | custom-call | flops 540000000 | bytes 5500000 | tf_op jit(solution)/shard_map/project_sent/pallas_call | solution.py:238
  25.0 0.4 slice_reduce_fusion.7
  25.5 1.0 collective-permute-start.9
  26.4 1.2 collective-permute-start.3
  27.6 2.5 %project_kept.1 = (bf16[8,16,1024]{2,1,0:T(8,128)(2,1)S(1)}, bf16[8,16,1024]{2,1,0:T(8,128)(2,1)S(1)}, bf16[8,16,1024]{2,1,0:T(8,128)(2,1)S(1)}, bf16[8,16,1024]{2,1,0:T(8,128)(2,1)S(1)}) custom-call(s32[2]{0:T(128)S(1)} %pad_add_fusion.spot, bf16[16,16,512]{2,1,0:T(8,128)(2,1)S(1)} %all-to-all-done.x_ref, bf16[256,4096]{1,0:T(8,128)(2,1)S(1)} %copy-done.1, ...), custom_call_target="tpu_custom_call" | custom-call | flops 540000000 | bytes 5500000 | tf_op jit(solution)/shard_map/project_kept/pallas_call | solution.py:238
  30.1 1.4 %collective-permute-done.7 = bf16[8,16,1024]{2,1,0:T(8,128)(2,1)S(1)} collective-permute-done((bf16[8,16,1024]{2,1,0:T(8,128)(2,1)S(1)}, bf16[8,16,1024]{2,1,0:T(8,128)(2,1)S(1)}, u32[]{:S(2)}, u32[]{:S(2)}) %collective-permute-start.7) | collective-permute-done | bytes 262176 | tf_op jit(solution)/shard_map/ppermute | solution.py:523
  31.6 0.7 collective-permute-start.8
  32.4 0.6 collective-permute-done.9
  33.3 0.9 collective-permute-start.2
  34.3 0.9 collective-permute-start.4
  35.1 1.6 %collective-permute-done.8 = bf16[4,16,1024]{2,1,0:T(8,128)(2,1)S(1)} collective-permute-done((bf16[4,16,1024]{2,1,0:T(8,128)(2,1)S(1)}, bf16[4,16,1024]{2,1,0:T(8,128)(2,1)S(1)}, u32[]{:S(2)}, u32[]{:S(2)}) %collective-permute-start.8) | collective-permute-done | bytes 131104 | tf_op jit(solution)/shard_map/ppermute | solution.py:523
  37.0 1.9 %collective-permute-start.11 = (bf16[2,16,2048]{2,1,0:T(8,128)(2,1)S(1)}, bf16[2,16,2048]{2,1,0:T(8,128)(2,1)S(1)}, u32[]{:S(2)}, u32[]{:S(2)}) collective-permute-start(bf16[2,16,2048]{2,1,0:T(8,128)(2,1)S(1)} %pad_maximum_fusion), channel_id=1, source_target_pairs={{0,2},{1,3},{2,0},{3,1},{4,6},{5,7},{6,4},{7,5},{8,10},{9,11},{10,... | collective-permute-start | bytes 393224 | tf_op jit(solution)/shard_map/ppermute | solution.py:523
  39.1 0.9 collective-permute-start.5
  40.0 2.4 %collective-permute-done.11 = bf16[2,16,2048]{2,1,0:T(8,128)(2,1)S(1)} collective-permute-done((bf16[2,16,2048]{2,1,0:T(8,128)(2,1)S(1)}, bf16[2,16,2048]{2,1,0:T(8,128)(2,1)S(1)}, u32[]{:S(2)}, u32[]{:S(2)}) %collective-permute-start.11) | collective-permute-done | bytes 131104 | tf_op jit(solution)/shard_map/ppermute | solution.py:523
  42.6 0.4 collective-permute-done.5
  43.1 1.2 collective-permute-start.6
  44.2 0.9 fusion.7.placing
  45.2 1.7 %collective-permute-done.12.got_b = bf16[16,2048]{1,0:T(8,128)(2,1)S(1)} collective-permute-done((bf16[16,2048]{1,0:T(8,128)(2,1)S(1)}, bf16[16,2048]{1,0:T(8,128)(2,1)S(1)}, u32[]{:S(2)}, u32[]{:S(2)}) %collective-permute-start.12) | collective-permute-done | bytes 65568 | tf_op jit(solution)/shard_map/ppermute | solution.py:523
  46.9 0.6 collective-permute-done.6.got_a
  47.5 0.9 dispatch.1
  48.4 43.7 %all_to_all.15.arrived = bf16[128,16,512]{2,1,0:T(8,128)(2,1)S(1)} all-to-all(bf16[128,16,512]{2,1,0:T(8,128)(2,1)S(1)} %bitcast.24), channel_id=1, replica_groups=mesh['attn'=4,'dev'=32] {'attn','dev'}, dimensions={0} | all-to-all | bytes 4194304 | tf_op jit(solution)/shard_map/all_to_all | solution.py:617
  92.1 7.2 %expert.1 = bf16[128,16,512]{2,1,0:T(8,128)(2,1)} custom-call(bf16[128,16,512]{2,1,0:T(8,128)(2,1)S(1)} %all_to_all.15.arrived, bf16[1,4096,768]{2,1,0:T(8,128)(2,1)S(1)} %bitcast.21, bf16[1,4096,768]{2,1,0:T(8,128)(2,1)S(1)} %bitcast.23, bf16[1,768,4096]{2,1,0:T(8,128)(2,1)S(1)} %copy-done.2), custom_call_target="tpu_custom_call" | custom-call | flops 5900000256 | bytes 23000000 | tf_op jit(solution)/shard_map/expert/pallas_call | solution.py:397
  99.3 4.7 %all-to-all-start.2 = ((bf16[128,16,512]{2,1,0:T(8,128)(2,1)}), bf16[128,16,512]{2,1,0:T(8,128)(2,1)S(1)}, u32[]{:S(2)}, u32[]{:S(2)}) async-start(bf16[128,16,512]{2,1,0:T(8,128)(2,1)} %expert.1), calls=%async_computation.2 | async-start | bytes 4194304 | tf_op jit(solution)/shard_map/all_to_all | solution.py:625
  104.1 0.2 fusion.11
  104.7 3.7 %mixing.1 = (bf16[128,2048]{1,0:T(8,128)(2,1)}, bf16[128,2048]{1,0:T(8,128)(2,1)}) custom-call(s32[128,8]{1,0:T(8,128)S(1)} %broadcast_add_fusion.target, f32[128,8]{1,0:T(8,128)S(1)} %bitcast.25), custom_call_target="tpu_custom_call" | custom-call | flops 6000000 | bytes 1200000 | tf_op jit(solution)/shard_map/mixing/pallas_call | solution.py:443
  108.4 26.2 %all-to-all-done.2 = bf16[128,16,512]{2,1,0:T(8,128)(2,1)S(1)} async-done(((bf16[128,16,512]{2,1,0:T(8,128)(2,1)}), bf16[128,16,512]{2,1,0:T(8,128)(2,1)S(1)}, u32[]{:S(2)}, u32[]{:S(2)}) %all-to-all-start.2) | async-done | bytes 2097184 | tf_op jit(solution)/shard_map/all_to_all | solution.py:625
  134.6 2.7 %combine.1 = bf16[16,4096]{1,0:T(8,128)(2,1)} custom-call(bf16[128,2048]{1,0:T(8,128)(2,1)} %get-tuple-element.37.high_far, bf16[128,2048]{1,0:T(8,128)(2,1)} %get-tuple-element.38.low_far, bf16[2048,512]{1,0:T(8,128)(2,1)S(1)} %bitcast.19, f32[16,4096]{1,0:T(8,128)} %get-tuple-element.40.hidden_far), custom_call_target="tpu_custom_call" | custom-call | flops 540000000 | bytes 3500000 | tf_op jit(solution)/shard_map/combine/pallas_call | solution.py:482
  (69 shorter events, 2.4 us)
Async XLA Ops:
  0.0 104.1 %copy-start = (bf16[4096,128]{1,0:T(8,128)(2,1)S(1)}, bf16[4096,128]{1,0:T(8,128)(2,1)}, u32[]{:S(2)}) copy-start(bf16[4096,128]{1,0:T(8,128)(2,1)} %param.25) | copy-start | bytes 3145732
  0.0 22.4 %copy-start.1 = (bf16[256,4096]{1,0:T(8,128)(2,1)S(1)}, bf16[256,4096]{1,0:T(8,128)(2,1)}, u32[]{:S(2)}) copy-start(bf16[256,4096]{1,0:T(8,128)(2,1)} %mine.3) | copy-start | bytes 6291460
  0.0 21.6 %copy-start.6 = (s32[16,8]{0,1:T(8,128)S(1)}, s32[16,8]{0,1:T(8,128)}, u32[]{:S(2)}) copy-start(s32[16,8]{0,1:T(8,128)} %param.26) | copy-start | bytes 1540
  0.0 22.3 %collective-permute-start = (bf16[256,4096]{1,0:T(8,128)(2,1)}, bf16[256,4096]{1,0:T(8,128)(2,1)}, u32[]{:S(2)}, u32[]{:S(2)}) collective-permute-start(bf16[256,4096]{1,0:T(8,128)(2,1)} %mine.3), channel_id=1, source_target_pairs={{0,1},{1,0},{2,3},{3,2},{4,5},{5,4},{6,7},{7,6},{8,9},{9,8},{10,11... | collective-permute-start | bytes 6291464 | tf_op jit(solution)/shard_map/ppermute | solution.py:589
  5.1 16.5 %all-to-all-start = ((bf16[16,16,512]{2,1,0:T(8,128)(2,1)}), bf16[16,16,512]{2,1,0:T(8,128)(2,1)S(1)}, u32[]{:S(2)}, u32[]{:S(2)}) async-start(bf16[16,16,512]{2,1,0:T(8,128)(2,1)} %attention.1), calls=%async_computation | async-start | bytes 524288 | tf_op jit(solution)/shard_map/all_to_all | solution.py:600
  22.3 2.6 %copy-start.7 = (s32[128]{0:T(128)S(1)}, s32[128]{0:T(128)}, u32[]{:S(2)}) copy-start(s32[128]{0:T(128)} %add.57) | copy-start | bytes 1540
  22.4 25.1 %copy-start.3 = (bf16[16,4096]{1,0:T(8,128)(2,1)S(1)}, bf16[16,4096]{1,0:T(8,128)(2,1)}, u32[]{:S(2)}) copy-start(bf16[16,4096]{1,0:T(8,128)(2,1)} %residual.1) | copy-start | bytes 393220
  22.4 25.1 %copy-start.4 = (f32[4096]{0:T(1024)S(1)}, f32[4096]{0:T(1024)}, u32[]{:S(2)}) copy-start(f32[4096]{0:T(1024)} %param.24) | copy-start | bytes 49156
  24.8 6.8 %collective-permute-start.7 = (bf16[8,16,1024]{2,1,0:T(8,128)(2,1)S(1)}, bf16[8,16,1024]{2,1,0:T(8,128)(2,1)S(1)}, u32[]{:S(2)}, u32[]{:S(2)}) collective-permute-start(bf16[8,16,1024]{2,1,0:T(8,128)(2,1)S(1)} %get-tuple-element.33), channel_id=1, source_target_pairs={{0,8},{1,9},{2,10},{3,11},{4,12},{5,13},{6,14},{7,15},{8,0},{9,1},... | collective-permute-start | bytes 786440 | tf_op jit(solution)/shard_map/ppermute | solution.py:523
  25.0 67.1 %slice-start.2 = ((s8[6291456]{0:T(1024)(128)(4,1)}), s8[4194304]{0:T(1024)(128)(4,1)S(1)}, s32[]{:S(2)}) async-start(s8[6291456]{0:T(1024)(128)(4,1)} %bitcast.22), calls=%async_computation.5 | async-start | bytes 8388608
  25.4 7.8 %collective-permute-start.1 = (bf16[8,16,1024]{2,1,0:T(8,128)(2,1)S(1)}, bf16[8,16,1024]{2,1,0:T(8,128)(2,1)S(1)}, u32[]{:S(2)}, u32[]{:S(2)}) collective-permute-start(bf16[8,16,1024]{2,1,0:T(8,128)(2,1)S(1)} %get-tuple-element.27), channel_id=1, source_target_pairs={{0,2},{1,3},{2,0},{3,1},{4,6},{5,7},{6,4},{7,5},{8,10},{9,11},{10,... | collective-permute-start | bytes 786440 | tf_op jit(solution)/shard_map/ppermute | solution.py:523
  25.5 7.5 %collective-permute-start.9 = (bf16[8,16,1024]{2,1,0:T(8,128)(2,1)S(1)}, bf16[8,16,1024]{2,1,0:T(8,128)(2,1)S(1)}, u32[]{:S(2)}, u32[]{:S(2)}) collective-permute-start(bf16[8,16,1024]{2,1,0:T(8,128)(2,1)S(1)} %get-tuple-element.35), channel_id=1, source_target_pairs={{0,24},{1,25},{2,26},{3,27},{4,28},{5,29},{6,30},{7,31},{8,16},{9,... | collective-permute-start | bytes 786440 | tf_op jit(solution)/shard_map/ppermute | solution.py:523
  26.4 7.7 %collective-permute-start.3 = (bf16[8,16,1024]{2,1,0:T(8,128)(2,1)S(1)}, bf16[8,16,1024]{2,1,0:T(8,128)(2,1)S(1)}, u32[]{:S(2)}, u32[]{:S(2)}) collective-permute-start(bf16[8,16,1024]{2,1,0:T(8,128)(2,1)S(1)} %get-tuple-element.31), channel_id=1, source_target_pairs={{0,6},{1,7},{2,4},{3,5},{4,2},{5,3},{6,0},{7,1},{8,14},{9,15},{10,... | collective-permute-start | bytes 786440 | tf_op jit(solution)/shard_map/ppermute | solution.py:523
  27.6 64.4 %slice-start = ((s8[6291456]{0:T(1024)(128)(4,1)}), s8[4194304]{0:T(1024)(128)(4,1)S(1)}, s32[]{:S(2)}) async-start(s8[6291456]{0:T(1024)(128)(4,1)} %bitcast.20), calls=%async_computation.3 | async-start | bytes 8388608
  31.6 5.1 %collective-permute-start.8 = (bf16[4,16,1024]{2,1,0:T(8,128)(2,1)S(1)}, bf16[4,16,1024]{2,1,0:T(8,128)(2,1)S(1)}, u32[]{:S(2)}, u32[]{:S(2)}) collective-permute-start(bf16[4,16,1024]{2,1,0:T(8,128)(2,1)S(1)} %slice.105), channel_id=1, source_target_pairs={{0,24},{1,25},{2,26},{3,27},{4,28},{5,29},{6,30},{7,31},{8,16},{9,... | collective-permute-start | bytes 393224 | tf_op jit(solution)/shard_map/ppermute | solution.py:523
  33.1 3.9 %collective-permute-start.10 = (bf16[4,16,1024]{2,1,0:T(8,128)(2,1)S(1)}, bf16[4,16,1024]{2,1,0:T(8,128)(2,1)S(1)}, u32[]{:S(2)}, u32[]{:S(2)}) collective-permute-start(bf16[4,16,1024]{2,1,0:T(8,128)(2,1)S(1)} %slice.107), channel_id=1, source_target_pairs={{0,8},{1,9},{2,10},{3,11},{4,12},{5,13},{6,14},{7,15},{8,0},{9,1},... | collective-permute-start | bytes 393224 | tf_op jit(solution)/shard_map/ppermute | solution.py:523
  33.3 5.7 %collective-permute-start.2 = (bf16[4,16,1024]{2,1,0:T(8,128)(2,1)S(1)}, bf16[4,16,1024]{2,1,0:T(8,128)(2,1)S(1)}, u32[]{:S(2)}, u32[]{:S(2)}) collective-permute-start(bf16[4,16,1024]{2,1,0:T(8,128)(2,1)S(1)} %slice.97), channel_id=1, source_target_pairs={{0,6},{1,7},{2,4},{3,5},{4,2},{5,3},{6,0},{7,1},{8,14},{9,15},{10,... | collective-permute-start | bytes 393224 | tf_op jit(solution)/shard_map/ppermute | solution.py:523
  34.1 57.9 %copy-start.2 = (bf16[1,768,4096]{2,1,0:T(8,128)(2,1)S(1)}, bf16[1,768,4096]{2,1,0:T(8,128)(2,1)}, u32[]{:S(2)}) copy-start(bf16[1,768,4096]{2,1,0:T(8,128)(2,1)} %down.1) | copy-start | bytes 18874372
  34.2 57.8 %slice-start.3 = ((s8[6291456]{0:T(1024)(128)(4,1)}), s8[2097152]{0:T(1024)(128)(4,1)S(1)}, s32[]{:S(2)}) async-start(s8[6291456]{0:T(1024)(128)(4,1)} %bitcast.22), calls=%async_computation.6 | async-start | bytes 4194304
  34.3 4.8 %collective-permute-start.4 = (bf16[4,16,1024]{2,1,0:T(8,128)(2,1)S(1)}, bf16[4,16,1024]{2,1,0:T(8,128)(2,1)S(1)}, u32[]{:S(2)}, u32[]{:S(2)}) collective-permute-start(bf16[4,16,1024]{2,1,0:T(8,128)(2,1)S(1)} %slice.99), channel_id=1, source_target_pairs={{0,2},{1,3},{2,0},{3,1},{4,6},{5,7},{6,4},{7,5},{8,10},{9,11},{10,... | collective-permute-start | bytes 393224 | tf_op jit(solution)/shard_map/ppermute | solution.py:523
  36.8 55.3 %slice-start.1 = ((s8[6291456]{0:T(1024)(128)(4,1)}), s8[2097152]{0:T(1024)(128)(4,1)S(1)}, s32[]{:S(2)}) async-start(s8[6291456]{0:T(1024)(128)(4,1)} %bitcast.20), calls=%async_computation.4 | async-start | bytes 4194304
  37.0 5.4 %collective-permute-start.11 = (bf16[2,16,2048]{2,1,0:T(8,128)(2,1)S(1)}, bf16[2,16,2048]{2,1,0:T(8,128)(2,1)S(1)}, u32[]{:S(2)}, u32[]{:S(2)}) collective-permute-start(bf16[2,16,2048]{2,1,0:T(8,128)(2,1)S(1)} %pad_maximum_fusion), channel_id=1, source_target_pairs={{0,2},{1,3},{2,0},{3,1},{4,6},{5,7},{6,4},{7,5},{8,10},{9,11},{10,... | collective-permute-start | bytes 393224 | tf_op jit(solution)/shard_map/ppermute | solution.py:523
  39.1 3.9 %collective-permute-start.5 = (bf16[2,16,2048]{2,1,0:T(8,128)(2,1)S(1)}, bf16[2,16,2048]{2,1,0:T(8,128)(2,1)S(1)}, u32[]{:S(2)}, u32[]{:S(2)}) collective-permute-start(bf16[2,16,2048]{2,1,0:T(8,128)(2,1)S(1)} %pad_maximum_fusion.1), channel_id=1, source_target_pairs={{0,8},{1,9},{2,10},{3,11},{4,12},{5,13},{6,14},{7,15},{8,0},{9,1},... | collective-permute-start | bytes 393224 | tf_op jit(solution)/shard_map/ppermute | solution.py:523
  42.5 4.4 %collective-permute-start.12 = (bf16[16,2048]{1,0:T(8,128)(2,1)S(1)}, bf16[16,2048]{1,0:T(8,128)(2,1)S(1)}, u32[]{:S(2)}, u32[]{:S(2)}) collective-permute-start(bf16[16,2048]{1,0:T(8,128)(2,1)S(1)} %get-tuple-element.49), channel_id=1, source_target_pairs={{0,6},{1,7},{2,4},{3,5},{4,2},{5,3},{6,0},{7,1},{8,14},{9,15},{10,... | collective-permute-start | bytes 196616 | tf_op jit(solution)/shard_map/ppermute | solution.py:523
  43.1 4.4 %collective-permute-start.6 = (bf16[16,2048]{1,0:T(8,128)(2,1)S(1)}, bf16[16,2048]{1,0:T(8,128)(2,1)S(1)}, u32[]{:S(2)}, u32[]{:S(2)}) collective-permute-start(bf16[16,2048]{1,0:T(8,128)(2,1)S(1)} %get-tuple-element.51), channel_id=1, source_target_pairs={{0,24},{1,25},{2,26},{3,27},{4,28},{5,29},{6,30},{7,31},{8,16},{9,... | collective-permute-start | bytes 196616 | tf_op jit(solution)/shard_map/ppermute | solution.py:523
  99.3 4.7 %copy-start.5 = (bf16[16,4096]{1,0:T(8,128)(2,1)S(1)}, bf16[16,4096]{1,0:T(8,128)(2,1)}, u32[]{:S(2)}) copy-start(bf16[16,4096]{1,0:T(8,128)(2,1)} %get-tuple-element.36) | copy-start | bytes 393220
  99.3 35.2 %all-to-all-start.2 = ((bf16[128,16,512]{2,1,0:T(8,128)(2,1)}), bf16[128,16,512]{2,1,0:T(8,128)(2,1)S(1)}, u32[]{:S(2)}, u32[]{:S(2)}) async-start(bf16[128,16,512]{2,1,0:T(8,128)(2,1)} %expert.1), calls=%async_computation.2 | async-start | bytes 4194304 | tf_op jit(solution)/shard_map/all_to_all | solution.py:625

commit v5 on v4

--- a/solution.py
+++ b/solution.py
@@ -17,6 +17,7 @@
 EPSILON = 1e-06
 BLOCK = 512
 ROWS = 32
+CAPACITY = 2
 TOGETHER = 4
 CONTRACT_LAST = (((1,), (1,)), ((), ()))
 VMEM = pl.BlockSpec(memory_space=pltpu.VMEM)
@@ -32,9 +33,14 @@
     own_value_far,
     keys_far,
     values_far,
+    routes_far,
     out_far,
+    target_far,
     tables,
     lengths,
+    routes,
+    routes_near,
+    target,
     q_near,
     own_key,
     own_value,
@@ -66,11 +72,30 @@
                 (own_value_far, own_value),
                 (tables_far, tables),
                 (lengths_far, lengths),
+                (routes_far, routes),
+                (routes_far, routes_near),
             )
         )
     ]
-    for copy in inward:
+    for copy in inward[:3] + inward[5:]:
         copy.start()
+    inward[7].wait()
+    inward[8].wait()
+    chosen = routes_near[...]
+    column = lax.broadcasted_iota(jnp.int32, chosen.shape, 1)
+    rank = jnp.zeros_like(chosen)
+    for t in range(rows - 1):
+        named = jnp.zeros_like(chosen)
+        for k in range(routes.shape[0]):
+            named = jnp.where(chosen == routes[k, t], 1, named)
+        rank = rank + jnp.where(column > t, named, 0)
+    blocks = target.shape[1] // rows
+    first_line = chosen * (blocks * CAPACITY) + rank
+    target[...] = jnp.concatenate(
+        [first_line + block * CAPACITY for block in range(blocks)], axis=1
+    )
+    target_copy = pltpu.make_async_copy(target, target_far, sems.at[9])
+    target_copy.start()
     inward[0].wait()
     for head in range(HEADS):
         q_turned[head // GROUP, pl.ds(head % GROUP * rows, rows), :] = q_near[
@@ -78,6 +103,8 @@
         ].astype(jnp.float32)
     inward[1].wait()
     inward[2].wait()
+    inward[3].start()
+    inward[4].start()
     inward[5].wait()
     inward[6].wait()
     for first in range(0, rows, TOGETHER):
@@ -153,9 +180,12 @@
         outward.append(copy)
     for copy in outward:
         copy.wait()
-
-
-def attend(queries, new_keys, new_values, key_pool, value_pool, tables, lengths, chips):
+    target_copy.wait()
+
+
+def attend(
+    queries, new_keys, new_values, key_pool, value_pool, tables, lengths, routes, chips, blocks
+):
     rows = queries.shape[0]
     total = HEADS * rows
     shape = (chips, rows, HEADS * HD // chips)
@@ -163,12 +193,18 @@
     bf16, f32 = jnp.bfloat16, jnp.float32
     return pl.pallas_call(
         attention_kernel,
-        out_shape=pltpu.HBM(shape, bf16),
-        in_specs=[HBM] * 7,
-        out_specs=HBM,
+        out_shape=[
+            pltpu.HBM(shape, bf16),
+            pltpu.HBM((routes.shape[1], blocks * rows), jnp.int32),
+        ],
+        in_specs=[HBM] * 8,
+        out_specs=[HBM] * 2,
         scratch_shapes=[
             pltpu.SMEM(tables.shape[::-1], jnp.int32),
             pltpu.SMEM(lengths.shape, jnp.int32),
+            pltpu.SMEM(routes.shape[::-1], jnp.int32),
+            pltpu.VMEM(routes.shape[::-1], jnp.int32),
+            pltpu.VMEM((routes.shape[1], blocks * rows), jnp.int32),
             pltpu.VMEM(queries.shape, bf16),
             pltpu.VMEM(new_keys.shape, bf16),
             pltpu.VMEM(new_values.shape, bf16),
@@ -181,7 +217,7 @@
             pltpu.VMEM((total, wide), bf16),
             pltpu.VMEM((total, rows), bf16),
             pltpu.VMEM(shape, bf16),
-            pltpu.SemaphoreType.DMA((7,)),
+            pltpu.SemaphoreType.DMA((10,)),
             pltpu.SemaphoreType.DMA((KVH,)),
         ],
         compiler_params=pltpu.CompilerParams(vmem_limit_bytes=12 << 20),
@@ -200,6 +236,7 @@
                 new_values,
                 key_pool,
                 value_pool,
+                routes.T,
             )
         )
     )
@@ -417,84 +454,72 @@
     )
 
 
-def mixing_kernel(target, gate_of, high_far, low_far, high_ref, low_ref, sems):
-    tall, wide = high_ref.shape
+def mixing_kernel(target_ref, gates, mixing_far, mixing_ref, sem):
+    tall, wide = mixing_ref.shape
+    target = target_ref[...].T
+    gate_of = jnp.concatenate([gates[...]] * (tall // gates.shape[0]), axis=0)
     step = 256
     for at in range(0, wide, step):
         line = lax.broadcasted_iota(jnp.int32, (tall, step), 1) + at
         mixing = jnp.zeros((tall, step), jnp.float32)
         for k in range(target.shape[1]):
             mixing = jnp.where(line == target[:, k : k + 1], gate_of[:, k : k + 1], mixing)
-        high = mixing.astype(jnp.bfloat16)
-        high_ref[:, at : at + step] = high
-        low_ref[:, at : at + step] = (mixing - high.astype(jnp.float32)).astype(jnp.bfloat16)
+        mixing_ref[:, at : at + step] = mixing.astype(jnp.bfloat16)
+    copy = pltpu.make_async_copy(mixing_ref, mixing_far, sem)
+    copy.start()
+    copy.wait()
+
+
+def mix(target, gates, lines):
+    shape = (target.shape[1], lines)
+    return pl.pallas_call(
+        mixing_kernel,
+        out_shape=pltpu.HBM(shape, jnp.bfloat16),
+        in_specs=[VMEM, VMEM],
+        out_specs=HBM,
+        scratch_shapes=[pltpu.VMEM(shape, jnp.bfloat16), pltpu.SemaphoreType.DMA],
+        compiler_params=pltpu.CompilerParams(vmem_limit_bytes=8 << 20),
+        cost_estimate=pl.CostEstimate(flops=6_000_000, bytes_accessed=600_000, transcendentals=0),
+        name="mixing",
+    )(target, gates)
+
+
+def combine_kernel(mixing_far, returned, hidden_far, out_ref, mixing, hidden, sems):
+    rows = hidden.shape[0]
     copies = [
-        pltpu.make_async_copy(high_ref, high_far, sems.at[0]),
-        pltpu.make_async_copy(low_ref, low_far, sems.at[1]),
+        pltpu.make_async_copy(mixing_far, mixing, sems.at[0]),
+        pltpu.make_async_copy(hidden_far, hidden, sems.at[1]),
     ]
     for copy in copies:
         copy.start()
-    for copy in copies:
-        copy.wait()
-
-
-def mix(target, gate_of, lines):
-    shape = (target.shape[0], lines)
+    copies[0].wait()
+    mixed = jnp.dot(mixing[...], returned[...], preferred_element_type=jnp.float32)
+    copies[1].wait()
+    for i in range(mixed.shape[0] // rows):
+        lanes = slice(i * BLOCK, (i + 1) * BLOCK)
+        out_ref[:, lanes] = (hidden[:, lanes] + mixed[i * rows : (i + 1) * rows]).astype(
+            jnp.bfloat16
+        )
+
+
+def combine(mixing, returned, hidden):
+    far = [pltpu.with_memory_space_constraint(array, pltpu.HBM) for array in (mixing, hidden)]
     return pl.pallas_call(
-        mixing_kernel,
-        out_shape=[pltpu.HBM(shape, jnp.bfloat16)] * 2,
-        in_specs=[VMEM, VMEM],
-        out_specs=[HBM, HBM],
+        combine_kernel,
+        out_shape=jax.ShapeDtypeStruct(hidden.shape, jnp.bfloat16),
+        in_specs=[HBM, VMEM, HBM],
+        out_specs=VMEM,
         scratch_shapes=[
-            pltpu.VMEM(shape, jnp.bfloat16),
-            pltpu.VMEM(shape, jnp.bfloat16),
+            pltpu.VMEM(mixing.shape, jnp.bfloat16),
+            pltpu.VMEM(hidden.shape, jnp.float32),
             pltpu.SemaphoreType.DMA((2,)),
         ],
         compiler_params=pltpu.CompilerParams(vmem_limit_bytes=8 << 20),
-        cost_estimate=pl.CostEstimate(flops=6_000_000, bytes_accessed=1_200_000, transcendentals=0),
-        name="mixing",
-    )(target, gate_of)
-
-
-def combine_kernel(high_far, low_far, returned, hidden_far, out_ref, mixing, hidden, sems):
-    rows = hidden.shape[0]
-    half = high_far.shape[0]
-    copies = [
-        pltpu.make_async_copy(high_far, mixing.at[pl.ds(0, half)], sems.at[0]),
-        pltpu.make_async_copy(low_far, mixing.at[pl.ds(half, half)], sems.at[1]),
-        pltpu.make_async_copy(hidden_far, hidden, sems.at[2]),
-    ]
-    for copy in copies:
-        copy.start()
-    for copy in copies:
-        copy.wait()
-    mixed = jnp.dot(mixing[...], returned[...], preferred_element_type=jnp.float32)
-    mixed = mixed[:half] + mixed[half:]
-    for i in range(half // rows):
-        lanes = slice(i * BLOCK, (i + 1) * BLOCK)
-        out_ref[:, lanes] = (hidden[:, lanes] + mixed[i * rows : (i + 1) * rows]).astype(
-            jnp.bfloat16
-        )
-
-
-def combine(high, low, returned, hidden):
-    far = [pltpu.with_memory_space_constraint(array, pltpu.HBM) for array in (high, low, hidden)]
-    return pl.pallas_call(
-        combine_kernel,
-        out_shape=jax.ShapeDtypeStruct(hidden.shape, jnp.bfloat16),
-        in_specs=[HBM, HBM, VMEM, HBM],
-        out_specs=VMEM,
-        scratch_shapes=[
-            pltpu.VMEM((2 * high.shape[0], high.shape[1]), jnp.bfloat16),
-            pltpu.VMEM(hidden.shape, jnp.float32),
-            pltpu.SemaphoreType.DMA((3,)),
-        ],
-        compiler_params=pltpu.CompilerParams(vmem_limit_bytes=8 << 20),
         cost_estimate=pl.CostEstimate(
-            flops=540_000_000, bytes_accessed=3_500_000, transcendentals=0
+            flops=270_000_000, bytes_accessed=3_000_000, transcendentals=0
         ),
         name="combine",
-    )(far[0], far[1], returned, far[2])
+    )(far[0], returned, far[1])
 
 
 def route_gates(logits, routes):
@@ -502,14 +527,6 @@
     chosen = jnp.sum(jnp.where(matches, logits[:, None, :], 0.0), axis=-1)
     raised = jnp.exp(chosen)
     return raised / jnp.sum(raised, axis=1, keepdims=True)
-
-
-def rank_of(flat_routes, experts):
-    onehot = (flat_routes[:, None] == jnp.arange(experts, dtype=jnp.int32)[None, :]).astype(
-        jnp.int32
-    )
-    earlier = jnp.cumsum(onehot, axis=0) - onehot
-    return jnp.sum(earlier * onehot, axis=1)
 
 
 def add(left, right):
@@ -582,12 +599,11 @@
     queries, spot = lax.optimization_barrier((queries, spot))
     same_core = [[2 * chip + side for chip in range(chips)] for side in range(2)]
     experts = router_weight.shape[1]
-    capacity = 2
     blocks = width // BLOCK
-    lines = blocks * capacity
+    lines = blocks * CAPACITY
 
     weight_beside = lax.ppermute(out_weight, "dev", [(i, i ^ 1) for i in range(peers)])
-    attended = attend(
+    attended, target = attend(
         queries,
         new_keys,
         new_values,
@@ -595,22 +611,19 @@
         value_pages,
         block_tables,
         context_lengths,
+        routes,
         chips,
+        blocks,
     )
     regrouped = lax.all_to_all(
         attended, "dev", split_axis=0, concat_axis=0, axis_index_groups=same_core, tiled=True
     )
-    routes, regrouped = lax.optimization_barrier((routes, regrouped))
     ends = scatter_sum(regrouped, out_weight, weight_beside, spot, peers)
 
-    rank = rank_of(routes.reshape(-1), experts).reshape(rows, -1)
-    block_ids = jnp.arange(blocks, dtype=jnp.int32)
-    target = (routes * lines + rank)[None] + (block_ids * capacity)[:, None, None]
-    target = target.reshape(blocks * rows, -1)
     line = jnp.arange(experts * lines, dtype=jnp.int32)
-    placed = line[:, None] == target[:, 0][None, :]
-    for k in range(1, target.shape[1]):
-        placed = placed | (line[:, None] == target[:, k][None, :])
+    placed = line[:, None] == target[0][None, :]
+    for k in range(1, target.shape[0]):
+        placed = placed | (line[:, None] == target[k][None, :])
     placing = placed.astype(jnp.bfloat16)
 
     hidden_state, normed, sent = dispatch(*ends, residual, norm_gain[None], placing)
@@ -628,9 +641,8 @@
 
     logits = jnp.dot(normed, router_weight, preferred_element_type=jnp.float32)
     gate_values = route_gates(logits, routes)
-    gate_of = jnp.tile(gate_values, (blocks, 1))
-    high, low = mix(target, gate_of, experts * lines)
-    return combine(high, low, returned, hidden_state)
+    mixing = mix(target, gate_values, experts * lines)
+    return combine(mixing, returned, hidden_state)
 
 
 def solution(mesh):

time: 138 us -> 136 us (0.986)
  blocking collectives: 43.7 us -> 60.1 us
  starting transfers between devices: 23.1 us -> 15.4 us
  waiting for transfers between devices: 43.1 us -> 36.3 us
  Pallas kernels: 22.9 us -> 21 us
    all_to_all x0 -> x1, blocking collectives: none -> 16.2 us  [shards(): lax.all_to_all(attended, 'dev', split_axis=0, concat_axis=0, axis_index_g...]
    all_to_all x1 -> x0, starting transfers between devices: 7.99 us -> none  [shards(): lax.all_to_all(attended, 'dev', split_axis=0, concat_axis=0, axis_index_g...]
    all_to_all x1 -> x0, waiting for transfers between devices: 7.87 us -> none  [shards(): lax.all_to_all(attended, 'dev', split_axis=0, concat_axis=0, axis_index_g...]
    all_to_all x1, waiting for transfers between devices: 26.2 us -> 27.9 us  [shards(): lax.all_to_all(output_rows, ('attn', 'dev'), split_axis=0, concat_axis=0,...]
    pallas_call x2, Pallas kernels: 7.23 us -> 5.74 us  [the longest x1 3.82 us: attend(): pl.pallas_call(attention_kernel, out_shape=[pltpu.HBM(shape, bf16), pltpu...]
  transfers between devices with their start and end apart: 15 -> 14, of which waited for: 10 -> 8; matrix products, arithmetic and copies ran while one was open for 3% -> 2% of each run, Pallas kernels for 7% -> 6%
where the time goes in v5:
time: 136 us
  blocking collectives  60.1 us (44%)
  waiting for transfers between devices  36.3 us (27%)
  Pallas kernels  21 us (15%)
  starting transfers between devices  15.4 us (11%)
  other arithmetic  1.89 us (1%)
    all_to_all x1, blocking collectives, shards(): lax.all_to_all(sent.reshape(experts, lines, BLOCK), ('attn', 'dev'), spli...  43.9 us
    all_to_all x1, waiting for transfers between devices, shards(): lax.all_to_all(output_rows, ('attn', 'dev'), split_axis=0, concat_axis=0,...  27.9 us
    all_to_all x1, blocking collectives, shards(): lax.all_to_all(attended, 'dev', split_axis=0, concat_axis=0, axis_index_g...  16.2 us
    ppermute x12, starting transfers between devices, swap(): lax.ppermute(array, 'dev', [(i, i ^ 2 * jump[way]) for i in range(peers)])  9.32 us
    ppermute x12, waiting for transfers between devices, swap(): lax.ppermute(array, 'dev', [(i, i ^ 2 * jump[way]) for i in range(peers)])  8.39 us
    pallas_call x1, Pallas kernels, run_expert(): pl.pallas_call(expert_kernel, out_shape=pltpu.HBM(arrived.shape, jnp.bflo...  7.18 us
    pallas_call x2, Pallas kernels, project(): pl.pallas_call(functools.partial(projection_kernel, orders), out_shape=[j...  4.99 us
    all_to_all x1, starting transfers between devices, shards(): lax.all_to_all(output_rows, ('attn', 'dev'), split_axis=0, concat_axis=0,...  4.7 us
  transfers between devices with their start and end apart: 14, of which 8 were waited for; matrix products, arithmetic and copies ran while one was open for 2% of the time, Pallas kernels for 6%

profile of v5, /device:TPU:1, one launch (start us, length us, event | category | flops | bytes accessed | tf_op | source)
XLA Modules:
  0.0 135.7 jit_solution(10972459138322797302)
XLA Ops:
  0.0 1.4 %collective-permute-start = (bf16[256,4096]{1,0:T(8,128)(2,1)}, bf16[256,4096]{1,0:T(8,128)(2,1)}, u32[]{:S(2)}, u32[]{:S(2)}) collective-permute-start(bf16[256,4096]{1,0:T(8,128)(2,1)} %mine.3), channel_id=1, source_target_pairs={{0,1},{1,0},{2,3},{3,2},{4,5},{5,4},{6,7},{7,6},{8,9},{9,8},{10,11... | collective-permute-start | bytes 6291464 | tf_op jit(solution)/shard_map/ppermute | solution.py:605
  1.5 3.8 %attention.1 = (bf16[16,16,512]{2,1,0:T(8,128)(2,1)}, s32[8,128]{1,0:T(8,128)}) custom-call(s32[4,16]{1,0:T(4,128)} %bitcast.41, s32[16]{0:T(128)} %lengths_far.1, bf16[16,8192]{1,0:T(8,128)(2,1)} %q_far, bf16[16,512]{1,0:T(8,128)(2,1)} %own_key_far.1, bf16[16,512]{1,0:T(8,128)(2,1)} %own_value_far.1, bf16[64,16,512]{2,1,0:T(8,128)(2,1)} %keys_far.1, ...), custom_call_target="tpu_custom_call" | custom-call | flops 600000000 | bytes 5000000 | tf_op jit(solution)/shard_map/attention/pallas_call | solution.py:194
  5.3 16.2 %all_to_all.15.x_ref = bf16[16,16,512]{2,1,0:T(8,128)(2,1)S(1)} all-to-all(bf16[16,16,512]{2,1,0:T(8,128)(2,1)} %get-tuple-element.24), channel_id=1, replica_groups={{0,2,4,6,8,10,12,14,16,18,20,22,24,26,28,30},{1,3,5,7,9,11,13,15,17,19,..., dimensions={0} | all-to-all | bytes 524288 | tf_op jit(solution)/shard_map/all_to_all | solution.py:618
  21.6 2.5 %project_sent.1 = (bf16[8,16,1024]{2,1,0:T(8,128)(2,1)S(1)}, bf16[8,16,1024]{2,1,0:T(8,128)(2,1)S(1)}, bf16[8,16,1024]{2,1,0:T(8,128)(2,1)S(1)}, bf16[8,16,1024]{2,1,0:T(8,128)(2,1)S(1)}) custom-call(s32[2]{0:T(128)S(1)} %pad_add_fusion.spot, bf16[16,16,512]{2,1,0:T(8,128)(2,1)S(1)} %all_to_all.15.x_ref, bf16[256,4096]{1,0:T(8,128)(2,1)S(1)} %copy-done.1, ...), custom_call_target="tpu_custom_call" | custom-call | flops 540000000 | bytes 5500000 | tf_op jit(solution)/shard_map/project_sent/pallas_call | solution.py:275
  24.2 0.1 collective-permute-start.1
  24.3 1.1 collective-permute-start.9
  25.4 1.2 collective-permute-start.3
  26.6 2.5 %project_kept.1 = (bf16[8,16,1024]{2,1,0:T(8,128)(2,1)S(1)}, bf16[8,16,1024]{2,1,0:T(8,128)(2,1)S(1)}, bf16[8,16,1024]{2,1,0:T(8,128)(2,1)S(1)}, bf16[8,16,1024]{2,1,0:T(8,128)(2,1)S(1)}) custom-call(s32[2]{0:T(128)S(1)} %pad_add_fusion.spot, bf16[16,16,512]{2,1,0:T(8,128)(2,1)S(1)} %all_to_all.15.x_ref, bf16[256,4096]{1,0:T(8,128)(2,1)S(1)} %copy-done.1, ...), custom_call_target="tpu_custom_call" | custom-call | flops 540000000 | bytes 5500000 | tf_op jit(solution)/shard_map/project_kept/pallas_call | solution.py:275
  29.1 1.5 %collective-permute-done.7 = bf16[8,16,1024]{2,1,0:T(8,128)(2,1)S(1)} collective-permute-done((bf16[8,16,1024]{2,1,0:T(8,128)(2,1)S(1)}, bf16[8,16,1024]{2,1,0:T(8,128)(2,1)S(1)}, u32[]{:S(2)}, u32[]{:S(2)}) %collective-permute-start.7) | collective-permute-done | bytes 262176 | tf_op jit(solution)/shard_map/ppermute | solution.py:540
  30.8 0.7 collective-permute-start.8
  31.4 0.2 collective-permute-done.9
  31.9 1.1 collective-permute-start.2
  33.1 0.7 collective-permute-start.4
  33.8 2.1 %collective-permute-done.8 = bf16[4,16,1024]{2,1,0:T(8,128)(2,1)S(1)} collective-permute-done((bf16[4,16,1024]{2,1,0:T(8,128)(2,1)S(1)}, bf16[4,16,1024]{2,1,0:T(8,128)(2,1)S(1)}, u32[]{:S(2)}, u32[]{:S(2)}) %collective-permute-start.8) | collective-permute-done | bytes 131104 | tf_op jit(solution)/shard_map/ppermute | solution.py:540
  36.0 1.3 collective-permute-start.11
  37.4 1.2 collective-permute-start.5
  38.7 2.0 %collective-permute-done.11 = bf16[2,16,2048]{2,1,0:T(8,128)(2,1)S(1)} collective-permute-done((bf16[2,16,2048]{2,1,0:T(8,128)(2,1)S(1)}, bf16[2,16,2048]{2,1,0:T(8,128)(2,1)S(1)}, u32[]{:S(2)}, u32[]{:S(2)}) %collective-permute-start.11) | collective-permute-done | bytes 131104 | tf_op jit(solution)/shard_map/ppermute | solution.py:540
  40.8 0.8 collective-permute-done.5
  41.7 1.7 %collective-permute-start.6 = (bf16[16,2048]{1,0:T(8,128)(2,1)S(1)}, bf16[16,2048]{1,0:T(8,128)(2,1)S(1)}, u32[]{:S(2)}, u32[]{:S(2)}) collective-permute-start(bf16[16,2048]{1,0:T(8,128)(2,1)S(1)} %get-tuple-element.39), channel_id=1, source_target_pairs={{0,24},{1,25},{2,26},{3,27},{4,28},{5,29},{6,30},{7,31},{8,16},{9,... | collective-permute-start | bytes 196616 | tf_op jit(solution)/shard_map/ppermute | solution.py:540
  43.4 0.9 fusion.7.placing
  44.3 0.8 collective-permute-done.12.got_b
  45.1 1.0 collective-permute-done.6.got_a
  46.1 0.9 dispatch.1
  47.0 43.9 %all_to_all.16.arrived = bf16[128,16,512]{2,1,0:T(8,128)(2,1)S(1)} all-to-all(bf16[128,16,512]{2,1,0:T(8,128)(2,1)S(1)} %bitcast.38), channel_id=1, replica_groups=mesh['attn'=4,'dev'=32] {'attn','dev'}, dimensions={0} | all-to-all | bytes 4194304 | tf_op jit(solution)/shard_map/all_to_all | solution.py:630
  90.9 7.2 %expert.1 = bf16[128,16,512]{2,1,0:T(8,128)(2,1)} custom-call(bf16[128,16,512]{2,1,0:T(8,128)(2,1)S(1)} %all_to_all.16.arrived, bf16[1,4096,768]{2,1,0:T(8,128)(2,1)S(1)} %bitcast.35, bf16[1,4096,768]{2,1,0:T(8,128)(2,1)S(1)} %bitcast.37, bf16[1,768,4096]{2,1,0:T(8,128)(2,1)S(1)} %copy-done.2), custom_call_target="tpu_custom_call" | custom-call | flops 5900000256 | bytes 23000000 | tf_op jit(solution)/shard_map/expert/pallas_call | solution.py:434
  98.1 4.7 %all-to-all-start.2 = ((bf16[128,16,512]{2,1,0:T(8,128)(2,1)}), bf16[128,16,512]{2,1,0:T(8,128)(2,1)S(1)}, u32[]{:S(2)}, u32[]{:S(2)}) async-start(bf16[128,16,512]{2,1,0:T(8,128)(2,1)} %expert.1), calls=%async_computation.2 | async-start | bytes 4194304 | tf_op jit(solution)/shard_map/all_to_all | solution.py:638
  102.9 0.2 fusion.10
  103.1 0.2 select_reduce_fusion
  103.3 0.1 exponential_reduce_fusion
  103.5 1.9 %mixing.1.mixing_far = bf16[128,2048]{1,0:T(8,128)(2,1)} custom-call(s32[8,128]{1,0:T(8,128)S(1)} %copy-done.3, f32[16,8]{1,0:T(8,128)S(1)} %exponential_divide_fusion.gates), custom_call_target="tpu_custom_call" | custom-call | flops 6000000 | bytes 600000 | tf_op jit(solution)/shard_map/mixing/pallas_call | solution.py:475
  105.4 27.9 %all-to-all-done.2 = bf16[128,16,512]{2,1,0:T(8,128)(2,1)S(1)} async-done(((bf16[128,16,512]{2,1,0:T(8,128)(2,1)}), bf16[128,16,512]{2,1,0:T(8,128)(2,1)S(1)}, u32[]{:S(2)}, u32[]{:S(2)}) %all-to-all-start.2) | async-done | bytes 2097184 | tf_op jit(solution)/shard_map/all_to_all | solution.py:638
  133.3 2.2 %combine.1 = bf16[16,4096]{1,0:T(8,128)(2,1)} custom-call(bf16[128,2048]{1,0:T(8,128)(2,1)} %mixing.1.mixing_far, bf16[2048,512]{1,0:T(8,128)(2,1)S(1)} %bitcast.33, f32[16,4096]{1,0:T(8,128)} %get-tuple-element.36.hidden_far), custom_call_target="tpu_custom_call" | custom-call | flops 270000000 | bytes 3000000 | tf_op jit(solution)/shard_map/combine/pallas_call | solution.py:507
  (57 shorter events, 1.1 us)
Async XLA Ops:
  0.0 102.9 %copy-start = (bf16[4096,128]{1,0:T(8,128)(2,1)S(1)}, bf16[4096,128]{1,0:T(8,128)(2,1)}, u32[]{:S(2)}) copy-start(bf16[4096,128]{1,0:T(8,128)(2,1)} %param.25) | copy-start | bytes 3145732
  0.0 21.6 %copy-start.1 = (bf16[256,4096]{1,0:T(8,128)(2,1)S(1)}, bf16[256,4096]{1,0:T(8,128)(2,1)}, u32[]{:S(2)}) copy-start(bf16[256,4096]{1,0:T(8,128)(2,1)} %mine.3) | copy-start | bytes 6291460
  0.0 21.5 %collective-permute-start = (bf16[256,4096]{1,0:T(8,128)(2,1)}, bf16[256,4096]{1,0:T(8,128)(2,1)}, u32[]{:S(2)}, u32[]{:S(2)}) collective-permute-start(bf16[256,4096]{1,0:T(8,128)(2,1)} %mine.3), channel_id=1, source_target_pairs={{0,1},{1,0},{2,3},{3,2},{4,5},{5,4},{6,7},{7,6},{8,9},{9,8},{10,11... | collective-permute-start | bytes 6291464 | tf_op jit(solution)/shard_map/ppermute | solution.py:605
  21.6 2.6 %copy-start.3 = (s32[8,128]{1,0:T(8,128)S(1)}, s32[8,128]{1,0:T(8,128)}, u32[]{:S(2)}) copy-start(s32[8,128]{1,0:T(8,128)} %get-tuple-element.22.target_ref) | copy-start | bytes 12292
  21.6 69.3 %slice-start.2 = ((s8[6291456]{0:T(1024)(128)(4,1)}), s8[4194304]{0:T(1024)(128)(4,1)S(1)}, s32[]{:S(2)}) async-start(s8[6291456]{0:T(1024)(128)(4,1)} %bitcast.36), calls=%async_computation.5 | async-start | bytes 8388608
  24.1 6.6 %collective-permute-start.7 = (bf16[8,16,1024]{2,1,0:T(8,128)(2,1)S(1)}, bf16[8,16,1024]{2,1,0:T(8,128)(2,1)S(1)}, u32[]{:S(2)}, u32[]{:S(2)}) collective-permute-start(bf16[8,16,1024]{2,1,0:T(8,128)(2,1)S(1)} %get-tuple-element.31), channel_id=1, source_target_pairs={{0,8},{1,9},{2,10},{3,11},{4,12},{5,13},{6,14},{7,15},{8,0},{9,1},... | collective-permute-start | bytes 786440 | tf_op jit(solution)/shard_map/ppermute | solution.py:540
  24.2 7.6 %collective-permute-start.1 = (bf16[8,16,1024]{2,1,0:T(8,128)(2,1)S(1)}, bf16[8,16,1024]{2,1,0:T(8,128)(2,1)S(1)}, u32[]{:S(2)}, u32[]{:S(2)}) collective-permute-start(bf16[8,16,1024]{2,1,0:T(8,128)(2,1)S(1)} %get-tuple-element.25), channel_id=1, source_target_pairs={{0,2},{1,3},{2,0},{3,1},{4,6},{5,7},{6,4},{7,5},{8,10},{9,11},{10,... | collective-permute-start | bytes 786440 | tf_op jit(solution)/shard_map/ppermute | solution.py:540
  24.3 7.3 %collective-permute-start.9 = (bf16[8,16,1024]{2,1,0:T(8,128)(2,1)S(1)}, bf16[8,16,1024]{2,1,0:T(8,128)(2,1)S(1)}, u32[]{:S(2)}, u32[]{:S(2)}) collective-permute-start(bf16[8,16,1024]{2,1,0:T(8,128)(2,1)S(1)} %get-tuple-element.33), channel_id=1, source_target_pairs={{0,24},{1,25},{2,26},{3,27},{4,28},{5,29},{6,30},{7,31},{8,16},{9,... | collective-permute-start | bytes 786440 | tf_op jit(solution)/shard_map/ppermute | solution.py:540
  25.4 7.6 %collective-permute-start.3 = (bf16[8,16,1024]{2,1,0:T(8,128)(2,1)S(1)}, bf16[8,16,1024]{2,1,0:T(8,128)(2,1)S(1)}, u32[]{:S(2)}, u32[]{:S(2)}) collective-permute-start(bf16[8,16,1024]{2,1,0:T(8,128)(2,1)S(1)} %get-tuple-element.29), channel_id=1, source_target_pairs={{0,6},{1,7},{2,4},{3,5},{4,2},{5,3},{6,0},{7,1},{8,14},{9,15},{10,... | collective-permute-start | bytes 786440 | tf_op jit(solution)/shard_map/ppermute | solution.py:540
  26.6 64.2 %slice-start = ((s8[6291456]{0:T(1024)(128)(4,1)}), s8[4194304]{0:T(1024)(128)(4,1)S(1)}, s32[]{:S(2)}) async-start(s8[6291456]{0:T(1024)(128)(4,1)} %bitcast.34), calls=%async_computation.3 | async-start | bytes 8388608
  30.8 5.1 %collective-permute-start.8 = (bf16[4,16,1024]{2,1,0:T(8,128)(2,1)S(1)}, bf16[4,16,1024]{2,1,0:T(8,128)(2,1)S(1)}, u32[]{:S(2)}, u32[]{:S(2)}) collective-permute-start(bf16[4,16,1024]{2,1,0:T(8,128)(2,1)S(1)} %slice.105), channel_id=1, source_target_pairs={{0,24},{1,25},{2,26},{3,27},{4,28},{5,29},{6,30},{7,31},{8,16},{9,... | collective-permute-start | bytes 393224 | tf_op jit(solution)/shard_map/ppermute | solution.py:540
  31.7 4.2 %collective-permute-start.10 = (bf16[4,16,1024]{2,1,0:T(8,128)(2,1)S(1)}, bf16[4,16,1024]{2,1,0:T(8,128)(2,1)S(1)}, u32[]{:S(2)}, u32[]{:S(2)}) collective-permute-start(bf16[4,16,1024]{2,1,0:T(8,128)(2,1)S(1)} %slice.107), channel_id=1, source_target_pairs={{0,8},{1,9},{2,10},{3,11},{4,12},{5,13},{6,14},{7,15},{8,0},{9,1},... | collective-permute-start | bytes 393224 | tf_op jit(solution)/shard_map/ppermute | solution.py:540
  31.8 59.0 %slice-start.3 = ((s8[6291456]{0:T(1024)(128)(4,1)}), s8[2097152]{0:T(1024)(128)(4,1)S(1)}, s32[]{:S(2)}) async-start(s8[6291456]{0:T(1024)(128)(4,1)} %bitcast.36), calls=%async_computation.6 | async-start | bytes 4194304
  31.9 5.4 %collective-permute-start.2 = (bf16[4,16,1024]{2,1,0:T(8,128)(2,1)S(1)}, bf16[4,16,1024]{2,1,0:T(8,128)(2,1)S(1)}, u32[]{:S(2)}, u32[]{:S(2)}) collective-permute-start(bf16[4,16,1024]{2,1,0:T(8,128)(2,1)S(1)} %slice.97), channel_id=1, source_target_pairs={{0,6},{1,7},{2,4},{3,5},{4,2},{5,3},{6,0},{7,1},{8,14},{9,15},{10,... | collective-permute-start | bytes 393224 | tf_op jit(solution)/shard_map/ppermute | solution.py:540
  33.1 4.3 %collective-permute-start.4 = (bf16[4,16,1024]{2,1,0:T(8,128)(2,1)S(1)}, bf16[4,16,1024]{2,1,0:T(8,128)(2,1)S(1)}, u32[]{:S(2)}, u32[]{:S(2)}) collective-permute-start(bf16[4,16,1024]{2,1,0:T(8,128)(2,1)S(1)} %slice.99), channel_id=1, source_target_pairs={{0,2},{1,3},{2,0},{3,1},{4,6},{5,7},{6,4},{7,5},{8,10},{9,11},{10,... | collective-permute-start | bytes 393224 | tf_op jit(solution)/shard_map/ppermute | solution.py:540
  35.9 10.2 %copy-start.4 = (bf16[16,4096]{1,0:T(8,128)(2,1)S(1)}, bf16[16,4096]{1,0:T(8,128)(2,1)}, u32[]{:S(2)}) copy-start(bf16[16,4096]{1,0:T(8,128)(2,1)} %residual.1) | copy-start | bytes 393220
  35.9 10.2 %copy-start.5 = (f32[4096]{0:T(1024)S(1)}, f32[4096]{0:T(1024)}, u32[]{:S(2)}) copy-start(f32[4096]{0:T(1024)} %param.24) | copy-start | bytes 49156
  35.9 54.9 %slice-start.1 = ((s8[6291456]{0:T(1024)(128)(4,1)}), s8[2097152]{0:T(1024)(128)(4,1)S(1)}, s32[]{:S(2)}) async-start(s8[6291456]{0:T(1024)(128)(4,1)} %bitcast.34), calls=%async_computation.4 | async-start | bytes 4194304
  36.0 4.6 %collective-permute-start.11 = (bf16[2,16,2048]{2,1,0:T(8,128)(2,1)S(1)}, bf16[2,16,2048]{2,1,0:T(8,128)(2,1)S(1)}, u32[]{:S(2)}, u32[]{:S(2)}) collective-permute-start(bf16[2,16,2048]{2,1,0:T(8,128)(2,1)S(1)} %pad_maximum_fusion), channel_id=1, source_target_pairs={{0,2},{1,3},{2,0},{3,1},{4,6},{5,7},{6,4},{7,5},{8,10},{9,11},{10,... | collective-permute-start | bytes 393224 | tf_op jit(solution)/shard_map/ppermute | solution.py:540
  37.4 4.2 %collective-permute-start.5 = (bf16[2,16,2048]{2,1,0:T(8,128)(2,1)S(1)}, bf16[2,16,2048]{2,1,0:T(8,128)(2,1)S(1)}, u32[]{:S(2)}, u32[]{:S(2)}) collective-permute-start(bf16[2,16,2048]{2,1,0:T(8,128)(2,1)S(1)} %pad_maximum_fusion.1), channel_id=1, source_target_pairs={{0,8},{1,9},{2,10},{3,11},{4,12},{5,13},{6,14},{7,15},{8,0},{9,1},... | collective-permute-start | bytes 393224 | tf_op jit(solution)/shard_map/ppermute | solution.py:540
  40.7 4.4 %collective-permute-start.12 = (bf16[16,2048]{1,0:T(8,128)(2,1)S(1)}, bf16[16,2048]{1,0:T(8,128)(2,1)S(1)}, u32[]{:S(2)}, u32[]{:S(2)}) collective-permute-start(bf16[16,2048]{1,0:T(8,128)(2,1)S(1)} %get-tuple-element.37), channel_id=1, source_target_pairs={{0,6},{1,7},{2,4},{3,5},{4,2},{5,3},{6,0},{7,1},{8,14},{9,15},{10,... | collective-permute-start | bytes 196616 | tf_op jit(solution)/shard_map/ppermute | solution.py:540
  41.6 49.2 %copy-start.2 = (bf16[1,768,4096]{2,1,0:T(8,128)(2,1)S(1)}, bf16[1,768,4096]{2,1,0:T(8,128)(2,1)}, u32[]{:S(2)}) copy-start(bf16[1,768,4096]{2,1,0:T(8,128)(2,1)} %down.1) | copy-start | bytes 18874372
  41.7 4.4 %collective-permute-start.6 = (bf16[16,2048]{1,0:T(8,128)(2,1)S(1)}, bf16[16,2048]{1,0:T(8,128)(2,1)S(1)}, u32[]{:S(2)}, u32[]{:S(2)}) collective-permute-start(bf16[16,2048]{1,0:T(8,128)(2,1)S(1)} %get-tuple-element.39), channel_id=1, source_target_pairs={{0,24},{1,25},{2,26},{3,27},{4,28},{5,29},{6,30},{7,31},{8,16},{9,... | collective-permute-start | bytes 196616 | tf_op jit(solution)/shard_map/ppermute | solution.py:540
  98.1 4.7 %copy-start.7 = (s32[16,8]{0,1:T(8,128)S(1)}, s32[16,8]{0,1:T(8,128)}, u32[]{:S(2)}) copy-start(s32[16,8]{0,1:T(8,128)} %param.26) | copy-start | bytes 1540
  98.1 4.8 %copy-start.6 = (bf16[16,4096]{1,0:T(8,128)(2,1)S(1)}, bf16[16,4096]{1,0:T(8,128)(2,1)}, u32[]{:S(2)}) copy-start(bf16[16,4096]{1,0:T(8,128)(2,1)} %get-tuple-element.34) | copy-start | bytes 393220
  98.1 35.2 %all-to-all-start.2 = ((bf16[128,16,512]{2,1,0:T(8,128)(2,1)}), bf16[128,16,512]{2,1,0:T(8,128)(2,1)S(1)}, u32[]{:S(2)}, u32[]{:S(2)}) async-start(bf16[128,16,512]{2,1,0:T(8,128)(2,1)} %expert.1), calls=%async_computation.2 | async-start | bytes 4194304 | tf_op jit(solution)/shard_map/all_to_all | solution.py:638

commit v6 on v5

--- a/solution.py
+++ b/solution.py
@@ -602,7 +602,6 @@
     blocks = width // BLOCK
     lines = blocks * CAPACITY
 
-    weight_beside = lax.ppermute(out_weight, "dev", [(i, i ^ 1) for i in range(peers)])
     attended, target = attend(
         queries,
         new_keys,
@@ -615,6 +614,8 @@
         chips,
         blocks,
     )
+    attended, weight_sent = lax.optimization_barrier((attended, out_weight))
+    weight_beside = lax.ppermute(weight_sent, "dev", [(i, i ^ 1) for i in range(peers)])
     regrouped = lax.all_to_all(
         attended, "dev", split_axis=0, concat_axis=0, axis_index_groups=same_core, tiled=True
     )

time: 136 us -> 135 us (level)
  Pallas kernels: 21 us -> 18.7 us
  waiting for transfers between devices: 36.3 us -> 37.8 us
    pallas_call x2, Pallas kernels: 4.99 us -> 2.54 us  [project(): pl.pallas_call(functools.partial(projection_kernel, orders), out_shape=[j...]
    ppermute x12, waiting for transfers between devices: 8.39 us -> 9.89 us  [swap(): lax.ppermute(array, 'dev', [(i, i ^ 2 * jump[way]) for i in range(peers)])]
  transfers between devices with their start and end apart: 14 -> 14, of which waited for: 8 -> 8; matrix products, arithmetic and copies ran while one was open for 2% -> 2% of each run, Pallas kernels for 6% -> 2%
where the time goes in v6:
time: 135 us
  blocking collectives  59.9 us (44%)
  waiting for transfers between devices  37.8 us (28%)
  Pallas kernels  18.7 us (14%)
  starting transfers between devices  15.5 us (11%)
  other arithmetic  1.89 us (1%)
    all_to_all x1, blocking collectives, shards(): lax.all_to_all(sent.reshape(experts, lines, BLOCK), ('attn', 'dev'), spli...  43.6 us
    all_to_all x1, waiting for transfers between devices, shards(): lax.all_to_all(output_rows, ('attn', 'dev'), split_axis=0, concat_axis=0,...  27.9 us
    all_to_all x1, blocking collectives, shards(): lax.all_to_all(attended, 'dev', split_axis=0, concat_axis=0, axis_index_g...  16.4 us
    ppermute x12, waiting for transfers between devices, swap(): lax.ppermute(array, 'dev', [(i, i ^ 2 * jump[way]) for i in range(peers)])  9.89 us
    ppermute x12, starting transfers between devices, swap(): lax.ppermute(array, 'dev', [(i, i ^ 2 * jump[way]) for i in range(peers)])  9.27 us
    pallas_call x1, Pallas kernels, run_expert(): pl.pallas_call(expert_kernel, out_shape=pltpu.HBM(arrived.shape, jnp.bflo...  7.18 us
    all_to_all x1, starting transfers between devices, shards(): lax.all_to_all(output_rows, ('attn', 'dev'), split_axis=0, concat_axis=0,...  4.7 us
    pallas_call x1, Pallas kernels, attend(): pl.pallas_call(attention_kernel, out_shape=[pltpu.HBM(shape, bf16), pltpu...  3.96 us
  transfers between devices with their start and end apart: 14, of which 8 were waited for; matrix products, arithmetic and copies ran while one was open for 2% of the time, Pallas kernels for 2%

profile of v6, /device:TPU:1, one launch (start us, length us, event | category | flops | bytes accessed | tf_op | source)
XLA Modules:
  0.0 134.7 jit_solution(18048427896522549016)
XLA Ops:
  0.1 4.0 %attention.1 = (bf16[16,16,512]{2,1,0:T(8,128)(2,1)}, s32[8,128]{1,0:T(8,128)}) custom-call(s32[4,16]{1,0:T(4,128)} %bitcast.41, s32[16]{0:T(128)} %lengths_far.1, bf16[16,8192]{1,0:T(8,128)(2,1)} %q_far, bf16[16,512]{1,0:T(8,128)(2,1)} %own_key_far.1, bf16[16,512]{1,0:T(8,128)(2,1)} %own_value_far.1, bf16[64,16,512]{2,1,0:T(8,128)(2,1)} %keys_far.1, ...), custom_call_target="tpu_custom_call" | custom-call | flops 600000000 | bytes 5000000 | tf_op jit(solution)/shard_map/attention/pallas_call | solution.py:194
  4.1 1.5 %collective-permute-start = (bf16[256,4096]{1,0:T(8,128)(2,1)S(1)}, bf16[256,4096]{1,0:T(8,128)(2,1)S(1)}, u32[]{:S(2)}, u32[]{:S(2)}) collective-permute-start(bf16[256,4096]{1,0:T(8,128)(2,1)S(1)} %copy-done.1), channel_id=1, source_target_pairs={{0,1},{1,0},{2,3},{3,2},{4,5},{5,4},{6,7},{7,6},{8,9},{9,8},{10,11... | collective-permute-start | bytes 6291464 | tf_op jit(solution)/shard_map/ppermute | solution.py:618
  5.6 16.4 %all_to_all.15.x_ref = bf16[16,16,512]{2,1,0:T(8,128)(2,1)S(1)} all-to-all(bf16[16,16,512]{2,1,0:T(8,128)(2,1)} %get-tuple-element.27), channel_id=1, replica_groups={{0,2,4,6,8,10,12,14,16,18,20,22,24,26,28,30},{1,3,5,7,9,11,13,15,17,19,..., dimensions={0} | all-to-all | bytes 524288 | tf_op jit(solution)/shard_map/all_to_all | solution.py:619
  21.9 1.3 project_sent.1
  23.4 1.1 collective-permute-start.9
  24.5 1.1 collective-permute-start.3
  25.6 1.3 project_kept.1
  26.9 3.1 %collective-permute-done.7 = bf16[8,16,1024]{2,1,0:T(8,128)(2,1)S(1)} collective-permute-done((bf16[8,16,1024]{2,1,0:T(8,128)(2,1)S(1)}, bf16[8,16,1024]{2,1,0:T(8,128)(2,1)S(1)}, u32[]{:S(2)}, u32[]{:S(2)}) %collective-permute-start.7) | collective-permute-done | bytes 262176 | tf_op jit(solution)/shard_map/ppermute | solution.py:540
  30.0 0.7 collective-permute-start.8
  30.7 0.2 collective-permute-done.9
  31.2 0.5 collective-permute-start.2
  31.9 1.2 collective-permute-start.4
  33.1 2.1 %collective-permute-done.8 = bf16[4,16,1024]{2,1,0:T(8,128)(2,1)S(1)} collective-permute-done((bf16[4,16,1024]{2,1,0:T(8,128)(2,1)S(1)}, bf16[4,16,1024]{2,1,0:T(8,128)(2,1)S(1)}, u32[]{:S(2)}, u32[]{:S(2)}) %collective-permute-start.8) | collective-permute-done | bytes 131104 | tf_op jit(solution)/shard_map/ppermute | solution.py:540
  35.3 1.6 %collective-permute-start.11 = (bf16[2,16,2048]{2,1,0:T(8,128)(2,1)S(1)}, bf16[2,16,2048]{2,1,0:T(8,128)(2,1)S(1)}, u32[]{:S(2)}, u32[]{:S(2)}) collective-permute-start(bf16[2,16,2048]{2,1,0:T(8,128)(2,1)S(1)} %pad_maximum_fusion), channel_id=1, source_target_pairs={{0,2},{1,3},{2,0},{3,1},{4,6},{5,7},{6,4},{7,5},{8,10},{9,11},{10,... | collective-permute-start | bytes 393224 | tf_op jit(solution)/shard_map/ppermute | solution.py:540
  37.0 0.9 collective-permute-start.5
  38.0 1.8 %collective-permute-done.11 = bf16[2,16,2048]{2,1,0:T(8,128)(2,1)S(1)} collective-permute-done((bf16[2,16,2048]{2,1,0:T(8,128)(2,1)S(1)}, bf16[2,16,2048]{2,1,0:T(8,128)(2,1)S(1)}, u32[]{:S(2)}, u32[]{:S(2)}) %collective-permute-start.11) | collective-permute-done | bytes 131104 | tf_op jit(solution)/shard_map/ppermute | solution.py:540
  39.8 0.2 collective-permute-start.12
  40.0 1.0 collective-permute-done.5
  41.0 1.7 %collective-permute-start.6 = (bf16[16,2048]{1,0:T(8,128)(2,1)S(1)}, bf16[16,2048]{1,0:T(8,128)(2,1)S(1)}, u32[]{:S(2)}, u32[]{:S(2)}) collective-permute-start(bf16[16,2048]{1,0:T(8,128)(2,1)S(1)} %get-tuple-element.43), channel_id=1, source_target_pairs={{0,24},{1,25},{2,26},{3,27},{4,28},{5,29},{6,30},{7,31},{8,16},{9,... | collective-permute-start | bytes 196616 | tf_op jit(solution)/shard_map/ppermute | solution.py:540
  42.7 0.9 fusion.7.placing
  43.6 0.6 collective-permute-done.12.got_b
  44.2 1.2 collective-permute-done.6.got_a
  45.4 0.9 dispatch.1
  46.3 43.6 %all_to_all.16.arrived = bf16[128,16,512]{2,1,0:T(8,128)(2,1)S(1)} all-to-all(bf16[128,16,512]{2,1,0:T(8,128)(2,1)S(1)} %bitcast.38), channel_id=1, replica_groups=mesh['attn'=4,'dev'=32] {'attn','dev'}, dimensions={0} | all-to-all | bytes 4194304 | tf_op jit(solution)/shard_map/all_to_all | solution.py:631
  89.9 7.2 %expert.1 = bf16[128,16,512]{2,1,0:T(8,128)(2,1)} custom-call(bf16[128,16,512]{2,1,0:T(8,128)(2,1)S(1)} %all_to_all.16.arrived, bf16[1,4096,768]{2,1,0:T(8,128)(2,1)S(1)} %bitcast.35, bf16[1,4096,768]{2,1,0:T(8,128)(2,1)S(1)} %bitcast.37, bf16[1,768,4096]{2,1,0:T(8,128)(2,1)S(1)} %copy-done.2), custom_call_target="tpu_custom_call" | custom-call | flops 5900000256 | bytes 23000000 | tf_op jit(solution)/shard_map/expert/pallas_call | solution.py:434
  97.1 4.7 %all-to-all-start.2 = ((bf16[128,16,512]{2,1,0:T(8,128)(2,1)}), bf16[128,16,512]{2,1,0:T(8,128)(2,1)S(1)}, u32[]{:S(2)}, u32[]{:S(2)}) async-start(bf16[128,16,512]{2,1,0:T(8,128)(2,1)} %expert.1), calls=%async_computation.2 | async-start | bytes 4194304 | tf_op jit(solution)/shard_map/all_to_all | solution.py:639
  101.9 0.2 fusion.10
  102.2 0.2 select_reduce_fusion
  102.4 0.1 exponential_reduce_fusion
  102.6 1.9 %mixing.1.mixing_far = bf16[128,2048]{1,0:T(8,128)(2,1)} custom-call(s32[8,128]{1,0:T(8,128)S(1)} %copy-done.3, f32[16,8]{1,0:T(8,128)S(1)} %exponential_divide_fusion.gates), custom_call_target="tpu_custom_call" | custom-call | flops 6000000 | bytes 600000 | tf_op jit(solution)/shard_map/mixing/pallas_call | solution.py:475
  104.5 27.9 %all-to-all-done.2 = bf16[128,16,512]{2,1,0:T(8,128)(2,1)S(1)} async-done(((bf16[128,16,512]{2,1,0:T(8,128)(2,1)}), bf16[128,16,512]{2,1,0:T(8,128)(2,1)S(1)}, u32[]{:S(2)}, u32[]{:S(2)}) %all-to-all-start.2) | async-done | bytes 2097184 | tf_op jit(solution)/shard_map/all_to_all | solution.py:639
  132.4 2.2 %combine.1 = bf16[16,4096]{1,0:T(8,128)(2,1)} custom-call(bf16[128,2048]{1,0:T(8,128)(2,1)} %mixing.1.mixing_far, bf16[2048,512]{1,0:T(8,128)(2,1)S(1)} %bitcast.33, f32[16,4096]{1,0:T(8,128)} %get-tuple-element.40.hidden_far), custom_call_target="tpu_custom_call" | custom-call | flops 270000000 | bytes 3000000 | tf_op jit(solution)/shard_map/combine/pallas_call | solution.py:507
  (57 shorter events, 1.1 us)
Async XLA Ops:
  0.0 101.9 %copy-start = (bf16[4096,128]{1,0:T(8,128)(2,1)S(1)}, bf16[4096,128]{1,0:T(8,128)(2,1)}, u32[]{:S(2)}) copy-start(bf16[4096,128]{1,0:T(8,128)(2,1)} %param.25) | copy-start | bytes 3145732
  0.0 4.0 %copy-start.1 = (bf16[256,4096]{1,0:T(8,128)(2,1)S(1)}, bf16[256,4096]{1,0:T(8,128)(2,1)}, u32[]{:S(2)}) copy-start(bf16[256,4096]{1,0:T(8,128)(2,1)} %mine.3) | copy-start | bytes 6291460
  4.1 17.9 %collective-permute-start = (bf16[256,4096]{1,0:T(8,128)(2,1)S(1)}, bf16[256,4096]{1,0:T(8,128)(2,1)S(1)}, u32[]{:S(2)}, u32[]{:S(2)}) collective-permute-start(bf16[256,4096]{1,0:T(8,128)(2,1)S(1)} %copy-done.1), channel_id=1, source_target_pairs={{0,1},{1,0},{2,3},{3,2},{4,5},{5,4},{6,7},{7,6},{8,9},{9,8},{10,11... | collective-permute-start | bytes 6291464 | tf_op jit(solution)/shard_map/ppermute | solution.py:618
  21.9 1.4 %copy-start.3 = (s32[8,128]{1,0:T(8,128)S(1)}, s32[8,128]{1,0:T(8,128)}, u32[]{:S(2)}) copy-start(s32[8,128]{1,0:T(8,128)} %get-tuple-element.24.target_ref) | copy-start | bytes 12292
  21.9 68.0 %slice-start.2 = ((s8[6291456]{0:T(1024)(128)(4,1)}), s8[4194304]{0:T(1024)(128)(4,1)S(1)}, s32[]{:S(2)}) async-start(s8[6291456]{0:T(1024)(128)(4,1)} %bitcast.36), calls=%async_computation.5 | async-start | bytes 8388608
  23.2 6.7 %collective-permute-start.7 = (bf16[8,16,1024]{2,1,0:T(8,128)(2,1)S(1)}, bf16[8,16,1024]{2,1,0:T(8,128)(2,1)S(1)}, u32[]{:S(2)}, u32[]{:S(2)}) collective-permute-start(bf16[8,16,1024]{2,1,0:T(8,128)(2,1)S(1)} %get-tuple-element.35), channel_id=1, source_target_pairs={{0,8},{1,9},{2,10},{3,11},{4,12},{5,13},{6,14},{7,15},{8,0},{9,1},... | collective-permute-start | bytes 786440 | tf_op jit(solution)/shard_map/ppermute | solution.py:540
  23.3 7.8 %collective-permute-start.1 = (bf16[8,16,1024]{2,1,0:T(8,128)(2,1)S(1)}, bf16[8,16,1024]{2,1,0:T(8,128)(2,1)S(1)}, u32[]{:S(2)}, u32[]{:S(2)}) collective-permute-start(bf16[8,16,1024]{2,1,0:T(8,128)(2,1)S(1)} %get-tuple-element.29), channel_id=1, source_target_pairs={{0,2},{1,3},{2,0},{3,1},{4,6},{5,7},{6,4},{7,5},{8,10},{9,11},{10,... | collective-permute-start | bytes 786440 | tf_op jit(solution)/shard_map/ppermute | solution.py:540
  23.4 7.5 %collective-permute-start.9 = (bf16[8,16,1024]{2,1,0:T(8,128)(2,1)S(1)}, bf16[8,16,1024]{2,1,0:T(8,128)(2,1)S(1)}, u32[]{:S(2)}, u32[]{:S(2)}) collective-permute-start(bf16[8,16,1024]{2,1,0:T(8,128)(2,1)S(1)} %get-tuple-element.37), channel_id=1, source_target_pairs={{0,24},{1,25},{2,26},{3,27},{4,28},{5,29},{6,30},{7,31},{8,16},{9,... | collective-permute-start | bytes 786440 | tf_op jit(solution)/shard_map/ppermute | solution.py:540
  24.5 7.3 %collective-permute-start.3 = (bf16[8,16,1024]{2,1,0:T(8,128)(2,1)S(1)}, bf16[8,16,1024]{2,1,0:T(8,128)(2,1)S(1)}, u32[]{:S(2)}, u32[]{:S(2)}) collective-permute-start(bf16[8,16,1024]{2,1,0:T(8,128)(2,1)S(1)} %get-tuple-element.33), channel_id=1, source_target_pairs={{0,6},{1,7},{2,4},{3,5},{4,2},{5,3},{6,0},{7,1},{8,14},{9,15},{10,... | collective-permute-start | bytes 786440 | tf_op jit(solution)/shard_map/ppermute | solution.py:540
  25.6 64.3 %slice-start = ((s8[6291456]{0:T(1024)(128)(4,1)}), s8[2097152]{0:T(1024)(128)(4,1)S(1)}, s32[]{:S(2)}) async-start(s8[6291456]{0:T(1024)(128)(4,1)} %bitcast.34), calls=%async_computation.3 | async-start | bytes 4194304
  30.0 5.1 %collective-permute-start.8 = (bf16[4,16,1024]{2,1,0:T(8,128)(2,1)S(1)}, bf16[4,16,1024]{2,1,0:T(8,128)(2,1)S(1)}, u32[]{:S(2)}, u32[]{:S(2)}) collective-permute-start(bf16[4,16,1024]{2,1,0:T(8,128)(2,1)S(1)} %slice.105), channel_id=1, source_target_pairs={{0,24},{1,25},{2,26},{3,27},{4,28},{5,29},{6,30},{7,31},{8,16},{9,... | collective-permute-start | bytes 393224 | tf_op jit(solution)/shard_map/ppermute | solution.py:540
  30.9 59.0 %copy-start.2 = (bf16[1,768,4096]{2,1,0:T(8,128)(2,1)S(1)}, bf16[1,768,4096]{2,1,0:T(8,128)(2,1)}, u32[]{:S(2)}) copy-start(bf16[1,768,4096]{2,1,0:T(8,128)(2,1)} %down.1) | copy-start | bytes 18874372
  31.0 4.2 %collective-permute-start.10 = (bf16[4,16,1024]{2,1,0:T(8,128)(2,1)S(1)}, bf16[4,16,1024]{2,1,0:T(8,128)(2,1)S(1)}, u32[]{:S(2)}, u32[]{:S(2)}) collective-permute-start(bf16[4,16,1024]{2,1,0:T(8,128)(2,1)S(1)} %slice.107), channel_id=1, source_target_pairs={{0,8},{1,9},{2,10},{3,11},{4,12},{5,13},{6,14},{7,15},{8,0},{9,1},... | collective-permute-start | bytes 393224 | tf_op jit(solution)/shard_map/ppermute | solution.py:540
  31.1 14.3 %copy-start.4 = (bf16[16,4096]{1,0:T(8,128)(2,1)S(1)}, bf16[16,4096]{1,0:T(8,128)(2,1)}, u32[]{:S(2)}) copy-start(bf16[16,4096]{1,0:T(8,128)(2,1)} %residual.1) | copy-start | bytes 393220
  31.1 14.3 %copy-start.5 = (f32[4096]{0:T(1024)S(1)}, f32[4096]{0:T(1024)}, u32[]{:S(2)}) copy-start(f32[4096]{0:T(1024)} %param.24) | copy-start | bytes 49156
  31.1 58.8 %slice-start.3 = ((s8[6291456]{0:T(1024)(128)(4,1)}), s8[2097152]{0:T(1024)(128)(4,1)S(1)}, s32[]{:S(2)}) async-start(s8[6291456]{0:T(1024)(128)(4,1)} %bitcast.36), calls=%async_computation.6 | async-start | bytes 4194304
  31.2 5.7 %collective-permute-start.2 = (bf16[4,16,1024]{2,1,0:T(8,128)(2,1)S(1)}, bf16[4,16,1024]{2,1,0:T(8,128)(2,1)S(1)}, u32[]{:S(2)}, u32[]{:S(2)}) collective-permute-start(bf16[4,16,1024]{2,1,0:T(8,128)(2,1)S(1)} %slice.97), channel_id=1, source_target_pairs={{0,6},{1,7},{2,4},{3,5},{4,2},{5,3},{6,0},{7,1},{8,14},{9,15},{10,... | collective-permute-start | bytes 393224 | tf_op jit(solution)/shard_map/ppermute | solution.py:540
  31.9 5.1 %collective-permute-start.4 = (bf16[4,16,1024]{2,1,0:T(8,128)(2,1)S(1)}, bf16[4,16,1024]{2,1,0:T(8,128)(2,1)S(1)}, u32[]{:S(2)}, u32[]{:S(2)}) collective-permute-start(bf16[4,16,1024]{2,1,0:T(8,128)(2,1)S(1)} %slice.99), channel_id=1, source_target_pairs={{0,2},{1,3},{2,0},{3,1},{4,6},{5,7},{6,4},{7,5},{8,10},{9,11},{10,... | collective-permute-start | bytes 393224 | tf_op jit(solution)/shard_map/ppermute | solution.py:540
  35.2 54.7 %slice-start.1 = ((s8[6291456]{0:T(1024)(128)(4,1)}), s8[4194304]{0:T(1024)(128)(4,1)S(1)}, s32[]{:S(2)}) async-start(s8[6291456]{0:T(1024)(128)(4,1)} %bitcast.34), calls=%async_computation.4 | async-start | bytes 8388608
  35.3 4.5 %collective-permute-start.11 = (bf16[2,16,2048]{2,1,0:T(8,128)(2,1)S(1)}, bf16[2,16,2048]{2,1,0:T(8,128)(2,1)S(1)}, u32[]{:S(2)}, u32[]{:S(2)}) collective-permute-start(bf16[2,16,2048]{2,1,0:T(8,128)(2,1)S(1)} %pad_maximum_fusion), channel_id=1, source_target_pairs={{0,2},{1,3},{2,0},{3,1},{4,6},{5,7},{6,4},{7,5},{8,10},{9,11},{10,... | collective-permute-start | bytes 393224 | tf_op jit(solution)/shard_map/ppermute | solution.py:540
  37.0 3.9 %collective-permute-start.5 = (bf16[2,16,2048]{2,1,0:T(8,128)(2,1)S(1)}, bf16[2,16,2048]{2,1,0:T(8,128)(2,1)S(1)}, u32[]{:S(2)}, u32[]{:S(2)}) collective-permute-start(bf16[2,16,2048]{2,1,0:T(8,128)(2,1)S(1)} %pad_maximum_fusion.1), channel_id=1, source_target_pairs={{0,8},{1,9},{2,10},{3,11},{4,12},{5,13},{6,14},{7,15},{8,0},{9,1},... | collective-permute-start | bytes 393224 | tf_op jit(solution)/shard_map/ppermute | solution.py:540
  39.8 4.4 %collective-permute-start.12 = (bf16[16,2048]{1,0:T(8,128)(2,1)S(1)}, bf16[16,2048]{1,0:T(8,128)(2,1)S(1)}, u32[]{:S(2)}, u32[]{:S(2)}) collective-permute-start(bf16[16,2048]{1,0:T(8,128)(2,1)S(1)} %get-tuple-element.41), channel_id=1, source_target_pairs={{0,6},{1,7},{2,4},{3,5},{4,2},{5,3},{6,0},{7,1},{8,14},{9,15},{10,... | collective-permute-start | bytes 196616 | tf_op jit(solution)/shard_map/ppermute | solution.py:540
  41.0 4.4 %collective-permute-start.6 = (bf16[16,2048]{1,0:T(8,128)(2,1)S(1)}, bf16[16,2048]{1,0:T(8,128)(2,1)S(1)}, u32[]{:S(2)}, u32[]{:S(2)}) collective-permute-start(bf16[16,2048]{1,0:T(8,128)(2,1)S(1)} %get-tuple-element.43), channel_id=1, source_target_pairs={{0,24},{1,25},{2,26},{3,27},{4,28},{5,29},{6,30},{7,31},{8,16},{9,... | collective-permute-start | bytes 196616 | tf_op jit(solution)/shard_map/ppermute | solution.py:540
  97.1 4.7 %copy-start.7 = (s32[16,8]{0,1:T(8,128)S(1)}, s32[16,8]{0,1:T(8,128)}, u32[]{:S(2)}) copy-start(s32[16,8]{0,1:T(8,128)} %param.26) | copy-start | bytes 1540
  97.1 4.8 %copy-start.6 = (bf16[16,4096]{1,0:T(8,128)(2,1)S(1)}, bf16[16,4096]{1,0:T(8,128)(2,1)}, u32[]{:S(2)}) copy-start(bf16[16,4096]{1,0:T(8,128)(2,1)} %get-tuple-element.38) | copy-start | bytes 393220
  97.1 35.2 %all-to-all-start.2 = ((bf16[128,16,512]{2,1,0:T(8,128)(2,1)}), bf16[128,16,512]{2,1,0:T(8,128)(2,1)S(1)}, u32[]{:S(2)}, u32[]{:S(2)}) async-start(bf16[128,16,512]{2,1,0:T(8,128)(2,1)} %expert.1), calls=%async_computation.2 | async-start | bytes 4194304 | tf_op jit(solution)/shard_map/all_to_all | solution.py:639

commit v7 on v6

--- a/solution.py
+++ b/solution.py
@@ -79,23 +79,6 @@
     ]
     for copy in inward[:3] + inward[5:]:
         copy.start()
-    inward[7].wait()
-    inward[8].wait()
-    chosen = routes_near[...]
-    column = lax.broadcasted_iota(jnp.int32, chosen.shape, 1)
-    rank = jnp.zeros_like(chosen)
-    for t in range(rows - 1):
-        named = jnp.zeros_like(chosen)
-        for k in range(routes.shape[0]):
-            named = jnp.where(chosen == routes[k, t], 1, named)
-        rank = rank + jnp.where(column > t, named, 0)
-    blocks = target.shape[1] // rows
-    first_line = chosen * (blocks * CAPACITY) + rank
-    target[...] = jnp.concatenate(
-        [first_line + block * CAPACITY for block in range(blocks)], axis=1
-    )
-    target_copy = pltpu.make_async_copy(target, target_far, sems.at[9])
-    target_copy.start()
     inward[0].wait()
     for head in range(HEADS):
         q_turned[head // GROUP, pl.ds(head % GROUP * rows, rows), :] = q_near[
@@ -150,6 +133,23 @@
         )
         weights_held[at, :] = (weights * share).astype(jnp.bfloat16)
         own_weights_held[at, :] = (own_weights * share).astype(jnp.bfloat16)
+    inward[7].wait()
+    inward[8].wait()
+    chosen = routes_near[...]
+    column = lax.broadcasted_iota(jnp.int32, chosen.shape, 1)
+    rank = jnp.zeros_like(chosen)
+    for t in range(rows - 1):
+        named = jnp.zeros_like(chosen)
+        for k in range(routes.shape[0]):
+            named = jnp.where(chosen == routes[k, t], 1, named)
+        rank = rank + jnp.where(column > t, named, 0)
+    blocks = target.shape[1] // rows
+    first_line = chosen * (blocks * CAPACITY) + rank
+    target[...] = jnp.concatenate(
+        [first_line + block * CAPACITY for block in range(blocks)], axis=1
+    )
+    target_copy = pltpu.make_async_copy(target, target_far, sems.at[9])
+    target_copy.start()
     inward[3].wait()
     inward[4].wait()
     outward = []
@@ -619,7 +619,7 @@
     regrouped = lax.all_to_all(
         attended, "dev", split_axis=0, concat_axis=0, axis_index_groups=same_core, tiled=True
     )
-    ends = scatter_sum(regrouped, out_weight, weight_beside, spot, peers)
+    ends = scatter_sum(regrouped, weight_sent, weight_beside, spot, peers)
 
     line = jnp.arange(experts * lines, dtype=jnp.int32)
     placed = line[:, None] == target[0][None, :]

time: 135 us -> 135 us (level)
  no operation moved by 1% of the time
where the time goes in v7:
time: 135 us
  blocking collectives  59.9 us (44%)
  waiting for transfers between devices  37.8 us (28%)
  Pallas kernels  18.7 us (14%)
  starting transfers between devices  15.5 us (11%)
  other arithmetic  1.89 us (1%)
    all_to_all x1, blocking collectives, shards(): lax.all_to_all(sent.reshape(experts, lines, BLOCK), ('attn', 'dev'), spli...  43.6 us
    all_to_all x1, waiting for transfers between devices, shards(): lax.all_to_all(output_rows, ('attn', 'dev'), split_axis=0, concat_axis=0,...  27.9 us
    all_to_all x1, blocking collectives, shards(): lax.all_to_all(attended, 'dev', split_axis=0, concat_axis=0, axis_index_g...  16.4 us
    ppermute x12, waiting for transfers between devices, swap(): lax.ppermute(array, 'dev', [(i, i ^ 2 * jump[way]) for i in range(peers)])  9.88 us
    ppermute x12, starting transfers between devices, swap(): lax.ppermute(array, 'dev', [(i, i ^ 2 * jump[way]) for i in range(peers)])  9.28 us
    pallas_call x1, Pallas kernels, run_expert(): pl.pallas_call(expert_kernel, out_shape=pltpu.HBM(arrived.shape, jnp.bflo...  7.18 us
    all_to_all x1, starting transfers between devices, shards(): lax.all_to_all(output_rows, ('attn', 'dev'), split_axis=0, concat_axis=0,...  4.7 us
    pallas_call x1, Pallas kernels, attend(): pl.pallas_call(attention_kernel, out_shape=[pltpu.HBM(shape, bf16), pltpu...  3.95 us
  transfers between devices with their start and end apart: 14, of which 8 were waited for; matrix products, arithmetic and copies ran while one was open for 2% of the time, Pallas kernels for 2%

profile of v7, /device:TPU:1, one launch (start us, length us, event | category | flops | bytes accessed | tf_op | source)
XLA Modules:
  0.0 134.7 jit_solution(5562499849518732098)
XLA Ops:
  0.1 3.9 %attention.1 = (bf16[16,16,512]{2,1,0:T(8,128)(2,1)}, s32[8,128]{1,0:T(8,128)}) custom-call(s32[4,16]{1,0:T(4,128)} %bitcast.41, s32[16]{0:T(128)} %lengths_far.1, bf16[16,8192]{1,0:T(8,128)(2,1)} %q_far, bf16[16,512]{1,0:T(8,128)(2,1)} %own_key_far.1, bf16[16,512]{1,0:T(8,128)(2,1)} %own_value_far.1, bf16[64,16,512]{2,1,0:T(8,128)(2,1)} %keys_far.1, ...), custom_call_target="tpu_custom_call" | custom-call | flops 600000000 | bytes 5000000 | tf_op jit(solution)/shard_map/attention/pallas_call | solution.py:194
  4.0 1.5 %collective-permute-start = (bf16[256,4096]{1,0:T(8,128)(2,1)S(1)}, bf16[256,4096]{1,0:T(8,128)(2,1)S(1)}, u32[]{:S(2)}, u32[]{:S(2)}) collective-permute-start(bf16[256,4096]{1,0:T(8,128)(2,1)S(1)} %copy-done.1), channel_id=1, source_target_pairs={{0,1},{1,0},{2,3},{3,2},{4,5},{5,4},{6,7},{7,6},{8,9},{9,8},{10,11... | collective-permute-start | bytes 6291464 | tf_op jit(solution)/shard_map/ppermute | solution.py:618
  5.5 16.4 %all_to_all.15.x_ref = bf16[16,16,512]{2,1,0:T(8,128)(2,1)S(1)} all-to-all(bf16[16,16,512]{2,1,0:T(8,128)(2,1)} %get-tuple-element.27), channel_id=1, replica_groups={{0,2,4,6,8,10,12,14,16,18,20,22,24,26,28,30},{1,3,5,7,9,11,13,15,17,19,..., dimensions={0} | all-to-all | bytes 524288 | tf_op jit(solution)/shard_map/all_to_all | solution.py:619
  21.9 1.3 project_sent.1
  23.4 1.1 collective-permute-start.9
  24.5 1.1 collective-permute-start.3
  25.6 1.3 project_kept.1
  26.9 3.1 %collective-permute-done.7 = bf16[8,16,1024]{2,1,0:T(8,128)(2,1)S(1)} collective-permute-done((bf16[8,16,1024]{2,1,0:T(8,128)(2,1)S(1)}, bf16[8,16,1024]{2,1,0:T(8,128)(2,1)S(1)}, u32[]{:S(2)}, u32[]{:S(2)}) %collective-permute-start.7) | collective-permute-done | bytes 262176 | tf_op jit(solution)/shard_map/ppermute | solution.py:540
  30.0 0.7 collective-permute-start.8
  30.7 0.2 collective-permute-done.9
  31.2 0.5 collective-permute-start.2
  31.9 1.2 collective-permute-start.4
  33.1 2.1 %collective-permute-done.8 = bf16[4,16,1024]{2,1,0:T(8,128)(2,1)S(1)} collective-permute-done((bf16[4,16,1024]{2,1,0:T(8,128)(2,1)S(1)}, bf16[4,16,1024]{2,1,0:T(8,128)(2,1)S(1)}, u32[]{:S(2)}, u32[]{:S(2)}) %collective-permute-start.8) | collective-permute-done | bytes 131104 | tf_op jit(solution)/shard_map/ppermute | solution.py:540
  35.3 1.6 %collective-permute-start.11 = (bf16[2,16,2048]{2,1,0:T(8,128)(2,1)S(1)}, bf16[2,16,2048]{2,1,0:T(8,128)(2,1)S(1)}, u32[]{:S(2)}, u32[]{:S(2)}) collective-permute-start(bf16[2,16,2048]{2,1,0:T(8,128)(2,1)S(1)} %pad_maximum_fusion), channel_id=1, source_target_pairs={{0,2},{1,3},{2,0},{3,1},{4,6},{5,7},{6,4},{7,5},{8,10},{9,11},{10,... | collective-permute-start | bytes 393224 | tf_op jit(solution)/shard_map/ppermute | solution.py:540
  37.0 0.9 collective-permute-start.5
  37.9 1.8 %collective-permute-done.11 = bf16[2,16,2048]{2,1,0:T(8,128)(2,1)S(1)} collective-permute-done((bf16[2,16,2048]{2,1,0:T(8,128)(2,1)S(1)}, bf16[2,16,2048]{2,1,0:T(8,128)(2,1)S(1)}, u32[]{:S(2)}, u32[]{:S(2)}) %collective-permute-start.11) | collective-permute-done | bytes 131104 | tf_op jit(solution)/shard_map/ppermute | solution.py:540
  39.8 0.2 collective-permute-start.12
  40.0 1.0 collective-permute-done.5
  41.0 1.7 %collective-permute-start.6 = (bf16[16,2048]{1,0:T(8,128)(2,1)S(1)}, bf16[16,2048]{1,0:T(8,128)(2,1)S(1)}, u32[]{:S(2)}, u32[]{:S(2)}) collective-permute-start(bf16[16,2048]{1,0:T(8,128)(2,1)S(1)} %get-tuple-element.43), channel_id=1, source_target_pairs={{0,24},{1,25},{2,26},{3,27},{4,28},{5,29},{6,30},{7,31},{8,16},{9,... | collective-permute-start | bytes 196616 | tf_op jit(solution)/shard_map/ppermute | solution.py:540
  42.7 0.9 fusion.7.placing
  43.6 0.6 collective-permute-done.12.got_b
  44.2 1.2 collective-permute-done.6.got_a
  45.4 0.9 dispatch.1
  46.3 43.6 %all_to_all.16.arrived = bf16[128,16,512]{2,1,0:T(8,128)(2,1)S(1)} all-to-all(bf16[128,16,512]{2,1,0:T(8,128)(2,1)S(1)} %bitcast.38), channel_id=1, replica_groups=mesh['attn'=4,'dev'=32] {'attn','dev'}, dimensions={0} | all-to-all | bytes 4194304 | tf_op jit(solution)/shard_map/all_to_all | solution.py:631
  89.9 7.2 %expert.1 = bf16[128,16,512]{2,1,0:T(8,128)(2,1)} custom-call(bf16[128,16,512]{2,1,0:T(8,128)(2,1)S(1)} %all_to_all.16.arrived, bf16[1,4096,768]{2,1,0:T(8,128)(2,1)S(1)} %bitcast.35, bf16[1,4096,768]{2,1,0:T(8,128)(2,1)S(1)} %bitcast.37, bf16[1,768,4096]{2,1,0:T(8,128)(2,1)S(1)} %copy-done.2), custom_call_target="tpu_custom_call" | custom-call | flops 5900000256 | bytes 23000000 | tf_op jit(solution)/shard_map/expert/pallas_call | solution.py:434
  97.1 4.7 %all-to-all-start.2 = ((bf16[128,16,512]{2,1,0:T(8,128)(2,1)}), bf16[128,16,512]{2,1,0:T(8,128)(2,1)S(1)}, u32[]{:S(2)}, u32[]{:S(2)}) async-start(bf16[128,16,512]{2,1,0:T(8,128)(2,1)} %expert.1), calls=%async_computation.2 | async-start | bytes 4194304 | tf_op jit(solution)/shard_map/all_to_all | solution.py:639
  101.9 0.2 fusion.10
  102.2 0.2 select_reduce_fusion
  102.4 0.1 exponential_reduce_fusion
  102.6 1.9 %mixing.1.mixing_far = bf16[128,2048]{1,0:T(8,128)(2,1)} custom-call(s32[8,128]{1,0:T(8,128)S(1)} %copy-done.3, f32[16,8]{1,0:T(8,128)S(1)} %exponential_divide_fusion.gates), custom_call_target="tpu_custom_call" | custom-call | flops 6000000 | bytes 600000 | tf_op jit(solution)/shard_map/mixing/pallas_call | solution.py:475
  104.5 27.9 %all-to-all-done.2 = bf16[128,16,512]{2,1,0:T(8,128)(2,1)S(1)} async-done(((bf16[128,16,512]{2,1,0:T(8,128)(2,1)}), bf16[128,16,512]{2,1,0:T(8,128)(2,1)S(1)}, u32[]{:S(2)}, u32[]{:S(2)}) %all-to-all-start.2) | async-done | bytes 2097184 | tf_op jit(solution)/shard_map/all_to_all | solution.py:639
  132.4 2.2 %combine.1 = bf16[16,4096]{1,0:T(8,128)(2,1)} custom-call(bf16[128,2048]{1,0:T(8,128)(2,1)} %mixing.1.mixing_far, bf16[2048,512]{1,0:T(8,128)(2,1)S(1)} %bitcast.33, f32[16,4096]{1,0:T(8,128)} %get-tuple-element.40.hidden_far), custom_call_target="tpu_custom_call" | custom-call | flops 270000000 | bytes 3000000 | tf_op jit(solution)/shard_map/combine/pallas_call | solution.py:507
  (57 shorter events, 1.1 us)
Async XLA Ops:
  0.0 101.9 %copy-start = (bf16[4096,128]{1,0:T(8,128)(2,1)S(1)}, bf16[4096,128]{1,0:T(8,128)(2,1)}, u32[]{:S(2)}) copy-start(bf16[4096,128]{1,0:T(8,128)(2,1)} %param.25) | copy-start | bytes 3145732
  0.0 4.0 %copy-start.1 = (bf16[256,4096]{1,0:T(8,128)(2,1)S(1)}, bf16[256,4096]{1,0:T(8,128)(2,1)}, u32[]{:S(2)}) copy-start(bf16[256,4096]{1,0:T(8,128)(2,1)} %mine.1) | copy-start | bytes 6291460
  4.0 17.9 %collective-permute-start = (bf16[256,4096]{1,0:T(8,128)(2,1)S(1)}, bf16[256,4096]{1,0:T(8,128)(2,1)S(1)}, u32[]{:S(2)}, u32[]{:S(2)}) collective-permute-start(bf16[256,4096]{1,0:T(8,128)(2,1)S(1)} %copy-done.1), channel_id=1, source_target_pairs={{0,1},{1,0},{2,3},{3,2},{4,5},{5,4},{6,7},{7,6},{8,9},{9,8},{10,11... | collective-permute-start | bytes 6291464 | tf_op jit(solution)/shard_map/ppermute | solution.py:618
  21.9 1.4 %copy-start.3 = (s32[8,128]{1,0:T(8,128)S(1)}, s32[8,128]{1,0:T(8,128)}, u32[]{:S(2)}) copy-start(s32[8,128]{1,0:T(8,128)} %get-tuple-element.24.target_ref) | copy-start | bytes 12292
  21.9 68.0 %slice-start.2 = ((s8[6291456]{0:T(1024)(128)(4,1)}), s8[4194304]{0:T(1024)(128)(4,1)S(1)}, s32[]{:S(2)}) async-start(s8[6291456]{0:T(1024)(128)(4,1)} %bitcast.36), calls=%async_computation.5 | async-start | bytes 8388608
  23.2 6.7 %collective-permute-start.7 = (bf16[8,16,1024]{2,1,0:T(8,128)(2,1)S(1)}, bf16[8,16,1024]{2,1,0:T(8,128)(2,1)S(1)}, u32[]{:S(2)}, u32[]{:S(2)}) collective-permute-start(bf16[8,16,1024]{2,1,0:T(8,128)(2,1)S(1)} %get-tuple-element.35), channel_id=1, source_target_pairs={{0,8},{1,9},{2,10},{3,11},{4,12},{5,13},{6,14},{7,15},{8,0},{9,1},... | collective-permute-start | bytes 786440 | tf_op jit(solution)/shard_map/ppermute | solution.py:540
  23.3 7.8 %collective-permute-start.1 = (bf16[8,16,1024]{2,1,0:T(8,128)(2,1)S(1)}, bf16[8,16,1024]{2,1,0:T(8,128)(2,1)S(1)}, u32[]{:S(2)}, u32[]{:S(2)}) collective-permute-start(bf16[8,16,1024]{2,1,0:T(8,128)(2,1)S(1)} %get-tuple-element.29), channel_id=1, source_target_pairs={{0,2},{1,3},{2,0},{3,1},{4,6},{5,7},{6,4},{7,5},{8,10},{9,11},{10,... | collective-permute-start | bytes 786440 | tf_op jit(solution)/shard_map/ppermute | solution.py:540
  23.4 7.5 %collective-permute-start.9 = (bf16[8,16,1024]{2,1,0:T(8,128)(2,1)S(1)}, bf16[8,16,1024]{2,1,0:T(8,128)(2,1)S(1)}, u32[]{:S(2)}, u32[]{:S(2)}) collective-permute-start(bf16[8,16,1024]{2,1,0:T(8,128)(2,1)S(1)} %get-tuple-element.37), channel_id=1, source_target_pairs={{0,24},{1,25},{2,26},{3,27},{4,28},{5,29},{6,30},{7,31},{8,16},{9,... | collective-permute-start | bytes 786440 | tf_op jit(solution)/shard_map/ppermute | solution.py:540
  24.5 7.3 %collective-permute-start.3 = (bf16[8,16,1024]{2,1,0:T(8,128)(2,1)S(1)}, bf16[8,16,1024]{2,1,0:T(8,128)(2,1)S(1)}, u32[]{:S(2)}, u32[]{:S(2)}) collective-permute-start(bf16[8,16,1024]{2,1,0:T(8,128)(2,1)S(1)} %get-tuple-element.33), channel_id=1, source_target_pairs={{0,6},{1,7},{2,4},{3,5},{4,2},{5,3},{6,0},{7,1},{8,14},{9,15},{10,... | collective-permute-start | bytes 786440 | tf_op jit(solution)/shard_map/ppermute | solution.py:540
  25.6 64.3 %slice-start = ((s8[6291456]{0:T(1024)(128)(4,1)}), s8[2097152]{0:T(1024)(128)(4,1)S(1)}, s32[]{:S(2)}) async-start(s8[6291456]{0:T(1024)(128)(4,1)} %bitcast.34), calls=%async_computation.3 | async-start | bytes 4194304
  30.0 5.1 %collective-permute-start.8 = (bf16[4,16,1024]{2,1,0:T(8,128)(2,1)S(1)}, bf16[4,16,1024]{2,1,0:T(8,128)(2,1)S(1)}, u32[]{:S(2)}, u32[]{:S(2)}) collective-permute-start(bf16[4,16,1024]{2,1,0:T(8,128)(2,1)S(1)} %slice.105), channel_id=1, source_target_pairs={{0,24},{1,25},{2,26},{3,27},{4,28},{5,29},{6,30},{7,31},{8,16},{9,... | collective-permute-start | bytes 393224 | tf_op jit(solution)/shard_map/ppermute | solution.py:540
  30.9 59.0 %copy-start.2 = (bf16[1,768,4096]{2,1,0:T(8,128)(2,1)S(1)}, bf16[1,768,4096]{2,1,0:T(8,128)(2,1)}, u32[]{:S(2)}) copy-start(bf16[1,768,4096]{2,1,0:T(8,128)(2,1)} %down.1) | copy-start | bytes 18874372
  31.0 4.2 %collective-permute-start.10 = (bf16[4,16,1024]{2,1,0:T(8,128)(2,1)S(1)}, bf16[4,16,1024]{2,1,0:T(8,128)(2,1)S(1)}, u32[]{:S(2)}, u32[]{:S(2)}) collective-permute-start(bf16[4,16,1024]{2,1,0:T(8,128)(2,1)S(1)} %slice.107), channel_id=1, source_target_pairs={{0,8},{1,9},{2,10},{3,11},{4,12},{5,13},{6,14},{7,15},{8,0},{9,1},... | collective-permute-start | bytes 393224 | tf_op jit(solution)/shard_map/ppermute | solution.py:540
  31.1 14.3 %copy-start.4 = (bf16[16,4096]{1,0:T(8,128)(2,1)S(1)}, bf16[16,4096]{1,0:T(8,128)(2,1)}, u32[]{:S(2)}) copy-start(bf16[16,4096]{1,0:T(8,128)(2,1)} %residual.1) | copy-start | bytes 393220
  31.1 14.3 %copy-start.5 = (f32[4096]{0:T(1024)S(1)}, f32[4096]{0:T(1024)}, u32[]{:S(2)}) copy-start(f32[4096]{0:T(1024)} %param.24) | copy-start | bytes 49156
  31.1 58.8 %slice-start.3 = ((s8[6291456]{0:T(1024)(128)(4,1)}), s8[2097152]{0:T(1024)(128)(4,1)S(1)}, s32[]{:S(2)}) async-start(s8[6291456]{0:T(1024)(128)(4,1)} %bitcast.36), calls=%async_computation.6 | async-start | bytes 4194304
  31.2 5.7 %collective-permute-start.2 = (bf16[4,16,1024]{2,1,0:T(8,128)(2,1)S(1)}, bf16[4,16,1024]{2,1,0:T(8,128)(2,1)S(1)}, u32[]{:S(2)}, u32[]{:S(2)}) collective-permute-start(bf16[4,16,1024]{2,1,0:T(8,128)(2,1)S(1)} %slice.97), channel_id=1, source_target_pairs={{0,6},{1,7},{2,4},{3,5},{4,2},{5,3},{6,0},{7,1},{8,14},{9,15},{10,... | collective-permute-start | bytes 393224 | tf_op jit(solution)/shard_map/ppermute | solution.py:540
  31.9 5.1 %collective-permute-start.4 = (bf16[4,16,1024]{2,1,0:T(8,128)(2,1)S(1)}, bf16[4,16,1024]{2,1,0:T(8,128)(2,1)S(1)}, u32[]{:S(2)}, u32[]{:S(2)}) collective-permute-start(bf16[4,16,1024]{2,1,0:T(8,128)(2,1)S(1)} %slice.99), channel_id=1, source_target_pairs={{0,2},{1,3},{2,0},{3,1},{4,6},{5,7},{6,4},{7,5},{8,10},{9,11},{10,... | collective-permute-start | bytes 393224 | tf_op jit(solution)/shard_map/ppermute | solution.py:540
  35.2 54.7 %slice-start.1 = ((s8[6291456]{0:T(1024)(128)(4,1)}), s8[4194304]{0:T(1024)(128)(4,1)S(1)}, s32[]{:S(2)}) async-start(s8[6291456]{0:T(1024)(128)(4,1)} %bitcast.34), calls=%async_computation.4 | async-start | bytes 8388608
  35.3 4.5 %collective-permute-start.11 = (bf16[2,16,2048]{2,1,0:T(8,128)(2,1)S(1)}, bf16[2,16,2048]{2,1,0:T(8,128)(2,1)S(1)}, u32[]{:S(2)}, u32[]{:S(2)}) collective-permute-start(bf16[2,16,2048]{2,1,0:T(8,128)(2,1)S(1)} %pad_maximum_fusion), channel_id=1, source_target_pairs={{0,2},{1,3},{2,0},{3,1},{4,6},{5,7},{6,4},{7,5},{8,10},{9,11},{10,... | collective-permute-start | bytes 393224 | tf_op jit(solution)/shard_map/ppermute | solution.py:540
  37.0 3.9 %collective-permute-start.5 = (bf16[2,16,2048]{2,1,0:T(8,128)(2,1)S(1)}, bf16[2,16,2048]{2,1,0:T(8,128)(2,1)S(1)}, u32[]{:S(2)}, u32[]{:S(2)}) collective-permute-start(bf16[2,16,2048]{2,1,0:T(8,128)(2,1)S(1)} %pad_maximum_fusion.1), channel_id=1, source_target_pairs={{0,8},{1,9},{2,10},{3,11},{4,12},{5,13},{6,14},{7,15},{8,0},{9,1},... | collective-permute-start | bytes 393224 | tf_op jit(solution)/shard_map/ppermute | solution.py:540
  39.8 4.4 %collective-permute-start.12 = (bf16[16,2048]{1,0:T(8,128)(2,1)S(1)}, bf16[16,2048]{1,0:T(8,128)(2,1)S(1)}, u32[]{:S(2)}, u32[]{:S(2)}) collective-permute-start(bf16[16,2048]{1,0:T(8,128)(2,1)S(1)} %get-tuple-element.41), channel_id=1, source_target_pairs={{0,6},{1,7},{2,4},{3,5},{4,2},{5,3},{6,0},{7,1},{8,14},{9,15},{10,... | collective-permute-start | bytes 196616 | tf_op jit(solution)/shard_map/ppermute | solution.py:540
  41.0 4.4 %collective-permute-start.6 = (bf16[16,2048]{1,0:T(8,128)(2,1)S(1)}, bf16[16,2048]{1,0:T(8,128)(2,1)S(1)}, u32[]{:S(2)}, u32[]{:S(2)}) collective-permute-start(bf16[16,2048]{1,0:T(8,128)(2,1)S(1)} %get-tuple-element.43), channel_id=1, source_target_pairs={{0,24},{1,25},{2,26},{3,27},{4,28},{5,29},{6,30},{7,31},{8,16},{9,... | collective-permute-start | bytes 196616 | tf_op jit(solution)/shard_map/ppermute | solution.py:540
  97.1 4.7 %copy-start.7 = (s32[16,8]{0,1:T(8,128)S(1)}, s32[16,8]{0,1:T(8,128)}, u32[]{:S(2)}) copy-start(s32[16,8]{0,1:T(8,128)} %param.26) | copy-start | bytes 1540
  97.1 4.8 %copy-start.6 = (bf16[16,4096]{1,0:T(8,128)(2,1)S(1)}, bf16[16,4096]{1,0:T(8,128)(2,1)}, u32[]{:S(2)}) copy-start(bf16[16,4096]{1,0:T(8,128)(2,1)} %get-tuple-element.38) | copy-start | bytes 393220
  97.1 35.2 %all-to-all-start.2 = ((bf16[128,16,512]{2,1,0:T(8,128)(2,1)}), bf16[128,16,512]{2,1,0:T(8,128)(2,1)S(1)}, u32[]{:S(2)}, u32[]{:S(2)}) async-start(bf16[128,16,512]{2,1,0:T(8,128)(2,1)} %expert.1), calls=%async_computation.2 | async-start | bytes 4194304 | tf_op jit(solution)/shard_map/all_to_all | solution.py:639

commit v8 on v6

--- a/solution.py
+++ b/solution.py
@@ -18,7 +18,7 @@
 BLOCK = 512
 ROWS = 32
 CAPACITY = 2
-TOGETHER = 4
+TOGETHER = 2
 CONTRACT_LAST = (((1,), (1,)), ((), ()))
 VMEM = pl.BlockSpec(memory_space=pltpu.VMEM)
 SMEM = pl.BlockSpec(memory_space=pltpu.SMEM)

time: 135 us -> 135 us (level)
  no operation moved by 1% of the time
where the time goes in v8:
time: 135 us
  blocking collectives  59.9 us (44%)
  waiting for transfers between devices  37.8 us (28%)
  Pallas kernels  18.6 us (14%)
  starting transfers between devices  15.5 us (11%)
  other arithmetic  1.89 us (1%)
    all_to_all x1, blocking collectives, shards(): lax.all_to_all(sent.reshape(experts, lines, BLOCK), ('attn', 'dev'), spli...  43.6 us
    all_to_all x1, waiting for transfers between devices, shards(): lax.all_to_all(output_rows, ('attn', 'dev'), split_axis=0, concat_axis=0,...  27.9 us
    all_to_all x1, blocking collectives, shards(): lax.all_to_all(attended, 'dev', split_axis=0, concat_axis=0, axis_index_g...  16.3 us
    ppermute x12, waiting for transfers between devices, swap(): lax.ppermute(array, 'dev', [(i, i ^ 2 * jump[way]) for i in range(peers)])  9.86 us
    ppermute x12, starting transfers between devices, swap(): lax.ppermute(array, 'dev', [(i, i ^ 2 * jump[way]) for i in range(peers)])  9.3 us
    pallas_call x1, Pallas kernels, run_expert(): pl.pallas_call(expert_kernel, out_shape=pltpu.HBM(arrived.shape, jnp.bflo...  7.18 us
    all_to_all x1, starting transfers between devices, shards(): lax.all_to_all(output_rows, ('attn', 'dev'), split_axis=0, concat_axis=0,...  4.7 us
    pallas_call x1, Pallas kernels, attend(): pl.pallas_call(attention_kernel, out_shape=[pltpu.HBM(shape, bf16), pltpu...  3.93 us
  transfers between devices with their start and end apart: 14, of which 8 were waited for; matrix products, arithmetic and copies ran while one was open for 2% of the time, Pallas kernels for 2%

profile of v8, /device:TPU:1, one launch (start us, length us, event | category | flops | bytes accessed | tf_op | source)
XLA Modules:
  0.0 134.7 jit_solution(1885904016434213807)
XLA Ops:
  0.1 3.9 %attention.1 = (bf16[16,16,512]{2,1,0:T(8,128)(2,1)}, s32[8,128]{1,0:T(8,128)}) custom-call(s32[4,16]{1,0:T(4,128)} %bitcast.41, s32[16]{0:T(128)} %lengths_far.1, bf16[16,8192]{1,0:T(8,128)(2,1)} %q_far, bf16[16,512]{1,0:T(8,128)(2,1)} %own_key_far.1, bf16[16,512]{1,0:T(8,128)(2,1)} %own_value_far.1, bf16[64,16,512]{2,1,0:T(8,128)(2,1)} %keys_far.1, ...), custom_call_target="tpu_custom_call" | custom-call | flops 600000000 | bytes 5000000 | tf_op jit(solution)/shard_map/attention/pallas_call | solution.py:194
  4.0 1.5 %collective-permute-start = (bf16[256,4096]{1,0:T(8,128)(2,1)S(1)}, bf16[256,4096]{1,0:T(8,128)(2,1)S(1)}, u32[]{:S(2)}, u32[]{:S(2)}) collective-permute-start(bf16[256,4096]{1,0:T(8,128)(2,1)S(1)} %copy-done.1), channel_id=1, source_target_pairs={{0,1},{1,0},{2,3},{3,2},{4,5},{5,4},{6,7},{7,6},{8,9},{9,8},{10,11... | collective-permute-start | bytes 6291464 | tf_op jit(solution)/shard_map/ppermute | solution.py:618
  5.5 16.3 %all_to_all.15.x_ref = bf16[16,16,512]{2,1,0:T(8,128)(2,1)S(1)} all-to-all(bf16[16,16,512]{2,1,0:T(8,128)(2,1)} %get-tuple-element.27), channel_id=1, replica_groups={{0,2,4,6,8,10,12,14,16,18,20,22,24,26,28,30},{1,3,5,7,9,11,13,15,17,19,..., dimensions={0} | all-to-all | bytes 524288 | tf_op jit(solution)/shard_map/all_to_all | solution.py:619
  21.9 1.3 project_sent.1
  23.4 1.1 collective-permute-start.9
  24.4 1.1 collective-permute-start.3
  25.6 1.3 project_kept.1
  26.9 3.1 %collective-permute-done.7 = bf16[8,16,1024]{2,1,0:T(8,128)(2,1)S(1)} collective-permute-done((bf16[8,16,1024]{2,1,0:T(8,128)(2,1)S(1)}, bf16[8,16,1024]{2,1,0:T(8,128)(2,1)S(1)}, u32[]{:S(2)}, u32[]{:S(2)}) %collective-permute-start.7) | collective-permute-done | bytes 262176 | tf_op jit(solution)/shard_map/ppermute | solution.py:540
  30.0 0.7 collective-permute-start.8
  30.7 0.2 collective-permute-done.9
  31.2 0.5 collective-permute-start.2
  31.8 1.2 collective-permute-start.4
  33.0 2.1 %collective-permute-done.8 = bf16[4,16,1024]{2,1,0:T(8,128)(2,1)S(1)} collective-permute-done((bf16[4,16,1024]{2,1,0:T(8,128)(2,1)S(1)}, bf16[4,16,1024]{2,1,0:T(8,128)(2,1)S(1)}, u32[]{:S(2)}, u32[]{:S(2)}) %collective-permute-start.8) | collective-permute-done | bytes 131104 | tf_op jit(solution)/shard_map/ppermute | solution.py:540
  35.2 1.6 %collective-permute-start.11 = (bf16[2,16,2048]{2,1,0:T(8,128)(2,1)S(1)}, bf16[2,16,2048]{2,1,0:T(8,128)(2,1)S(1)}, u32[]{:S(2)}, u32[]{:S(2)}) collective-permute-start(bf16[2,16,2048]{2,1,0:T(8,128)(2,1)S(1)} %pad_maximum_fusion), channel_id=1, source_target_pairs={{0,2},{1,3},{2,0},{3,1},{4,6},{5,7},{6,4},{7,5},{8,10},{9,11},{10,... | collective-permute-start | bytes 393224 | tf_op jit(solution)/shard_map/ppermute | solution.py:540
  37.0 1.0 collective-permute-start.5
  37.9 1.8 %collective-permute-done.11 = bf16[2,16,2048]{2,1,0:T(8,128)(2,1)S(1)} collective-permute-done((bf16[2,16,2048]{2,1,0:T(8,128)(2,1)S(1)}, bf16[2,16,2048]{2,1,0:T(8,128)(2,1)S(1)}, u32[]{:S(2)}, u32[]{:S(2)}) %collective-permute-start.11) | collective-permute-done | bytes 131104 | tf_op jit(solution)/shard_map/ppermute | solution.py:540
  39.7 0.2 collective-permute-start.12
  39.9 1.0 collective-permute-done.5
  41.0 1.7 %collective-permute-start.6 = (bf16[16,2048]{1,0:T(8,128)(2,1)S(1)}, bf16[16,2048]{1,0:T(8,128)(2,1)S(1)}, u32[]{:S(2)}, u32[]{:S(2)}) collective-permute-start(bf16[16,2048]{1,0:T(8,128)(2,1)S(1)} %get-tuple-element.43), channel_id=1, source_target_pairs={{0,24},{1,25},{2,26},{3,27},{4,28},{5,29},{6,30},{7,31},{8,16},{9,... | collective-permute-start | bytes 196616 | tf_op jit(solution)/shard_map/ppermute | solution.py:540
  42.6 0.9 fusion.7.placing
  43.6 0.5 collective-permute-done.12.got_b
  44.1 1.2 collective-permute-done.6.got_a
  45.4 0.9 dispatch.1
  46.3 43.6 %all_to_all.16.arrived = bf16[128,16,512]{2,1,0:T(8,128)(2,1)S(1)} all-to-all(bf16[128,16,512]{2,1,0:T(8,128)(2,1)S(1)} %bitcast.38), channel_id=1, replica_groups=mesh['attn'=4,'dev'=32] {'attn','dev'}, dimensions={0} | all-to-all | bytes 4194304 | tf_op jit(solution)/shard_map/all_to_all | solution.py:631
  89.9 7.2 %expert.1 = bf16[128,16,512]{2,1,0:T(8,128)(2,1)} custom-call(bf16[128,16,512]{2,1,0:T(8,128)(2,1)S(1)} %all_to_all.16.arrived, bf16[1,4096,768]{2,1,0:T(8,128)(2,1)S(1)} %bitcast.35, bf16[1,4096,768]{2,1,0:T(8,128)(2,1)S(1)} %bitcast.37, bf16[1,768,4096]{2,1,0:T(8,128)(2,1)S(1)} %copy-done.2), custom_call_target="tpu_custom_call" | custom-call | flops 5900000256 | bytes 23000000 | tf_op jit(solution)/shard_map/expert/pallas_call | solution.py:434
  97.1 4.7 %all-to-all-start.2 = ((bf16[128,16,512]{2,1,0:T(8,128)(2,1)}), bf16[128,16,512]{2,1,0:T(8,128)(2,1)S(1)}, u32[]{:S(2)}, u32[]{:S(2)}) async-start(bf16[128,16,512]{2,1,0:T(8,128)(2,1)} %expert.1), calls=%async_computation.2 | async-start | bytes 4194304 | tf_op jit(solution)/shard_map/all_to_all | solution.py:639
  101.9 0.2 fusion.10
  102.2 0.2 select_reduce_fusion
  102.3 0.1 exponential_reduce_fusion
  102.5 1.9 %mixing.1.mixing_far = bf16[128,2048]{1,0:T(8,128)(2,1)} custom-call(s32[8,128]{1,0:T(8,128)S(1)} %copy-done.3, f32[16,8]{1,0:T(8,128)S(1)} %exponential_divide_fusion.gates), custom_call_target="tpu_custom_call" | custom-call | flops 6000000 | bytes 600000 | tf_op jit(solution)/shard_map/mixing/pallas_call | solution.py:475
  104.4 27.9 %all-to-all-done.2 = bf16[128,16,512]{2,1,0:T(8,128)(2,1)S(1)} async-done(((bf16[128,16,512]{2,1,0:T(8,128)(2,1)}), bf16[128,16,512]{2,1,0:T(8,128)(2,1)S(1)}, u32[]{:S(2)}, u32[]{:S(2)}) %all-to-all-start.2) | async-done | bytes 2097184 | tf_op jit(solution)/shard_map/all_to_all | solution.py:639
  132.3 2.2 %combine.1 = bf16[16,4096]{1,0:T(8,128)(2,1)} custom-call(bf16[128,2048]{1,0:T(8,128)(2,1)} %mixing.1.mixing_far, bf16[2048,512]{1,0:T(8,128)(2,1)S(1)} %bitcast.33, f32[16,4096]{1,0:T(8,128)} %get-tuple-element.40.hidden_far), custom_call_target="tpu_custom_call" | custom-call | flops 270000000 | bytes 3000000 | tf_op jit(solution)/shard_map/combine/pallas_call | solution.py:507
  (57 shorter events, 1.1 us)
Async XLA Ops:
  0.0 101.9 %copy-start = (bf16[4096,128]{1,0:T(8,128)(2,1)S(1)}, bf16[4096,128]{1,0:T(8,128)(2,1)}, u32[]{:S(2)}) copy-start(bf16[4096,128]{1,0:T(8,128)(2,1)} %param.25) | copy-start | bytes 3145732
  0.0 4.0 %copy-start.1 = (bf16[256,4096]{1,0:T(8,128)(2,1)S(1)}, bf16[256,4096]{1,0:T(8,128)(2,1)}, u32[]{:S(2)}) copy-start(bf16[256,4096]{1,0:T(8,128)(2,1)} %mine.3) | copy-start | bytes 6291460
  4.0 17.9 %collective-permute-start = (bf16[256,4096]{1,0:T(8,128)(2,1)S(1)}, bf16[256,4096]{1,0:T(8,128)(2,1)S(1)}, u32[]{:S(2)}, u32[]{:S(2)}) collective-permute-start(bf16[256,4096]{1,0:T(8,128)(2,1)S(1)} %copy-done.1), channel_id=1, source_target_pairs={{0,1},{1,0},{2,3},{3,2},{4,5},{5,4},{6,7},{7,6},{8,9},{9,8},{10,11... | collective-permute-start | bytes 6291464 | tf_op jit(solution)/shard_map/ppermute | solution.py:618
  21.9 1.4 %copy-start.3 = (s32[8,128]{1,0:T(8,128)S(1)}, s32[8,128]{1,0:T(8,128)}, u32[]{:S(2)}) copy-start(s32[8,128]{1,0:T(8,128)} %get-tuple-element.24.target_ref) | copy-start | bytes 12292
  21.9 68.0 %slice-start.2 = ((s8[6291456]{0:T(1024)(128)(4,1)}), s8[4194304]{0:T(1024)(128)(4,1)S(1)}, s32[]{:S(2)}) async-start(s8[6291456]{0:T(1024)(128)(4,1)} %bitcast.36), calls=%async_computation.5 | async-start | bytes 8388608
  23.2 6.7 %collective-permute-start.7 = (bf16[8,16,1024]{2,1,0:T(8,128)(2,1)S(1)}, bf16[8,16,1024]{2,1,0:T(8,128)(2,1)S(1)}, u32[]{:S(2)}, u32[]{:S(2)}) collective-permute-start(bf16[8,16,1024]{2,1,0:T(8,128)(2,1)S(1)} %get-tuple-element.35), channel_id=1, source_target_pairs={{0,8},{1,9},{2,10},{3,11},{4,12},{5,13},{6,14},{7,15},{8,0},{9,1},... | collective-permute-start | bytes 786440 | tf_op jit(solution)/shard_map/ppermute | solution.py:540
  23.3 7.8 %collective-permute-start.1 = (bf16[8,16,1024]{2,1,0:T(8,128)(2,1)S(1)}, bf16[8,16,1024]{2,1,0:T(8,128)(2,1)S(1)}, u32[]{:S(2)}, u32[]{:S(2)}) collective-permute-start(bf16[8,16,1024]{2,1,0:T(8,128)(2,1)S(1)} %get-tuple-element.29), channel_id=1, source_target_pairs={{0,2},{1,3},{2,0},{3,1},{4,6},{5,7},{6,4},{7,5},{8,10},{9,11},{10,... | collective-permute-start | bytes 786440 | tf_op jit(solution)/shard_map/ppermute | solution.py:540
  23.4 7.5 %collective-permute-start.9 = (bf16[8,16,1024]{2,1,0:T(8,128)(2,1)S(1)}, bf16[8,16,1024]{2,1,0:T(8,128)(2,1)S(1)}, u32[]{:S(2)}, u32[]{:S(2)}) collective-permute-start(bf16[8,16,1024]{2,1,0:T(8,128)(2,1)S(1)} %get-tuple-element.37), channel_id=1, source_target_pairs={{0,24},{1,25},{2,26},{3,27},{4,28},{5,29},{6,30},{7,31},{8,16},{9,... | collective-permute-start | bytes 786440 | tf_op jit(solution)/shard_map/ppermute | solution.py:540
  24.4 7.3 %collective-permute-start.3 = (bf16[8,16,1024]{2,1,0:T(8,128)(2,1)S(1)}, bf16[8,16,1024]{2,1,0:T(8,128)(2,1)S(1)}, u32[]{:S(2)}, u32[]{:S(2)}) collective-permute-start(bf16[8,16,1024]{2,1,0:T(8,128)(2,1)S(1)} %get-tuple-element.33), channel_id=1, source_target_pairs={{0,6},{1,7},{2,4},{3,5},{4,2},{5,3},{6,0},{7,1},{8,14},{9,15},{10,... | collective-permute-start | bytes 786440 | tf_op jit(solution)/shard_map/ppermute | solution.py:540
  25.6 64.3 %slice-start = ((s8[6291456]{0:T(1024)(128)(4,1)}), s8[2097152]{0:T(1024)(128)(4,1)S(1)}, s32[]{:S(2)}) async-start(s8[6291456]{0:T(1024)(128)(4,1)} %bitcast.34), calls=%async_computation.3 | async-start | bytes 4194304
  30.0 5.1 %collective-permute-start.8 = (bf16[4,16,1024]{2,1,0:T(8,128)(2,1)S(1)}, bf16[4,16,1024]{2,1,0:T(8,128)(2,1)S(1)}, u32[]{:S(2)}, u32[]{:S(2)}) collective-permute-start(bf16[4,16,1024]{2,1,0:T(8,128)(2,1)S(1)} %slice.105), channel_id=1, source_target_pairs={{0,24},{1,25},{2,26},{3,27},{4,28},{5,29},{6,30},{7,31},{8,16},{9,... | collective-permute-start | bytes 393224 | tf_op jit(solution)/shard_map/ppermute | solution.py:540
  30.9 59.0 %copy-start.2 = (bf16[1,768,4096]{2,1,0:T(8,128)(2,1)S(1)}, bf16[1,768,4096]{2,1,0:T(8,128)(2,1)}, u32[]{:S(2)}) copy-start(bf16[1,768,4096]{2,1,0:T(8,128)(2,1)} %down.1) | copy-start | bytes 18874372
  31.0 4.2 %collective-permute-start.10 = (bf16[4,16,1024]{2,1,0:T(8,128)(2,1)S(1)}, bf16[4,16,1024]{2,1,0:T(8,128)(2,1)S(1)}, u32[]{:S(2)}, u32[]{:S(2)}) collective-permute-start(bf16[4,16,1024]{2,1,0:T(8,128)(2,1)S(1)} %slice.107), channel_id=1, source_target_pairs={{0,8},{1,9},{2,10},{3,11},{4,12},{5,13},{6,14},{7,15},{8,0},{9,1},... | collective-permute-start | bytes 393224 | tf_op jit(solution)/shard_map/ppermute | solution.py:540
  31.1 14.3 %copy-start.4 = (bf16[16,4096]{1,0:T(8,128)(2,1)S(1)}, bf16[16,4096]{1,0:T(8,128)(2,1)}, u32[]{:S(2)}) copy-start(bf16[16,4096]{1,0:T(8,128)(2,1)} %residual.1) | copy-start | bytes 393220
  31.1 14.3 %copy-start.5 = (f32[4096]{0:T(1024)S(1)}, f32[4096]{0:T(1024)}, u32[]{:S(2)}) copy-start(f32[4096]{0:T(1024)} %param.24) | copy-start | bytes 49156
  31.1 58.8 %slice-start.3 = ((s8[6291456]{0:T(1024)(128)(4,1)}), s8[2097152]{0:T(1024)(128)(4,1)S(1)}, s32[]{:S(2)}) async-start(s8[6291456]{0:T(1024)(128)(4,1)} %bitcast.36), calls=%async_computation.6 | async-start | bytes 4194304
  31.2 5.7 %collective-permute-start.2 = (bf16[4,16,1024]{2,1,0:T(8,128)(2,1)S(1)}, bf16[4,16,1024]{2,1,0:T(8,128)(2,1)S(1)}, u32[]{:S(2)}, u32[]{:S(2)}) collective-permute-start(bf16[4,16,1024]{2,1,0:T(8,128)(2,1)S(1)} %slice.97), channel_id=1, source_target_pairs={{0,6},{1,7},{2,4},{3,5},{4,2},{5,3},{6,0},{7,1},{8,14},{9,15},{10,... | collective-permute-start | bytes 393224 | tf_op jit(solution)/shard_map/ppermute | solution.py:540
  31.8 5.1 %collective-permute-start.4 = (bf16[4,16,1024]{2,1,0:T(8,128)(2,1)S(1)}, bf16[4,16,1024]{2,1,0:T(8,128)(2,1)S(1)}, u32[]{:S(2)}, u32[]{:S(2)}) collective-permute-start(bf16[4,16,1024]{2,1,0:T(8,128)(2,1)S(1)} %slice.99), channel_id=1, source_target_pairs={{0,2},{1,3},{2,0},{3,1},{4,6},{5,7},{6,4},{7,5},{8,10},{9,11},{10,... | collective-permute-start | bytes 393224 | tf_op jit(solution)/shard_map/ppermute | solution.py:540
  35.1 54.7 %slice-start.1 = ((s8[6291456]{0:T(1024)(128)(4,1)}), s8[4194304]{0:T(1024)(128)(4,1)S(1)}, s32[]{:S(2)}) async-start(s8[6291456]{0:T(1024)(128)(4,1)} %bitcast.34), calls=%async_computation.4 | async-start | bytes 8388608
  35.2 4.4 %collective-permute-start.11 = (bf16[2,16,2048]{2,1,0:T(8,128)(2,1)S(1)}, bf16[2,16,2048]{2,1,0:T(8,128)(2,1)S(1)}, u32[]{:S(2)}, u32[]{:S(2)}) collective-permute-start(bf16[2,16,2048]{2,1,0:T(8,128)(2,1)S(1)} %pad_maximum_fusion), channel_id=1, source_target_pairs={{0,2},{1,3},{2,0},{3,1},{4,6},{5,7},{6,4},{7,5},{8,10},{9,11},{10,... | collective-permute-start | bytes 393224 | tf_op jit(solution)/shard_map/ppermute | solution.py:540
  37.0 3.9 %collective-permute-start.5 = (bf16[2,16,2048]{2,1,0:T(8,128)(2,1)S(1)}, bf16[2,16,2048]{2,1,0:T(8,128)(2,1)S(1)}, u32[]{:S(2)}, u32[]{:S(2)}) collective-permute-start(bf16[2,16,2048]{2,1,0:T(8,128)(2,1)S(1)} %pad_maximum_fusion.1), channel_id=1, source_target_pairs={{0,8},{1,9},{2,10},{3,11},{4,12},{5,13},{6,14},{7,15},{8,0},{9,1},... | collective-permute-start | bytes 393224 | tf_op jit(solution)/shard_map/ppermute | solution.py:540
  39.7 4.4 %collective-permute-start.12 = (bf16[16,2048]{1,0:T(8,128)(2,1)S(1)}, bf16[16,2048]{1,0:T(8,128)(2,1)S(1)}, u32[]{:S(2)}, u32[]{:S(2)}) collective-permute-start(bf16[16,2048]{1,0:T(8,128)(2,1)S(1)} %get-tuple-element.41), channel_id=1, source_target_pairs={{0,6},{1,7},{2,4},{3,5},{4,2},{5,3},{6,0},{7,1},{8,14},{9,15},{10,... | collective-permute-start | bytes 196616 | tf_op jit(solution)/shard_map/ppermute | solution.py:540
  41.0 4.4 %collective-permute-start.6 = (bf16[16,2048]{1,0:T(8,128)(2,1)S(1)}, bf16[16,2048]{1,0:T(8,128)(2,1)S(1)}, u32[]{:S(2)}, u32[]{:S(2)}) collective-permute-start(bf16[16,2048]{1,0:T(8,128)(2,1)S(1)} %get-tuple-element.43), channel_id=1, source_target_pairs={{0,24},{1,25},{2,26},{3,27},{4,28},{5,29},{6,30},{7,31},{8,16},{9,... | collective-permute-start | bytes 196616 | tf_op jit(solution)/shard_map/ppermute | solution.py:540
  97.1 4.7 %copy-start.7 = (s32[16,8]{0,1:T(8,128)S(1)}, s32[16,8]{0,1:T(8,128)}, u32[]{:S(2)}) copy-start(s32[16,8]{0,1:T(8,128)} %param.26) | copy-start | bytes 1540
  97.1 4.8 %copy-start.6 = (bf16[16,4096]{1,0:T(8,128)(2,1)S(1)}, bf16[16,4096]{1,0:T(8,128)(2,1)}, u32[]{:S(2)}) copy-start(bf16[16,4096]{1,0:T(8,128)(2,1)} %get-tuple-element.38) | copy-start | bytes 393220
  97.1 35.2 %all-to-all-start.2 = ((bf16[128,16,512]{2,1,0:T(8,128)(2,1)}), bf16[128,16,512]{2,1,0:T(8,128)(2,1)S(1)}, u32[]{:S(2)}, u32[]{:S(2)}) async-start(bf16[128,16,512]{2,1,0:T(8,128)(2,1)} %expert.1), calls=%async_computation.2 | async-start | bytes 4194304 | tf_op jit(solution)/shard_map/all_to_all | solution.py:639
